TPU v7x, 32 devices: a whole 2x2x4 slice. The times are simulated.
32 devices in a mesh: dp: 8 (over z, y), expert: 4 (over x, core).
Axes of the slice: x: 2, y: 2, z: 4, core: 2. Of those that a mesh axis runs over, the one named last changes fastest.
Arguments:
- inputs: bfloat16 [4, 96, 197, 768], P(None, ('dp', 'expert')), may hold values from -6 to 6
- counts: int32 [4, 32], P(None, ('dp', 'expert')), may hold values from 1 to 3, 64 in all within a row
- ln1_gain: bfloat16 [768], P(('dp', 'expert')), may hold values from 0.099609375 to 1.8984375
- ln1_bias: bfloat16 [768], P(('dp', 'expert')), may hold values from -1.5 to 1.5
- w_qkv: bfloat16 [768, 2304], P(('dp', 'expert')), may hold values from -0.21875 to 0.21875
- w_out: bfloat16 [768, 768], P(('dp', 'expert')), may hold values from -0.625 to 0.625
- ln2_gain: bfloat16 [768], P(('dp', 'expert')), may hold values from 0.099609375 to 1.8984375
- ln2_bias: bfloat16 [768], P(('dp', 'expert')), may hold values from -1.5 to 1.5
- phi: bfloat16 [768, 8], P(('dp', 'expert')), may hold values from -0.125 to 0.125
- w_up: bfloat16 [8, 768, 3072], P('expert', None, 'dp'), may hold values from -1.75 to 1.75
- w_down: bfloat16 [8, 3072, 768], P('expert', 'dp'), may hold values from -0.4375 to 0.4375
- cotangent: bfloat16 [4, 96, 197, 768], P(None, ('dp', 'expert')), may hold values from -6 to 6
Outputs:
- output: bfloat16 [4, 96, 197, 768], P(None, ('dp', 'expert'))
- input_grad: bfloat16 [4, 96, 197, 768], P(None, ('dp', 'expert'))
- grad_ln1_gain: float32 [768], P(('dp', 'expert'))
- grad_ln1_bias: float32 [768], P(('dp', 'expert'))
- grad_w_qkv: float32 [768, 2304], P(('dp', 'expert'))
- grad_w_out: float32 [768, 768], P(('dp', 'expert'))
- grad_ln2_gain: float32 [768], P(('dp', 'expert'))
- grad_ln2_bias: float32 [768], P(('dp', 'expert'))
- grad_phi: float32 [768, 8], P(('dp', 'expert'))
- grad_w_up: float32 [8, 768, 3072], P('expert', None, 'dp')
- grad_w_down: float32 [8, 3072, 768], P('expert', 'dp')
Inputs may be any that keep to these rules, and one draw needn't show every extreme that they name: counts[b, d] is how many of device d's first 3 image places hold live images in micro-batch b; each micro-batch holds 64 live images and some device is full.
All inputs are finite; a program needn't handle non-finite values.
Results may differ from a plain program's by a relative error of at most 0.018.
Values may be sent and summed in bfloat16 or wider, within the bound.
No kernel may reach another device: no remote copies, remote signals or barrier semaphores. Data moves between devices by JAX's collectives and lax.ppermute only.
A program may use at most 384 MiB of HBM per device.

v0:
```python
from functools import partial

import jax
import jax.numpy as jnp
from jax import lax
from jax.experimental import pallas as pl
from jax.experimental.pallas import tpu as pltpu
from jax.sharding import PartitionSpec as P

HEAD_DIM = 64
EPSILON = 1e-06
BOTH = ("dp", "expert")
F32, BF16 = jnp.float32, jnp.bfloat16
LOW = -1e30
LIMIT = 52
SHARES = (2, 6, 4)
SMALL = 52
GATHER_CUT = 1664


class Grid:
    def __init__(self, n, m):
        self.n, self.m = n, m
        self.size = {"z": n // 2, "y": 2, "x": m // 2, "c": 2, "e": m}

    def coords(self):
        d, e = lax.axis_index("dp"), lax.axis_index("expert")
        return {"z": d // 2, "y": d % 2, "x": e // 2, "c": e % 2, "e": e}

    def perm(self, axis, k):
        pairs = []
        for source in range(self.n * self.m):
            d, e = divmod(source, self.m)
            p = {"z": d // 2, "y": d % 2, "x": e // 2, "c": e % 2, "e": e}
            q = (p[axis] + k) % self.size[axis]
            if axis == "e":
                target = d * self.m + q
            else:
                p[axis] = q
                target = (p["z"] * 2 + p["y"]) * self.m + p["x"] * 2 + p["c"]
            pairs.append((source, target))
        return pairs

    def send(self, a, axis, k):
        return lax.ppermute(a, BOTH, self.perm(axis, k))

    def by_coordinate(self, me, axis, pieces, at=0):
        s = self.size[axis]
        if s == 2:
            return jnp.stack([jnp.where(me == p, pieces[0], pieces[1]) for p in range(2)], axis=at)
        if s <= 4:
            return jnp.stack([lax.select_n((me - p) % s, *pieces) for p in range(s)], axis=at)
        shape = pieces[0].shape
        out = jnp.zeros(shape[:at] + (s,) + shape[at:], pieces[0].dtype)
        for k in range(s):
            out = lax.dynamic_update_index_in_dim(out, pieces[k], (me - k) % s, at)
        return out

    def block(self, a, axis, me, k, at=0):
        return lax.dynamic_index_in_dim(a, (me[axis] + k) % self.size[axis], at, keepdims=False)


def joined(parts, axis):
    return jnp.concatenate(parts, axis=axis) if len(parts) > 1 else parts[0]


def send_on(grid, items):
    return [[grid.send(a, axis, k) for k in range(1, grid.size[axis])] for a, axis in items]


def gather_steps(grid, me, a, cut):
    got = yield send_on(grid, [(a, "z")])
    a = grid.by_coordinate(me["z"], "z", [a] + got[0])
    parts = [a[..., :cut], a[..., cut:]]
    for axes, at in (("yx", (1, 1)), ("xy", (2, 1)), ("cc", (3, 3))):
        got = yield send_on(grid, list(zip(parts, axes)))
        parts = [grid.by_coordinate(me[x], x, [p] + r, i) for p, r, x, i in zip(parts, got, axes, at)]
    return [p.reshape(-1, p.shape[-1]) for p in parts]


def reduce_steps(grid, me, a, cut):
    s = grid.size
    a = a.reshape(s["z"], 2, s["x"], 2, -1, a.shape[1])
    got = yield [[grid.send(grid.block(a, "c", me, 1, 3), "c", 1)]]
    a = (grid.block(a, "c", me, 0, 3).astype(F32) + got[0][0].astype(F32)).astype(BF16)
    parts = [a[..., :cut], a[..., cut:]]
    for axes, at in (("xy", (2, 1)), ("yx", (1, 1))):
        blocks = [[grid.block(p, x, me, k, i) for k in range(s[x])] for p, x, i in zip(parts, axes, at)]
        got = yield [[grid.send(b, x, k) for k, b in enumerate(bs) if k] for bs, x in zip(blocks, axes)]
        parts = [sum([b.astype(F32) for b in r], bs[0].astype(F32)).astype(BF16) for bs, r in zip(blocks, got)]
    a = jnp.concatenate(parts, axis=-1)
    blocks = [grid.block(a, "z", me, k) for k in range(s["z"])]
    got = yield [[grid.send(b, "z", k) for k, b in enumerate(blocks) if k]]
    return sum([b.astype(F32) for b in got[0]], blocks[0].astype(F32))


def swap_step(grid, blocks, axis, sign):
    received = yield [[grid.send(b, axis, sign * k) for k, b in enumerate(blocks) if k]]
    return list(blocks[:1]) + received[0]


def out_steps(grid, rows):
    r = rows.shape[0] // grid.m
    pieces = yield from swap_step(grid, [rows[k * r : (k + 1) * r] for k in range(grid.m)], "e", 1)
    own = jnp.concatenate(pieces, axis=0)
    return (yield from swap_step(grid, [own] * grid.size["z"], "z", 1))


def home_steps(grid, pieces):
    pieces = yield from swap_step(grid, pieces, "z", -1)
    own = sum([p.astype(F32) for p in pieces]).astype(BF16)
    r = own.shape[0] // grid.m
    pieces = yield from swap_step(grid, [own[k * r : (k + 1) * r] for k in range(grid.m)], "e", -1)
    return jnp.concatenate(pieces, axis=0)


def neighbour_steps(grid, arrays):
    received = yield [[grid.send(a, "y", 1) for a in arrays]]
    return received[0]


class Flow:
    def __init__(self, steps):
        self.steps, self.value, self.done = steps, None, False
        self.advance(None)

    def advance(self, received):
        try:
            self.waiting = self.steps.send(received)
        except StopIteration as end:
            self.value, self.done, self.waiting = end.value, True, None


def beside(flows, token, work=None):
    flows = [flow for flow in flows if flow is not None and not flow.done]
    made = work(token) if work else ()
    received, made, token = lax.optimization_barrier(([flow.waiting for flow in flows], made, token))
    for flow, arrays in zip(flows, received):
        flow.advance(arrays)
    return made, token


def dot(a, b, ca=1, cb=0):
    return lax.dot_general(a, b, (((ca,), (cb,)), ((), ())), preferred_element_type=F32)


def padded(v, step):
    return -(-v // step) * step


def standardized(v):
    width = v.shape[-1]
    center = v - jnp.sum(v, axis=-1, keepdims=True) * (1.0 / width)
    root = lax.rsqrt(jnp.sum(center * center, axis=-1, keepdims=True) * (1.0 / width) + EPSILON)
    return center * root, root


def lanes_of(head, width):
    return lax.broadcasted_iota(jnp.int32, (1, width), 1) // HEAD_DIM == head


def by_head(v, scale):
    width = v.shape[1]
    return jnp.concatenate([v * jnp.where(lanes_of(h, width), scale, 0.0).astype(BF16) for h in range(width // HEAD_DIM)], axis=0)


def own_columns(v):
    half = v.shape[0] // 2
    return jnp.where(lanes_of(0, v.shape[1]), v[:half], v[half:])


def routed(logits, tokens, slots):
    row = lax.broadcasted_iota(jnp.int32, logits.shape, 0)
    lane = lax.broadcasted_iota(jnp.int32, logits.shape, 1)
    valid = (row < tokens) & (lane < slots)
    kept = jnp.where(valid, logits, LOW)
    down = jnp.where(valid, jnp.exp(kept - jnp.max(kept, axis=0, keepdims=True)), 0.0)
    down_sum = jnp.sum(down, axis=0, keepdims=True)
    over_tokens = down * (1.0 / jnp.where(down_sum > 0, down_sum, 1.0))
    across = jnp.where(valid, jnp.exp(kept - jnp.max(kept, axis=1, keepdims=True)), 0.0)
    across_sum = jnp.sum(across, axis=1, keepdims=True)
    over_slots = across * (1.0 / jnp.where(across_sum > 0, across_sum, 1.0))
    return over_tokens, over_slots


def longer(v, count):
    return jnp.concatenate([v, jnp.zeros((count - v.shape[0], v.shape[1]), v.dtype)], axis=0)


def pad_kernel(tokens, cot_ref, out_ref):
    rows = out_ref.shape[1]
    for k in range(cot_ref.shape[1]):
        out_ref[k] = jnp.zeros((rows, out_ref.shape[2]), BF16)
        out_ref[k, :tokens] = cot_ref[0, k]


def standardize_kernel(tokens, x_ref, n1_ref, root_ref, pad_ref):
    @pl.when(pl.program_id(0) == 0)
    def _():
        pad_ref[...] = jnp.zeros_like(pad_ref)

    for k in range(x_ref.shape[1]):
        pad_ref[k, :tokens] = x_ref[0, k].astype(F32)
        n1, root = standardized(pad_ref[k])
        n1_ref[k] = n1.astype(BF16)
        root_ref[k] = jnp.broadcast_to(root, root_ref.shape[1:])


def forward_kernel(
    tokens, slots, place, live, x_ref, n1_ref, cot_ref, one_ref, two_ref, vec_ref,
    triple_ref, mixed_ref, hidden_ref, logits_ref, slot_ref, pad_ref,
):
    i = pl.program_id(0)
    rows, features = pad_ref.shape
    keys = padded(rows, 128)

    @pl.when(i == 0)
    def _():
        pad_ref[...] = jnp.zeros_like(pad_ref)

    @pl.when(live[i] == 0)
    def _():
        mixed_ref[...] = jnp.zeros_like(mixed_ref)
        for s in range(slots):
            slot_ref[pl.ds(place(live, s, i), 1)] = jnp.zeros((1, slot_ref.shape[1]), F32)

    @pl.when(live[i] != 0)
    def _():
        pad_ref[:tokens] = x_ref[0, 0].astype(F32)
        normed = (n1_ref[0].astype(F32) * vec_ref[0:1] + vec_ref[1:2]).astype(BF16)
        for part in range(3):
            cut = slice(part * features, (part + 1) * features)
            weights = one_ref[:, cut] if part < 2 else two_ref[:, :features]
            triple_ref[0, :, cut] = dot(normed, weights).astype(BF16)
        bias = jnp.where(lax.broadcasted_iota(jnp.int32, (1, keys), 1) < tokens, 0.0, LOW)
        for low in range(0, features, 128):
            q = triple_ref[0, :, low : low + 128]
            k = longer(triple_ref[0, :, features + low : features + low + 128], keys)
            v = longer(triple_ref[0, :, 2 * features + low : 2 * features + low + 128], keys)
            scores = dot(by_head(q, HEAD_DIM**-0.5), k, 1, 1) + bias
            powers = jnp.exp(scores - jnp.max(scores, axis=1, keepdims=True))
            total = dot(powers.astype(BF16), v) * (1.0 / jnp.sum(powers, axis=1, keepdims=True))
            mixed_ref[0, :, low : low + 128] = own_columns(total).astype(BF16)
        hidden = pad_ref[...] + dot(mixed_ref[0], two_ref[:, features : 2 * features])
        hidden_ref[0] = hidden
        n2, _ = standardized(hidden)
        normed_two = (n2 * vec_ref[2:3] + vec_ref[3:4]).astype(BF16)
        logits = dot(normed_two, two_ref[:, 2 * features :])
        logits_ref[0] = logits
        dispatch, combine = routed(logits, tokens, slots)
        slot_in = dot(dispatch.astype(BF16), normed_two, 0, 0)
        grad_slot = dot(combine.astype(BF16), cot_ref[0], 0, 0)
        for s in range(slots):
            slot_ref[pl.ds(place(live, s, i), 1), :features] = slot_in[s : s + 1]
            slot_ref[pl.ds(place(live, s, i), 1), features:] = grad_slot[s : s + 1]


def expert_kernel(pieces, images, *refs):
    rows_in, (up, up_other, down, down_other) = refs[:pieces], refs[pieces : pieces + 4]
    rows_out, (active_ref, slope_ref) = refs[pieces + 4 : 2 * pieces + 4], refs[2 * pieces + 4 :]
    per, features = up.shape[:2]
    both = jnp.concatenate([r[...] for r in rows_in], axis=0)
    rows, grads = both[:, :features], both[:, features:]
    index = lax.broadcasted_iota(jnp.int32, (rows.shape[0], 1), 0)
    total = total_back = 0.0
    for part, (up_ref, down_ref) in enumerate(((up, down), (up_other, down_other))):
        for j in range(per):
            mine = (index // images) % per == j
            pre = dot(rows, up_ref[j])
            phi = 0.5 * (1.0 + lax.erf(pre * (0.5**0.5)))
            density = jnp.exp(pre * pre * -0.5) * (0.5 / jnp.pi) ** 0.5
            active = jnp.where(mine, pre * phi, 0.0).astype(BF16)
            grad = dot(grads, down_ref[j], 1, 1)
            grad = jnp.where(mine, grad * (phi + pre * density), 0.0).astype(BF16)
            active_ref[part, j] = active
            slope_ref[part, j] = grad
            total = total + dot(active, down_ref[j])
            total_back = total_back + dot(grad, up_ref[j], 1, 1)
    size = rows_in[0].shape[0]
    for k, ref in enumerate(rows_out):
        ref[:, :features] = total[k * size : (k + 1) * size].astype(BF16)
        ref[:, features:] = total_back[k * size : (k + 1) * size].astype(BF16)


def expert_grad_kernel(pieces, *refs):
    rows_in, (active_ref, slope_ref) = refs[:pieces], refs[pieces : pieces + 2]
    outs = refs[pieces + 2 :]
    features = outs[0].shape[1]
    both = jnp.concatenate([r[...] for r in rows_in], axis=0)
    rows, grads = both[:, :features].T, both[:, features:]
    for part in range(2):
        up_ref, down_ref = outs[2 * part : 2 * part + 2]
        for j in range(up_ref.shape[0]):
            up_ref[j] = dot(rows, slope_ref[part, j]).astype(up_ref.dtype)
            down_ref[j] = dot(active_ref[part, j], grads, 0, 0).astype(down_ref.dtype)


def backward_kernel(
    tokens, slots, place, live, cot_ref, triple_ref, hidden_ref, logits_ref, home_ref, two_ref, phit_ref, vec_ref,
    out_ref, branch_ref, grad_ref, total_ref, small_ref, gm_ref,
):
    i = pl.program_id(0)
    rows, features = hidden_ref.shape[1:]
    keys = gm_ref.shape[0]

    @pl.when(i == 0)
    def _():
        gm_ref[...] = jnp.zeros_like(gm_ref)
        total_ref[...] = jnp.zeros_like(total_ref)
        small_ref[...] = jnp.zeros_like(small_ref)

    @pl.when(live[i] == 0)
    def _():
        out_ref[...] = jnp.zeros_like(out_ref)
        branch_ref[...] = jnp.zeros_like(branch_ref)
        grad_ref[...] = jnp.zeros_like(grad_ref)

    @pl.when(live[i] != 0)
    def _():
        hidden = hidden_ref[0]
        n2, root = standardized(hidden)
        gain = vec_ref[2:3]
        normed_two = (n2 * gain + vec_ref[3:4]).astype(BF16)
        over_tokens, over_slots = routed(logits_ref[0], tokens, slots)
        over_tokens, over_slots = over_tokens[:, :slots], over_slots[:, :slots]
        dispatch, combine = over_tokens.astype(BF16), over_slots.astype(BF16)
        home = jnp.concatenate([home_ref[pl.ds(place(live, s, i), 1)] for s in range(slots)], axis=0).astype(BF16)
        slot_out, grad_in = home[:, :features], home[:, features:]
        cot = cot_ref[0].astype(F32)
        result = hidden + dot(combine, slot_out)
        out_ref[0] = result[:tokens].astype(BF16)
        grad_combine = dot(cot_ref[0], slot_out, 1, 1)
        grad_dispatch = dot(normed_two, grad_in, 1, 1)
        grad_logits = over_tokens * (grad_dispatch - jnp.sum(grad_dispatch * over_tokens, axis=0, keepdims=True))
        grad_logits += over_slots * (grad_combine - jnp.sum(grad_combine * over_slots, axis=1, keepdims=True))
        grad_logits = grad_logits.astype(BF16)
        grad_two = dot(dispatch, grad_in) + dot(grad_logits, phit_ref[:slots])
        small_ref[:slots] += dot(grad_logits, normed_two, 0, 0)
        small_ref[slots : slots + 1] += jnp.sum(grad_two * n2, axis=0, keepdims=True)
        small_ref[slots + 1 : slots + 2] += jnp.sum(grad_two, axis=0, keepdims=True)
        u = grad_two * gain
        inner = u - jnp.sum(u, axis=-1, keepdims=True) * (1.0 / features)
        inner = inner - n2 * (jnp.sum(u * n2, axis=-1, keepdims=True) * (1.0 / features))
        branch = (cot + root * inner).astype(BF16)
        branch_ref[0] = branch
        gm_ref[:rows] = dot(branch, two_ref[:, features : 2 * features], 1, 1).astype(BF16)
        valid = lax.broadcasted_iota(jnp.int32, (rows, 1), 0) < tokens
        for low in range(0, features, 256):
            q = longer(triple_ref[0, :, low : low + 256], keys)
            k = triple_ref[0, :, features + low : features + low + 256]
            v = triple_ref[0, :, 2 * features + low : 2 * features + low + 256]
            gm = gm_ref[:, low : low + 256]
            scores_all = dot(by_head(k, HEAD_DIM**-0.5), q, 1, 1)
            grad_all = dot(by_head(v, 1.0), gm, 1, 1)
            for pair in range(2):
                attention, grad_scores = [], []
                for head in (2 * pair, 2 * pair + 1):
                    cut = slice(head * rows, (head + 1) * rows)
                    scores = jnp.where(valid, scores_all[cut], LOW)
                    powers = jnp.exp(scores - jnp.max(scores, axis=0, keepdims=True))
                    inverse = 1.0 / jnp.sum(powers, axis=0, keepdims=True)
                    mean = jnp.sum(grad_all[cut] * powers, axis=0, keepdims=True) * inverse
                    powers = powers * inverse
                    attention.append(powers.astype(BF16))
                    grad_scores.append((powers * (grad_all[cut] - mean)).astype(BF16))
                own = slice(pair * 128, (pair + 1) * 128)
                grads = (
                    own_columns(dot(jnp.concatenate([g.T for g in grad_scores], axis=0), k[:, own]))[:rows] * HEAD_DIM**-0.5,
                    own_columns(dot(jnp.concatenate(grad_scores, axis=0), q[:, own])) * HEAD_DIM**-0.5,
                    own_columns(dot(jnp.concatenate(attention, axis=0), gm[:, own])),
                )
                for part, grad in enumerate(grads):
                    cut = slice(part * features + low + pair * 128, part * features + low + (pair + 1) * 128)
                    grad_ref[0, :, cut] = grad.astype(BF16)
                    total_ref[0:1, cut] += jnp.sum(grad, axis=0, keepdims=True)


def input_kernel(tokens, triple_ref, n1_ref, root_ref, branch_ref, one_ref, two_ref, vec_ref, *refs):
    out_ref = refs[-1]
    count, rows, features = branch_ref.shape
    flat = lambda a: a.reshape(count * rows, a.shape[-1])
    triple, n1, root = flat(triple_ref[...]), flat(n1_ref[...]).astype(F32), flat(root_ref[...])[:, :1]
    v = dot(triple[:, : 2 * features], one_ref[...], 1, 1) + dot(triple[:, 2 * features :], two_ref[...], 1, 1)
    v = v * vec_ref[0:1]
    inner = v - jnp.sum(v, axis=-1, keepdims=True) * (1.0 / features)
    inner = inner - n1 * (jnp.sum(v * n1, axis=-1, keepdims=True) * (1.0 / features))
    grad = flat(branch_ref[...]).astype(F32) + root * inner
    for k in range(count):
        out_ref[k] = grad[k * rows : k * rows + tokens].astype(BF16)


def weight_grad_kernel(slots, left_ref, left_out_ref, right_ref, right_out_ref, one_ref, two_ref, total_ref, small_ref, columns_ref, out_ref, norm_ref):
    i, (features, tile) = pl.program_id(0), out_ref.shape
    third = features // tile

    @pl.when(i == 0)
    def _():
        norm_ref[...] = jnp.zeros_like(norm_ref)

    def tokens(ref):
        return ref[...].reshape(-1, tile)

    def wide_part(w_ref):
        product = dot(left_ref[...], tokens(right_ref))
        total = total_ref[0:1]
        out_ref[...] = (product * columns_ref[:, 0:1] + columns_ref[:, 1:2] * total).astype(BF16)
        for low in range(0, tile, 128):
            cut = slice(low, low + 128)
            weights = w_ref[:, cut].astype(F32)
            norm_ref[:, :128] += weights * product[:, cut]
            norm_ref[:, 128:] += weights * total[:, cut]

    @pl.when(i < 2 * third)
    def _():
        wide_part(one_ref)

    @pl.when((i >= 2 * third) & (i < 3 * third))
    def _():
        wide_part(two_ref)

    @pl.when((i >= 3 * third) & (i < 4 * third))
    def _():
        out_ref[...] = dot(left_out_ref[...], tokens(right_out_ref)).astype(BF16)

    @pl.when(i == 4 * third)
    def _():
        lane = lax.broadcasted_iota(jnp.int32, (features, 128), 1)
        gain = jnp.sum(norm_ref[:, :128], axis=1, keepdims=True)
        bias = jnp.sum(norm_ref[:, 128:], axis=1, keepdims=True)
        narrow = jnp.where(lane == slots + 2, gain, jnp.where(lane == slots + 3, bias, small_ref[...]))
        out_ref[:, :128] = narrow.astype(BF16)


def own(*shape, low=0):
    return pl.BlockSpec((1,) + shape, lambda i, live: (i + low,) + (0,) * len(shape))


def fixed(*shape):
    return pl.BlockSpec(shape, lambda i, *live: (0,) * len(shape), pipeline_mode=pl.Buffered(1))


def shaped(*shape, dtype=BF16):
    return jax.ShapeDtypeStruct(shape, dtype)


def params(mib, axes=1):
    return pltpu.CompilerParams(vmem_limit_bytes=mib * 1024 * 1024, dimension_semantics=("arbitrary",) * axes)


def by_image(kernel, images, in_specs, out_specs, out_shape, scratch, flops, mib):
    return pl.pallas_call(
        kernel,
        grid_spec=pltpu.PrefetchScalarGridSpec(
            num_scalar_prefetch=1, grid=(images,), in_specs=in_specs, out_specs=out_specs, scratch_shapes=scratch
        ),
        out_shape=out_shape,
        compiler_params=params(mib),
        cost_estimate=pl.CostEstimate(flops=flops, bytes_accessed=flops // 1000, transcendentals=0),
    )


class Mixer:
    def __init__(self, grid, inputs, slots, live, expert):
        self.inputs, self.slots = inputs, slots
        self.live = jnp.concatenate([live, expert[None]])
        self.owners, self.per = grid.m, slots // grid.m
        self.batches, self.capacity, self.tokens, self.features = inputs.shape
        self.images = self.batches * self.capacity
        self.rows, self.keys = padded(self.tokens, 16), padded(self.tokens, 128)
        self.pad = pltpu.VMEM((self.rows, self.features), F32)
        self.flops = self.rows * self.features * self.features * 8

    def place(self, live, s, i):
        owner = lax.rem(s // self.per + self.owners - live[self.images], self.owners)
        return (owner * self.per + s % self.per) * self.images + i

    def image(self, low):
        return pl.BlockSpec((1, 1, self.tokens, self.features), lambda i, live: ((i + low) // self.capacity, (i + low) % self.capacity, 0, 0))

    def made(self, low=0):
        return pl.BlockSpec((1, self.tokens, self.features), lambda i, live: (i + low, 0, 0))

    def padded_cotangent(self, cotangent):
        n, c, r, f = self.images, self.capacity, self.rows, self.features
        return pl.pallas_call(
            partial(pad_kernel, self.tokens),
            grid=(self.batches,),
            in_specs=[pl.BlockSpec((1, c, self.tokens, f), lambda i: (i, 0, 0, 0))],
            out_specs=pl.BlockSpec((c, r, f), lambda i: (i, 0, 0)),
            out_shape=shaped(n, r, f),
            compiler_params=params(LIMIT),
        )(cotangent)

    def standardize(self):
        n, c, r, f = self.images, self.capacity, self.rows, self.features
        group = lambda *shape: pl.BlockSpec((c,) + shape, lambda i: (i,) + (0,) * len(shape))
        return pl.pallas_call(
            partial(standardize_kernel, self.tokens),
            grid=(self.batches,),
            in_specs=[pl.BlockSpec((1, c, self.tokens, f), lambda i: (i, 0, 0, 0))],
            out_specs=[group(r, f), group(r, 128)],
            out_shape=[shaped(n, r, f), shaped(n, r, 128, dtype=F32)],
            scratch_shapes=[pltpu.VMEM((c, r, f), F32)],
            compiler_params=params(LIMIT),
        )(self.inputs)

    def forward(self, n1, cot, one, two, vec):
        n, r, f = self.images, self.rows, self.features
        return by_image(
            partial(forward_kernel, self.tokens, self.slots, self.place), n,
            [self.image(0), own(r, f), own(r, f), fixed(*one.shape), fixed(*two.shape), fixed(*vec.shape)],
            [own(r, 3 * f), own(r, f), own(r, f), own(r, 128), fixed(self.slots * n, 2 * f)],
            [shaped(n, r, 3 * f), shaped(n, r, f), shaped(n, r, f, dtype=F32), shaped(n, r, 128, dtype=F32), shaped(self.slots * n, 2 * f, dtype=F32)],
            [self.pad], 3 * n * self.flops, LIMIT,
        )(self.live, self.inputs, n1, cot, one, two, vec)

    def backward(self, cot, triple, hidden, logits, home, two, phit, vec):
        n, r, f = self.images, self.rows, self.features
        small = padded(self.slots + 2, 8)
        return by_image(
            partial(backward_kernel, self.tokens, self.slots, self.place), n,
            [own(r, f), own(r, 3 * f), own(r, f), own(r, 128), fixed(self.slots * n, 2 * f), fixed(*two.shape), fixed(*phit.shape), fixed(*vec.shape)],
            [self.made(), own(r, f), own(r, 3 * f), fixed(8, 3 * f), fixed(small, f)],
            [shaped(n, self.tokens, f), shaped(n, r, f), shaped(n, r, 3 * f), shaped(8, 3 * f, dtype=F32), shaped(small, f, dtype=F32)],
            [pltpu.VMEM((self.keys, f), BF16)], 3 * n * self.flops, LIMIT,
        )(self.live, cot, triple, hidden, logits, home, two, phit, vec)

    def input_back(self, low, high, triple, n1, root, branch, one, two, vec, into, step):
        r, f = self.rows, self.features
        some = lambda *shape: pl.BlockSpec((step,) + shape, lambda i: (i + low // step,) + (0,) * len(shape))
        return pl.pallas_call(
            partial(input_kernel, self.tokens),
            grid=((high - low) // step,),
            in_specs=[some(r, 3 * f), some(r, f), some(r, 128), some(r, f), fixed(*one.shape), fixed(f, f), fixed(*vec.shape)]
            + [pl.BlockSpec(memory_space=pl.ANY)] * (into is not None),
            out_specs=some(self.tokens, f),
            out_shape=shaped(self.images, self.tokens, f),
            input_output_aliases={} if into is None else {7: 0},
            compiler_params=params(LIMIT),
        )(triple, n1, root, branch, one, two, vec, *([] if into is None else [into]))

    def turned(self, array):
        return array.reshape(-1, array.shape[-1]).T

    def weight_grads(self, left, left_out, right, right_out, one, two, total, small, columns, tile=256):
        f, third = self.features, self.features // tile
        def at(array, first, count):
            lead = array.shape[:-1]
            return pl.BlockSpec(lead + (tile,), lambda i: (0,) * len(lead) + (jnp.clip(i - first, 0, count - 1),))
        return pl.pallas_call(
            partial(weight_grad_kernel, self.slots),
            grid=(4 * third + 1,),
            in_specs=[fixed(*left.shape), fixed(*left_out.shape), at(right, 0, 3 * third), at(right_out, 3 * third, third),
                      at(one, 0, 2 * third), at(two, 2 * third, third), at(total, 0, 3 * third), fixed(*small.shape), fixed(*columns.shape)],
            out_specs=pl.BlockSpec((f, tile), lambda i: (0, i)),
            out_shape=shaped(f, 4 * f + 128),
            scratch_shapes=[pltpu.VMEM((f, 256), F32)],
            compiler_params=params(LIMIT),
        )(left, left_out, right, right_out, one, two, total, small, columns)


def expert_forward(pieces, weights, images):
    per, _, hidden = weights[0].shape
    size, count = pieces[0].shape[0], len(pieces)
    kept = shaped(2, per, size * count, hidden)
    made = pl.pallas_call(
        partial(expert_kernel, count, images),
        out_shape=[shaped(*p.shape) for p in pieces] + [kept, kept],
        compiler_params=params(SMALL, 0),
    )(*pieces, *weights)
    return made[:count], made[count:]


def expert_grads(pieces, kept, up, down):
    return pl.pallas_call(
        partial(expert_grad_kernel, len(pieces)),
        out_shape=[shaped(*up.shape, dtype=F32), shaped(*down.shape, dtype=F32), shaped(*up.shape), shaped(*down.shape)],
        compiler_params=params(SMALL, 0),
    )(*pieces, *kept)


def wide(a, width=128):
    return jnp.pad(a, ((0, 0), (0, width - a.shape[1])))


def body(grid, inputs, counts, ln1_gain, ln1_bias, w_qkv, w_out, ln2_gain, ln2_bias, phi, w_up, w_down, cotangent):
    me = grid.coords()
    batches, capacity, tokens, features = inputs.shape
    images = batches * capacity
    slots = phi.shape[1]
    per = slots // grid.m
    token = (jnp.arange(capacity)[None, :] < counts).astype(jnp.int32).reshape(-1)
    mixer = Mixer(grid, inputs, slots, token, me["e"])
    vectors = jnp.stack([ln1_gain, ln1_bias, ln2_gain, ln2_bias], axis=1)
    packed = jnp.concatenate([w_qkv, w_out, wide(jnp.concatenate([phi, vectors], axis=1))], axis=1)
    flow = Flow(gather_steps(grid, me, packed, 2 * features))
    cot, token = beside([flow], token, lambda token: mixer.padded_cotangent(cotangent))
    _, token = beside([flow], token)
    (n1, root), token = beside([flow], token, lambda token: mixer.standardize())
    other = Flow(neighbour_steps(grid, lax.optimization_barrier(([w_up, w_down], token))[0]))
    _, token = beside([flow], token)
    one, two = flow.value
    columns = two[:, 2 * features : 2 * features + padded(slots + 4, 16)].astype(F32)
    turned = columns.T
    vec = jnp.pad(turned[slots : slots + 4], ((0, 4), (0, 0)))

    made, token = beside([other], token, lambda token: mixer.forward(n1, cot, one, two, vec))
    triple, mixed, hidden, logits, slot = made
    flow = Flow(out_steps(grid, slot.astype(BF16)))
    _, token = beside([flow], token)
    lefts, token = beside([flow], token, lambda token: (mixer.turned(n1), mixer.turned(mixed)))
    pieces = flow.value
    back, kept = expert_forward(pieces, [w_up, other.value[0], w_down, other.value[1]], images)
    flow = Flow(home_steps(grid, back))
    made, token = beside([flow], token, lambda token: expert_grads(pieces, kept, w_up, w_down))
    grad_up, grad_down, *others = made
    _, token = beside([flow], token)
    other = Flow(neighbour_steps(grid, others))
    made, token = beside(
        [other], token, lambda token: mixer.backward(cot, triple, hidden, logits, flow.value.astype(F32), two, turned.astype(BF16), vec)
    )
    outs, branch, grad_triple, total, small = made
    packed = mixer.weight_grads(
        *lefts, grad_triple, branch, one, two, total, wide(small.T), columns[:, slots : slots + 2]
    )
    grad_up, grad_down = grad_up + other.value[0].astype(F32), grad_down + other.value[1].astype(F32)
    flow = Flow(reduce_steps(grid, me, packed, padded(packed.shape[1] // 2, 128)))
    grad_in, low = None, 0
    for count in SHARES:
        grad_in, token = beside(
            [flow],
            token,
            lambda token: mixer.input_back(
                low * images // 12, (low + count) * images // 12, grad_triple, n1, root, branch, one, two, vec, grad_in, max(images // 6, 1)
            ),
        )
        low += count
    while not flow.done:
        _, token = beside([flow], token)
    sums = flow.value
    small = sums[:, 4 * features :]
    return (
        outs.reshape(inputs.shape),
        grad_in.reshape(inputs.shape),
        small[:, slots + 2],
        small[:, slots + 3],
        sums[:, : 3 * features],
        sums[:, 3 * features : 4 * features],
        small[:, slots],
        small[:, slots + 1],
        small[:, :slots],
        grad_up,
        grad_down,
    )


def solution(mesh):
    rows = P(BOTH, None)
    row = P(BOTH)
    image = P(None, BOTH, None, None)
    up, down = P("expert", None, "dp"), P("expert", "dp", None)
    grid = Grid(mesh.shape["dp"], mesh.shape["expert"])
    return jax.shard_map(
        partial(body, grid),
        mesh=mesh,
        in_specs=(image, P(None, BOTH), row, row, rows, rows, row, row, rows, up, down, image),
        out_specs=(image, image, row, row, rows, rows, row, row, rows, up, down),
        check_vma=False,
    )
```

profile of v0, /device:TPU:0, one launch (start us, length us, event | category | flops | bytes accessed | tf_op | source)
XLA Modules:
  0.0 320.1 jit_solution(1593405198177802666)
XLA Ops:
  5.4 3.1 collective-permute-start
  8.5 2.6 collective-permute-start.1
  13.3 4.3 %copy.96.cot_ref = bf16[4,3,197,768]{3,2,1,0:T(8,128)(2,1)} copy(bf16[4,3,197,768]{3,0,2,1:T(4,128)(2,1)} %param.23) | data formatting | bytes 7262208 | tf_op args[11]
  17.5 4.6 %shard_map.203.cot_ref = bf16[12,208,768]{2,1,0:T(8,128)(2,1)} custom-call(bf16[4,3,197,768]{3,2,1,0:T(8,128)(2,1)} %copy.96.cot_ref), custom_call_target="tpu_custom_call" | custom-call | tf_op jit(solution)/shard_map/pallas_call | solution.py:485
  25.6 6.1 %collective-permute-done.3 = bf16[4,24,1536]{2,1,0:T(8,128)(2,1)S(1)} collective-permute-done((bf16[4,24,1536]{2,1,0:T(8,128)(2,1)S(1)}, bf16[4,24,1536]{2,1,0:T(8,128)(2,1)S(1)}, u32[]{:S(2)}, u32[]{:S(2)}) %collective-permute-start.3) | collective-permute-done | bytes 294944 | tf_op jit(solution)/shard_map/ppermute | solution.py:45
  34.5 2.3 copy.98.x_ref
  36.8 5.6 %shard_map.204 = (bf16[12,208,768]{2,1,0:T(8,128)(2,1)}, f32[12,208,128]{2,1,0:T(8,128)S(1)}) custom-call(bf16[4,3,197,768]{3,2,1,0:T(8,128)(2,1)} %copy.98.x_ref), custom_call_target="tpu_custom_call" | custom-call | tf_op jit(solution)/shard_map/pallas_call | solution.py:497
  42.3 4.2 %collective-permute-done.5 = bf16[4,2,24,1536]{3,2,0,1:T(8,128)(2,1)S(1)} collective-permute-done((bf16[4,2,24,1536]{3,2,0,1:T(8,128)(2,1)S(1)}, bf16[4,2,24,1536]{3,2,0,1:T(8,128)(2,1)S(1)}, u32[]{:S(2)}, u32[]{:S(2)}) %collective-permute-start.5) | collective-permute-done | bytes 589856 | tf_op jit(solution)/shard_map/ppermute | solution.py:45
  60.0 35.9 %shard_map.205 = (bf16[12,208,2304]{2,1,0:T(8,128)(2,1)}, bf16[12,208,768]{2,1,0:T(8,128)(2,1)}, f32[12,208,768]{2,1,0:T(8,128)}, f32[12,208,128]{2,1,0:T(8,128)S(1)}, f32[96,1536]{1,0:T(8,128)S(1)}) custom-call(s32[13]{0:T(128)S(1)} %pad_add_fusion.live, bf16[4,3,197,768]{3,2,1,0:T(8,128)(2,1)} %copy.98.x_ref, ...), custom_call_target="tpu_custom_call" | custom-call | flops 35332816896 | bytes 35332816 | tf_op jit(solution)/shard_map/pallas_call | solution.py:509
  95.9 7.9 %collective-permute-done.8.refs_7_ = bf16[2,384,768]{2,1,0:T(8,128)(2,1)} collective-permute-done((bf16[2,384,768]{2,1,0:T(8,128)(2,1)}, bf16[2,384,768]{2,1,0:T(8,128)(2,1)}, u32[]{:S(2)}, u32[]{:S(2)}) %collective-permute-start.8) | collective-permute-done | bytes 1179680 | tf_op jit(solution)/shard_map/ppermute | solution.py:45
  109.2 4.9 %collective-permute-start.14 = (bf16[96,1536]{1,0:T(8,128)(2,1)S(1)}, bf16[96,1536]{1,0:T(8,128)(2,1)S(1)}, u32[]{:S(2)}, u32[]{:S(2)}) collective-permute-start(bf16[96,1536]{1,0:T(8,128)(2,1)S(1)} %pad_maximum_fusion.10.refs_0_), channel_id=1, source_target_pairs={{0,8},{1,9},{2,10},{3,11},{4,12},{5,13},{6,14},{7,15},{8,16},{9,17... | collective-permute-start | bytes 884744 | tf_op jit(solution)/shard_map/ppermute | solution.py:45
  114.2 2.4 collective-permute-start.16
  116.6 6.1 %copy.104 = bf16[2496,768]{0,1:T(8,128)(2,1)} copy(bf16[2496,768]{1,0:T(8,128)(2,1)} %bitcast.103) | data formatting | bytes 7667712 | tf_op jit(solution)/shard_map/reshape | solution.py:543
  122.7 6.1 %copy.105 = bf16[2496,768]{0,1:T(8,128)(2,1)} copy(bf16[2496,768]{1,0:T(8,128)(2,1)} %bitcast.114) | data formatting | bytes 7667712 | tf_op jit(solution)/shard_map/reshape | solution.py:543
  128.8 4.8 %collective-permute-done.15.refs_2_ = bf16[96,1536]{1,0:T(8,128)(2,1)S(1)} collective-permute-done((bf16[96,1536]{1,0:T(8,128)(2,1)S(1)}, bf16[96,1536]{1,0:T(8,128)(2,1)S(1)}, u32[]{:S(2)}, u32[]{:S(2)}) %collective-permute-start.15) | collective-permute-done | bytes 294944 | tf_op jit(solution)/shard_map/ppermute | solution.py:45
  134.8 8.8 %shard_map.206 = (bf16[96,1536]{1,0:T(8,128)(2,1)S(1)}, bf16[96,1536]{1,0:T(8,128)(2,1)S(1)}, bf16[96,1536]{1,0:T(8,128)(2,1)S(1)}, bf16[96,1536]{1,0:T(8,128)(2...) custom-call(bf16[96,1536]{1,0:T(8,128)(2,1)S(1)} %pad_maximum_fusion.10.refs_0_, ...), custom_call_target="tpu_custom_call" | custom-call | tf_op jit(solution)/shard_map/pallas_call | solution.py:566
  143.6 9.3 %collective-permute-start.17 = (bf16[96,1536]{1,0:T(8,128)(2,1)S(1)}, bf16[96,1536]{1,0:T(8,128)(2,1)S(1)}, u32[]{:S(2)}, u32[]{:S(2)}) collective-permute-start(bf16[96,1536]{1,0:T(8,128)(2,1)S(1)} %get-tuple-element.126), channel_id=1, source_target_pairs={{0,24},{1,25},{2,26},{3,27},{4,28},{5,29},{6,30},{7,31},{8,0},{9,1... | collective-permute-start | bytes 884744 | tf_op jit(solution)/shard_map/ppermute | solution.py:45
  155.4 7.1 %shard_map.207 = (f32[2,768,384]{2,1,0:T(8,128)}, f32[2,384,768]{2,1,0:T(8,128)}, bf16[2,768,384]{2,1,0:T(8,128)(2,1)}, bf16[2,384,768]{2,1,0:T(8,128)(2,1)}) custom-call(bf16[96,1536]{1,0:T(8,128)(2,1)S(1)} %pad_maximum_fusion.10.refs_0_, bf16[96,1536]{1,0:T(8,128)(2,1)S(1)} %collective-permute-done.14.refs_1_, bf16[96,1536]{1,0:T(8,128)(2,1)S(1)} %copy-done.1, ...), custom_call_target="tpu_custom_call" | custom-call | tf_op jit(solution)/shard_map/pallas_call | solution.py:575
  162.5 15.2 %collective-permute-done.18 = bf16[96,1536]{1,0:T(8,128)(2,1)S(1)} collective-permute-done((bf16[96,1536]{1,0:T(8,128)(2,1)S(1)}, bf16[96,1536]{1,0:T(8,128)(2,1)S(1)}, u32[]{:S(2)}, u32[]{:S(2)}) %collective-permute-start.18) | collective-permute-done | bytes 294944 | tf_op jit(solution)/shard_map/ppermute | solution.py:45
  183.8 45.4 %shard_map.208 = (bf16[12,197,768]{2,1,0:T(8,128)(2,1)}, bf16[12,208,768]{2,1,0:T(8,128)(2,1)}, bf16[12,208,2304]{2,1,0:T(8,128)(2,1)}, f32[8,2304]{1,0:T(8,128)S(1)}, f32[16,768]{1,0:T(8,128)S(1)}) custom-call(s32[13]{0:T(128)S(1)} %pad_add_fusion.live, bf16[12,208,768]{2,1,0:T(8,128)(2,1)} %shard_map.203.cot_ref, ...), custom_call_target="tpu_custom_call" | custom-call | flops 35332816896 | bytes 35332816 | tf_op jit(solution)/shard_map/pallas_call | solution.py:520
  229.3 4.5 %collective-permute-done.21 = bf16[2,384,768]{2,1,0:T(8,128)(2,1)S(1)} collective-permute-done((bf16[2,384,768]{2,1,0:T(8,128)(2,1)}, bf16[2,384,768]{2,1,0:T(8,128)(2,1)S(1)}, u32[]{:S(2)}, u32[]{:S(2)}) %collective-permute-start.21) | collective-permute-done | bytes 1179680 | tf_op jit(solution)/shard_map/ppermute | solution.py:45
  235.0 22.0 %shard_map.209 = bf16[768,3200]{1,0:T(8,128)(2,1)} custom-call(bf16[768,2496]{1,0:T(8,128)(2,1)} %bitcast.112, bf16[768,2496]{1,0:T(8,128)(2,1)} %bitcast.113, bf16[12,208,2304]{2,1,0:T(8,128)(2,1)} %get-tuple-element.155.right_ref.triple_ref, bf16[12,208,768]{2,1,0:T(8,128)(2,1)} %get-tuple-element.156.right_out_ref.branch_ref, ...), custom_call_target="tpu_custom_call" | custom-call | tf_op jit(solution)/shard_map/pallas_call | solution.py:550
  257.0 3.3 %dynamic-slice_bitcast_fusion = bf16[4,2,2,24,3200]{4,3,2,1,0:T(8,128)(2,1)} fusion(bf16[4,2,2,2,24,3200]{5,4,3,2,1,0:T(8,128)(2,1)} %bitcast.110, s32[]{:T(128)S(6)} %select_n.383), kind=kLoop, calls=%fused_computation.3 | loop fusion | bytes 4915204 | tf_op jit(solution)/shard_map/jit(dynamic_index_in_dim)/squeeze | solution.py:60
  260.5 6.0 %shard_map.210.refs_0_ = bf16[12,197,768]{2,1,0:T(8,128)(2,1)} custom-call(bf16[12,208,2304]{2,1,0:T(8,128)(2,1)} %get-tuple-element.155.right_ref.triple_ref, bf16[12,208,768]{2,1,0:T(8,128)(2,1)} %get-tuple-element.105.n1_ref, f32[12,208,128]{2,1,0:T(8,128)S(1)} %get-tuple-element.159.root_ref, ...), custom_call_target="tpu_custom_call" | custom-call | tf_op jit(solution)/shard_map/pallas_call | solution.py:531
  266.4 2.3 fusion
  272.0 10.3 %shard_map.211.refs_0_ = bf16[12,197,768]{2,1,0:T(8,128)(2,1)} custom-call(bf16[12,208,2304]{2,1,0:T(8,128)(2,1)} %get-tuple-element.155.right_ref.triple_ref, bf16[12,208,768]{2,1,0:T(8,128)(2,1)} %get-tuple-element.105.n1_ref, f32[12,208,128]{2,1,0:T(8,128)S(1)} %get-tuple-element.159.root_ref, ...), custom_call_target="tpu_custom_call", output_to_operand_aliasing={{}: (7, {})} | custom-call | tf_op jit(solution)/shard_map/pallas_call | solution.py:531
  282.3 4.5 %collective-permute-done.27 = bf16[4,2,24,1536]{3,2,1,0:T(8,128)(2,1)} collective-permute-done((bf16[4,2,24,1536]{3,2,1,0:T(8,128)(2,1)}, bf16[4,2,24,1536]{3,2,1,0:T(8,128)(2,1)}, u32[]{:S(2)}, u32[]{:S(2)}) %collective-permute-start.27) | collective-permute-done | bytes 589856 | tf_op jit(solution)/shard_map/ppermute | solution.py:45
  293.2 8.2 %shard_map.212 = bf16[12,197,768]{2,1,0:T(8,128)(2,1)} custom-call(bf16[12,208,2304]{2,1,0:T(8,128)(2,1)} %get-tuple-element.155.right_ref.triple_ref, bf16[12,208,768]{2,1,0:T(8,128)(2,1)} %get-tuple-element.105.n1_ref, f32[12,208,128]{2,1,0:T(8,128)S(1)} %get-tuple-element.159.root_ref, ...), custom_call_target="tpu_custom_call", output_to_operand_aliasing={{}: (7, {})} | custom-call | tf_op jit(solution)/shard_map/pallas_call | solution.py:531
  303.0 2.0 collective-permute-start.31
  305.0 2.8 collective-permute-start.32
  310.8 3.2 %copy.109 = bf16[4,3,197,768]{3,0,2,1:T(4,128)(2,1)} copy(bf16[4,3,197,768]{3,2,1,0:T(8,128)(2,1)S(1)} %bitcast.115) | data formatting | bytes 7262208
  314.0 3.2 %copy.110 = bf16[4,3,197,768]{3,0,2,1:T(4,128)(2,1)} copy(bf16[4,3,197,768]{3,2,1,0:T(8,128)(2,1)S(1)} %bitcast.109) | data formatting | bytes 7262208
  (157 shorter events, 59.9 us)
Async XLA Ops:
  5.4 16.7 %collective-permute-start = (bf16[24,3200]{1,0:T(8,128)(2,1)S(1)}, bf16[24,3200]{1,0:T(8,128)(2,1)S(1)}, u32[]{:S(2)}, u32[]{:S(2)}) collective-permute-start(bf16[24,3200]{1,0:T(8,128)(2,1)S(1)} %fusion.8), channel_id=1, source_target_pairs={{0,8},{1,9},{2,10},{3,11},{4,12},{5,13},{6,14},{7,15},{8,16},{9,17... | collective-permute-start | bytes 460808 | tf_op jit(solution)/shard_map/ppermute | solution.py:45
  8.5 13.6 %collective-permute-start.1 = (bf16[24,3200]{1,0:T(8,128)(2,1)S(1)}, bf16[24,3200]{1,0:T(8,128)(2,1)S(1)}, u32[]{:S(2)}, u32[]{:S(2)}) collective-permute-start(bf16[24,3200]{1,0:T(8,128)(2,1)S(1)} %fusion.8), channel_id=1, source_target_pairs={{0,16},{1,17},{2,18},{3,19},{4,20},{5,21},{6,22},{7,23},{8,24},{9,... | collective-permute-start | bytes 460808 | tf_op jit(solution)/shard_map/ppermute | solution.py:45
  11.1 11.0 %collective-permute-start.2 = (bf16[24,3200]{1,0:T(8,128)(2,1)S(1)}, bf16[24,3200]{1,0:T(8,128)(2,1)S(1)}, u32[]{:S(2)}, u32[]{:S(2)}) collective-permute-start(bf16[24,3200]{1,0:T(8,128)(2,1)S(1)} %fusion.8), channel_id=1, source_target_pairs={{0,24},{1,25},{2,26},{3,27},{4,28},{5,29},{6,30},{7,31},{8,0},{9,1... | collective-permute-start | bytes 460808 | tf_op jit(solution)/shard_map/ppermute | solution.py:45
  22.4 9.3 %collective-permute-start.4 = (bf16[4,24,1664]{2,1,0:T(8,128)(2,1)S(1)}, bf16[4,24,1664]{2,1,0:T(8,128)(2,1)S(1)}, u32[]{:S(2)}, u32[]{:S(2)}) collective-permute-start(bf16[4,24,1664]{2,1,0:T(8,128)(2,1)S(1)} %pad_maximum_fusion.6), channel_id=1, source_target_pairs={{0,2},{1,3},{2,0},{3,1},{4,6},{5,7},{6,4},{7,5},{8,10},{9,11},{10,... | collective-permute-start | bytes 958472 | tf_op jit(solution)/shard_map/ppermute | solution.py:45
  24.0 7.7 %collective-permute-start.3 = (bf16[4,24,1536]{2,1,0:T(8,128)(2,1)S(1)}, bf16[4,24,1536]{2,1,0:T(8,128)(2,1)S(1)}, u32[]{:S(2)}, u32[]{:S(2)}) collective-permute-start(bf16[4,24,1536]{2,1,0:T(8,128)(2,1)S(1)} %pad_maximum_fusion.9), channel_id=1, source_target_pairs={{0,4},{1,5},{2,6},{3,7},{4,0},{5,1},{6,2},{7,3},{8,12},{9,13},{10,... | collective-permute-start | bytes 884744 | tf_op jit(solution)/shard_map/ppermute | solution.py:45
  31.9 14.6 %collective-permute-start.6 = (bf16[4,2,24,1664]{3,2,1,0:T(8,128)(2,1)S(1)}, bf16[4,2,24,1664]{3,2,1,0:T(8,128)(2,1)S(1)}, u32[]{:S(2)}, u32[]{:S(2)}) collective-permute-start(bf16[4,2,24,1664]{3,2,1,0:T(8,128)(2,1)S(1)} %pad_maximum_fusion.4), channel_id=1, source_target_pairs={{0,4},{1,5},{2,6},{3,7},{4,0},{5,1},{6,2},{7,3},{8,12},{9,13},{10,... | collective-permute-start | bytes 1916936 | tf_op jit(solution)/shard_map/ppermute | solution.py:45
  33.7 12.8 %collective-permute-start.5 = (bf16[4,2,24,1536]{3,2,0,1:T(8,128)(2,1)S(1)}, bf16[4,2,24,1536]{3,2,0,1:T(8,128)(2,1)S(1)}, u32[]{:S(2)}, u32[]{:S(2)}) collective-permute-start(bf16[4,2,24,1536]{3,2,0,1:T(8,128)(2,1)S(1)} %pad_maximum_fusion.5), channel_id=1, source_target_pairs={{0,2},{1,3},{2,0},{3,1},{4,6},{5,7},{6,4},{7,5},{8,10},{9,11},{10,... | collective-permute-start | bytes 1769480 | tf_op jit(solution)/shard_map/ppermute | solution.py:45
  47.8 5.3 %collective-permute-start.10 = (bf16[4,2,2,24,1664]{4,3,2,1,0:T(8,128)(2,1)}, bf16[4,2,2,24,1664]{4,3,2,1,0:T(8,128)(2,1)}, u32[]{:S(2)}, u32[]{:S(2)}) collective-permute-start(bf16[4,2,2,24,1664]{4,3,2,1,0:T(8,128)(2,1)} %pad_maximum_fusion.2), channel_id=1, source_target_pairs={{0,1},{1,0},{2,3},{3,2},{4,5},{5,4},{6,7},{7,6},{8,9},{9,8},{10,11... | collective-permute-start | bytes 3833864 | tf_op jit(solution)/shard_map/ppermute | solution.py:45
  50.4 45.5 %collective-permute-start.7 = (bf16[2,768,384]{2,1,0:T(8,128)(2,1)}, bf16[2,768,384]{2,1,0:T(8,128)(2,1)}, u32[]{:S(2)}, u32[]{:S(2)}) collective-permute-start(bf16[2,768,384]{2,1,0:T(8,128)(2,1)} %refs_4_.1), channel_id=1, source_target_pairs={{0,4},{1,5},{2,6},{3,7},{4,0},{5,1},{6,2},{7,3},{8,12},{9,13},{10,... | collective-permute-start | bytes 3538952 | tf_op jit(solution)/shard_map/ppermute | solution.py:45
  51.5 52.4 %collective-permute-start.8 = (bf16[2,384,768]{2,1,0:T(8,128)(2,1)}, bf16[2,384,768]{2,1,0:T(8,128)(2,1)}, u32[]{:S(2)}, u32[]{:S(2)}) collective-permute-start(bf16[2,384,768]{2,1,0:T(8,128)(2,1)} %refs_6_.1), channel_id=1, source_target_pairs={{0,4},{1,5},{2,6},{3,7},{4,0},{5,1},{6,2},{7,3},{8,12},{9,13},{10,... | collective-permute-start | bytes 3538952 | tf_op jit(solution)/shard_map/ppermute | solution.py:45
  104.0 4.0 %collective-permute-start.11 = (bf16[24,1536]{1,0:T(8,128)(2,1)S(1)}, bf16[24,1536]{1,0:T(8,128)(2,1)S(1)}, u32[]{:S(2)}, u32[]{:S(2)}) collective-permute-start(bf16[24,1536]{1,0:T(8,128)(2,1)S(1)} %get-tuple-element.249), channel_id=1, source_target_pairs={{0,1},{1,2},{2,3},{3,0},{4,5},{5,6},{6,7},{7,4},{8,9},{9,10},{10,1... | collective-permute-start | bytes 221192 | tf_op jit(solution)/shard_map/ppermute | solution.py:45
  104.0 5.2 %collective-permute-start.12 = (bf16[24,1536]{1,0:T(8,128)(2,1)S(1)}, bf16[24,1536]{1,0:T(8,128)(2,1)S(1)}, u32[]{:S(2)}, u32[]{:S(2)}) collective-permute-start(bf16[24,1536]{1,0:T(8,128)(2,1)S(1)} %get-tuple-element.248), channel_id=1, source_target_pairs={{0,2},{1,3},{2,0},{3,1},{4,6},{5,7},{6,4},{7,5},{8,10},{9,11},{10,... | collective-permute-start | bytes 221192 | tf_op jit(solution)/shard_map/ppermute | solution.py:45
  105.1 4.1 %collective-permute-start.13 = (bf16[24,1536]{1,0:T(8,128)(2,1)S(1)}, bf16[24,1536]{1,0:T(8,128)(2,1)S(1)}, u32[]{:S(2)}, u32[]{:S(2)}) collective-permute-start(bf16[24,1536]{1,0:T(8,128)(2,1)S(1)} %get-tuple-element.247), channel_id=1, source_target_pairs={{0,3},{1,0},{2,1},{3,2},{4,7},{5,4},{6,5},{7,6},{8,11},{9,8},{10,9... | collective-permute-start | bytes 221192 | tf_op jit(solution)/shard_map/ppermute | solution.py:45
  109.2 19.6 %collective-permute-start.14 = (bf16[96,1536]{1,0:T(8,128)(2,1)S(1)}, bf16[96,1536]{1,0:T(8,128)(2,1)S(1)}, u32[]{:S(2)}, u32[]{:S(2)}) collective-permute-start(bf16[96,1536]{1,0:T(8,128)(2,1)S(1)} %pad_maximum_fusion.10.refs_0_), channel_id=1, source_target_pairs={{0,8},{1,9},{2,10},{3,11},{4,12},{5,13},{6,14},{7,15},{8,16},{9,17... | collective-permute-start | bytes 884744 | tf_op jit(solution)/shard_map/ppermute | solution.py:45
  114.2 19.5 %collective-permute-start.15 = (bf16[96,1536]{1,0:T(8,128)(2,1)S(1)}, bf16[96,1536]{1,0:T(8,128)(2,1)S(1)}, u32[]{:S(2)}, u32[]{:S(2)}) collective-permute-start(bf16[96,1536]{1,0:T(8,128)(2,1)S(1)} %pad_maximum_fusion.10.refs_0_), channel_id=1, source_target_pairs={{0,16},{1,17},{2,18},{3,19},{4,20},{5,21},{6,22},{7,23},{8,24},{9,... | collective-permute-start | bytes 884744 | tf_op jit(solution)/shard_map/ppermute | solution.py:45
  114.2 19.9 %collective-permute-start.16 = (bf16[96,1536]{1,0:T(8,128)(2,1)S(1)}, bf16[96,1536]{1,0:T(8,128)(2,1)S(1)}, u32[]{:S(2)}, u32[]{:S(2)}) collective-permute-start(bf16[96,1536]{1,0:T(8,128)(2,1)S(1)} %pad_maximum_fusion.10.refs_0_), channel_id=1, source_target_pairs={{0,24},{1,25},{2,26},{3,27},{4,28},{5,29},{6,30},{7,31},{8,0},{9,1... | collective-permute-start | bytes 884744 | tf_op jit(solution)/shard_map/ppermute | solution.py:45
  143.6 18.9 %collective-permute-start.17 = (bf16[96,1536]{1,0:T(8,128)(2,1)S(1)}, bf16[96,1536]{1,0:T(8,128)(2,1)S(1)}, u32[]{:S(2)}, u32[]{:S(2)}) collective-permute-start(bf16[96,1536]{1,0:T(8,128)(2,1)S(1)} %get-tuple-element.126), channel_id=1, source_target_pairs={{0,24},{1,25},{2,26},{3,27},{4,28},{5,29},{6,30},{7,31},{8,0},{9,1... | collective-permute-start | bytes 884744 | tf_op jit(solution)/shard_map/ppermute | solution.py:45
  152.9 24.8 %collective-permute-start.18 = (bf16[96,1536]{1,0:T(8,128)(2,1)S(1)}, bf16[96,1536]{1,0:T(8,128)(2,1)S(1)}, u32[]{:S(2)}, u32[]{:S(2)}) collective-permute-start(bf16[96,1536]{1,0:T(8,128)(2,1)S(1)} %get-tuple-element.127), channel_id=1, source_target_pairs={{0,16},{1,17},{2,18},{3,19},{4,20},{5,21},{6,22},{7,23},{8,24},{9,... | collective-permute-start | bytes 884744 | tf_op jit(solution)/shard_map/ppermute | solution.py:45
  152.9 24.8 %collective-permute-start.19 = (bf16[96,1536]{1,0:T(8,128)(2,1)S(1)}, bf16[96,1536]{1,0:T(8,128)(2,1)S(1)}, u32[]{:S(2)}, u32[]{:S(2)}) collective-permute-start(bf16[96,1536]{1,0:T(8,128)(2,1)S(1)} %get-tuple-element.128), channel_id=1, source_target_pairs={{0,8},{1,9},{2,10},{3,11},{4,12},{5,13},{6,14},{7,15},{8,16},{9,17... | collective-permute-start | bytes 884744 | tf_op jit(solution)/shard_map/ppermute | solution.py:45
  177.9 3.6 %collective-permute-start.22 = (bf16[24,1536]{1,0:T(8,128)(2,1)S(1)}, bf16[24,1536]{1,0:T(8,128)(2,1)S(1)}, u32[]{:S(2)}, u32[]{:S(2)}) collective-permute-start(bf16[24,1536]{1,0:T(8,128)(2,1)S(1)} %get-tuple-element.245), channel_id=1, source_target_pairs={{0,3},{1,0},{2,1},{3,2},{4,7},{5,4},{6,5},{7,6},{8,11},{9,8},{10,9... | collective-permute-start | bytes 221192 | tf_op jit(solution)/shard_map/ppermute | solution.py:45
  178.1 5.3 %collective-permute-start.23 = (bf16[24,1536]{1,0:T(8,128)(2,1)S(1)}, bf16[24,1536]{1,0:T(8,128)(2,1)S(1)}, u32[]{:S(2)}, u32[]{:S(2)}) collective-permute-start(bf16[24,1536]{1,0:T(8,128)(2,1)S(1)} %get-tuple-element.244), channel_id=1, source_target_pairs={{0,2},{1,3},{2,0},{3,1},{4,6},{5,7},{6,4},{7,5},{8,10},{9,11},{10,... | collective-permute-start | bytes 221192 | tf_op jit(solution)/shard_map/ppermute | solution.py:45
  179.1 4.7 %collective-permute-start.24 = (bf16[24,1536]{1,0:T(8,128)(2,1)S(1)}, bf16[24,1536]{1,0:T(8,128)(2,1)S(1)}, u32[]{:S(2)}, u32[]{:S(2)}) collective-permute-start(bf16[24,1536]{1,0:T(8,128)(2,1)S(1)} %get-tuple-element.243), channel_id=1, source_target_pairs={{0,1},{1,2},{2,3},{3,0},{4,5},{5,6},{6,7},{7,4},{8,9},{9,10},{10,1... | collective-permute-start | bytes 221192 | tf_op jit(solution)/shard_map/ppermute | solution.py:45
  179.4 49.8 %collective-permute-start.20 = (bf16[2,768,384]{2,1,0:T(8,128)(2,1)}, bf16[2,768,384]{2,1,0:T(8,128)(2,1)S(1)}, u32[]{:S(2)}, u32[]{:S(2)}) collective-permute-start(bf16[2,768,384]{2,1,0:T(8,128)(2,1)} %get-tuple-element.135), channel_id=1, source_target_pairs={{0,4},{1,5},{2,6},{3,7},{4,0},{5,1},{6,2},{7,3},{8,12},{9,13},{10,... | collective-permute-start | bytes 3538952 | tf_op jit(solution)/shard_map/ppermute | solution.py:45
  180.6 53.2 %collective-permute-start.21 = (bf16[2,384,768]{2,1,0:T(8,128)(2,1)}, bf16[2,384,768]{2,1,0:T(8,128)(2,1)S(1)}, u32[]{:S(2)}, u32[]{:S(2)}) collective-permute-start(bf16[2,384,768]{2,1,0:T(8,128)(2,1)} %get-tuple-element.136), channel_id=1, source_target_pairs={{0,4},{1,5},{2,6},{3,7},{4,0},{5,1},{6,2},{7,3},{8,12},{9,13},{10,... | collective-permute-start | bytes 3538952 | tf_op jit(solution)/shard_map/ppermute | solution.py:45
  260.3 6.1 %collective-permute-start.25 = (bf16[4,2,2,24,3200]{4,3,2,1,0:T(8,128)(2,1)}, bf16[4,2,2,24,3200]{4,3,2,1,0:T(8,128)(2,1)}, u32[]{:S(2)}, u32[]{:S(2)}) collective-permute-start(bf16[4,2,2,24,3200]{4,3,2,1,0:T(8,128)(2,1)} %dynamic-slice_bitcast_fusion), channel_id=1, source_target_pairs={{0,1},{1,0},{2,3},{3,2},{4,5},{5,4},{6,7},{7,6},{8,9},{9,8},{10,11... | collective-permute-start | bytes 7372808 | tf_op jit(solution)/shard_map/ppermute | solution.py:45
  269.0 17.7 %collective-permute-start.26 = (bf16[4,2,24,1664]{3,2,1,0:T(8,128)(2,1)S(1)}, bf16[4,2,24,1664]{3,2,1,0:T(8,128)(2,1)}, u32[]{:S(2)}, u32[]{:S(2)}) collective-permute-start(bf16[4,2,24,1664]{3,2,1,0:T(8,128)(2,1)S(1)} %dynamic-slice_bitcast_fusion.1), channel_id=1, source_target_pairs={{0,2},{1,3},{2,0},{3,1},{4,6},{5,7},{6,4},{7,5},{8,10},{9,11},{10,... | collective-permute-start | bytes 1916936 | tf_op jit(solution)/shard_map/ppermute | solution.py:45
  270.9 15.8 %collective-permute-start.27 = (bf16[4,2,24,1536]{3,2,1,0:T(8,128)(2,1)}, bf16[4,2,24,1536]{3,2,1,0:T(8,128)(2,1)}, u32[]{:S(2)}, u32[]{:S(2)}) collective-permute-start(bf16[4,2,24,1536]{3,2,1,0:T(8,128)(2,1)} %dynamic-slice_bitcast_fusion.2), channel_id=1, source_target_pairs={{0,4},{1,5},{2,6},{3,7},{4,0},{5,1},{6,2},{7,3},{8,12},{9,13},{10,... | collective-permute-start | bytes 1769480 | tf_op jit(solution)/shard_map/ppermute | solution.py:45
  288.1 13.3 %collective-permute-start.29 = (bf16[4,24,1536]{2,1,0:T(8,128)(2,1)S(1)}, bf16[4,24,1536]{2,1,0:T(8,128)(2,1)S(1)}, u32[]{:S(2)}, u32[]{:S(2)}) collective-permute-start(bf16[4,24,1536]{2,1,0:T(8,128)(2,1)S(1)} %dynamic-slice_bitcast_fusion.4), channel_id=1, source_target_pairs={{0,2},{1,3},{2,0},{3,1},{4,6},{5,7},{6,4},{7,5},{8,10},{9,11},{10,... | collective-permute-start | bytes 884744 | tf_op jit(solution)/shard_map/ppermute | solution.py:45
  290.4 11.0 %collective-permute-start.28 = (bf16[4,24,1664]{2,1,0:T(8,128)(2,1)S(1)}, bf16[4,24,1664]{2,1,0:T(8,128)(2,1)S(1)}, u32[]{:S(2)}, u32[]{:S(2)}) collective-permute-start(bf16[4,24,1664]{2,1,0:T(8,128)(2,1)S(1)} %dynamic-slice_bitcast_fusion.3), channel_id=1, source_target_pairs={{0,4},{1,5},{2,6},{3,7},{4,0},{5,1},{6,2},{7,3},{8,12},{9,13},{10,... | collective-permute-start | bytes 958472 | tf_op jit(solution)/shard_map/ppermute | solution.py:45
  301.7 15.6 %collective-permute-start.30 = (bf16[24,3200]{1,0:T(8,128)(2,1)S(1)}, bf16[24,3200]{1,0:T(8,128)(2,1)S(1)}, u32[]{:S(2)}, u32[]{:S(2)}) collective-permute-start(bf16[24,3200]{1,0:T(8,128)(2,1)S(1)} %get-tuple-element.234), channel_id=1, source_target_pairs={{0,8},{1,9},{2,10},{3,11},{4,12},{5,13},{6,14},{7,15},{8,16},{9,17... | collective-permute-start | bytes 460808 | tf_op jit(solution)/shard_map/ppermute | solution.py:45
  303.0 14.2 %collective-permute-start.31 = (bf16[24,3200]{1,0:T(8,128)(2,1)S(1)}, bf16[24,3200]{1,0:T(8,128)(2,1)S(1)}, u32[]{:S(2)}, u32[]{:S(2)}) collective-permute-start(bf16[24,3200]{1,0:T(8,128)(2,1)S(1)} %get-tuple-element.235), channel_id=1, source_target_pairs={{0,16},{1,17},{2,18},{3,19},{4,20},{5,21},{6,22},{7,23},{8,24},{9,... | collective-permute-start | bytes 460808 | tf_op jit(solution)/shard_map/ppermute | solution.py:45
  305.0 12.2 %collective-permute-start.32 = (bf16[24,3200]{1,0:T(8,128)(2,1)S(1)}, bf16[24,3200]{1,0:T(8,128)(2,1)S(1)}, u32[]{:S(2)}, u32[]{:S(2)}) collective-permute-start(bf16[24,3200]{1,0:T(8,128)(2,1)S(1)} %get-tuple-element.233), channel_id=1, source_target_pairs={{0,24},{1,25},{2,26},{3,27},{4,28},{5,29},{6,30},{7,31},{8,0},{9,1... | collective-permute-start | bytes 460808 | tf_op jit(solution)/shard_map/ppermute | solution.py:45
  (23 other events, 104.0 us)
where the time goes:
time: 324 us; the launch traced here: 320 us
  Pallas kernels  154 us (48%)
  waiting for transfers between devices  53.3 us (16%)
  starting transfers between devices  48.9 us (15%)
  local copies, waits for them, and re-layouts  45.9 us (14%)
  other arithmetic  17.1 us (5%)
    ppermute x33, waiting for transfers between devices, send(): return lax.ppermute(a, BOTH, self.perm(axis, k))  53.3 us
    ppermute x33, starting transfers between devices, send(): return lax.ppermute(a, BOTH, self.perm(axis, k))  48.9 us
    pallas_call x1, Pallas kernels, backward(): by_image(partial(backward_kernel, self.tokens, self.slots, self.place), n...  45.4 us
    pallas_call x1, Pallas kernels, forward(): by_image(partial(forward_kernel, self.tokens, self.slots, self.place), n,...  35.9 us
    pallas_call x3, Pallas kernels, input_back(): pl.pallas_call(partial(input_kernel, self.tokens), grid=((high - low) //...  24.4 us
    pallas_call x1, Pallas kernels, weight_grads(): pl.pallas_call(partial(weight_grad_kernel, self.slots), grid=(4 * third +...  22 us
    unnamed x51, local copies, waits for them, and re-layouts  21.8 us
    reshape x2, local copies, waits for them, and re-layouts, turned(): return array.reshape(-1, array.shape[-1]).T  12.2 us
  transfers between devices with their start and end apart: 33, of which 13 were waited for; matrix products, arithmetic and copies ran while one was open for 12% of the time, Pallas kernels for 38%

commit v1 on v0

--- a/solution.py
+++ b/solution.py
@@ -80,9 +80,13 @@
 
 def reduce_steps(grid, me, a, cut):
     s = grid.size
-    a = a.reshape(s["z"], 2, s["x"], 2, -1, a.shape[1])
-    got = yield [[grid.send(grid.block(a, "c", me, 1, 3), "c", 1)]]
-    a = (grid.block(a, "c", me, 0, 3).astype(F32) + got[0][0].astype(F32)).astype(BF16)
+    if len(a) == 1:
+        a = a[0].reshape(s["z"], 2, s["x"], 2, -1, a[0].shape[1])
+        own, other = (grid.block(a, "c", me, k, 3) for k in range(2))
+    else:
+        own, other = (p.reshape(s["z"], 2, s["x"], -1, p.shape[1]) for p in a)
+    got = yield [[grid.send(other, "c", 1)]]
+    a = (own.astype(F32) + got[0][0].astype(F32)).astype(BF16)
     parts = [a[..., :cut], a[..., cut:]]
     for axes, at in (("xy", (2, 1)), ("yx", (1, 1))):
         blocks = [[grid.block(p, x, me, k, i) for k in range(s[x])] for p, x, i in zip(parts, axes, at)]
@@ -389,13 +393,30 @@
         out_ref[k] = grad[k * rows : k * rows + tokens].astype(BF16)
 
 
-def weight_grad_kernel(slots, left_ref, left_out_ref, right_ref, right_out_ref, one_ref, two_ref, total_ref, small_ref, columns_ref, out_ref, norm_ref):
-    i, (features, tile) = pl.program_id(0), out_ref.shape
+def weight_grad_kernel(slots, devices, core, left_ref, left_out_hbm, right_ref, right_out_ref, one_ref, two_ref, total_ref, small_ref, columns_ref, *refs):
+    *outs, norm_ref, left_out_ref, arrived = refs
+    i, features, tile = pl.program_id(0), left_ref.shape[0], outs[0].shape[1]
     third = features // tile
 
+    def store(value):
+        if len(outs) == 1:
+            outs[0][...] = value.astype(BF16)
+            return
+        value = value.reshape(devices // 2, 2, -1, tile)
+        for k, ref in enumerate(outs):
+            half = jnp.where(core[0] == k, value[:, 0], value[:, 1])
+            ref[...] = half.reshape(-1, tile).astype(BF16)
+
+    later = pltpu.make_async_copy(left_out_hbm, left_out_ref, arrived)
+
     @pl.when(i == 0)
     def _():
+        later.start()
         norm_ref[...] = jnp.zeros_like(norm_ref)
+
+    @pl.when(i == 3 * third)
+    def _():
+        later.wait()
 
     def tokens(ref):
         return ref[...].reshape(-1, tile)
@@ -403,7 +424,7 @@
     def wide_part(w_ref):
         product = dot(left_ref[...], tokens(right_ref))
         total = total_ref[0:1]
-        out_ref[...] = (product * columns_ref[:, 0:1] + columns_ref[:, 1:2] * total).astype(BF16)
+        store(product * columns_ref[:, 0:1] + columns_ref[:, 1:2] * total)
         for low in range(0, tile, 128):
             cut = slice(low, low + 128)
             weights = w_ref[:, cut].astype(F32)
@@ -420,7 +441,7 @@
 
     @pl.when((i >= 3 * third) & (i < 4 * third))
     def _():
-        out_ref[...] = dot(left_out_ref[...], tokens(right_out_ref)).astype(BF16)
+        store(dot(left_out_ref[...], tokens(right_out_ref)))
 
     @pl.when(i == 4 * third)
     def _():
@@ -428,7 +449,7 @@
         gain = jnp.sum(norm_ref[:, :128], axis=1, keepdims=True)
         bias = jnp.sum(norm_ref[:, 128:], axis=1, keepdims=True)
         narrow = jnp.where(lane == slots + 2, gain, jnp.where(lane == slots + 3, bias, small_ref[...]))
-        out_ref[:, :128] = narrow.astype(BF16)
+        store(jnp.concatenate([narrow] * (tile // 128), axis=1))
 
 
 def own(*shape, low=0):
@@ -542,21 +563,28 @@
     def turned(self, array):
         return array.reshape(-1, array.shape[-1]).T
 
-    def weight_grads(self, left, left_out, right, right_out, one, two, total, small, columns, tile=256):
+    def weight_grads(self, core, devices, left, left_out, right, right_out, one, two, total, small, columns, tile=256):
         f, third = self.features, self.features // tile
+        apart = f // devices % 8 == 0
+        rows = [f // 2, f // 2] if apart else [f]
+
         def at(array, first, count):
             lead = array.shape[:-1]
-            return pl.BlockSpec(lead + (tile,), lambda i: (0,) * len(lead) + (jnp.clip(i - first, 0, count - 1),))
+            return pl.BlockSpec(lead + (tile,), lambda i, core: (0,) * len(lead) + (jnp.clip(i - first, 0, count - 1),))
+
         return pl.pallas_call(
-            partial(weight_grad_kernel, self.slots),
-            grid=(4 * third + 1,),
-            in_specs=[fixed(*left.shape), fixed(*left_out.shape), at(right, 0, 3 * third), at(right_out, 3 * third, third),
-                      at(one, 0, 2 * third), at(two, 2 * third, third), at(total, 0, 3 * third), fixed(*small.shape), fixed(*columns.shape)],
-            out_specs=pl.BlockSpec((f, tile), lambda i: (0, i)),
-            out_shape=shaped(f, 4 * f + 128),
-            scratch_shapes=[pltpu.VMEM((f, 256), F32)],
+            partial(weight_grad_kernel, self.slots, devices),
+            grid_spec=pltpu.PrefetchScalarGridSpec(
+                num_scalar_prefetch=1,
+                grid=(4 * third + 1,),
+                in_specs=[fixed(*left.shape), pl.BlockSpec(memory_space=pl.ANY), at(right, 0, 3 * third), at(right_out, 3 * third, third),
+                          at(one, 0, 2 * third), at(two, 2 * third, third), at(total, 0, 3 * third), fixed(*small.shape), fixed(*columns.shape)],
+                out_specs=[pl.BlockSpec((r, tile), lambda i, core: (0, i)) for r in rows],
+                scratch_shapes=[pltpu.VMEM((f, 256), F32), pltpu.VMEM(left_out.shape, BF16), pltpu.SemaphoreType.DMA],
+            ),
+            out_shape=[shaped(r, 4 * f + 128) for r in rows],
             compiler_params=params(LIMIT),
-        )(left, left_out, right, right_out, one, two, total, small, columns)
+        )(core[None], left, left_out, right, right_out, one, two, total, small, columns)
 
 
 def expert_forward(pieces, weights, images):
@@ -591,7 +619,8 @@
     per = slots // grid.m
     token = (jnp.arange(capacity)[None, :] < counts).astype(jnp.int32).reshape(-1)
     mixer = Mixer(grid, inputs, slots, token, me["e"])
-    vectors = jnp.stack([ln1_gain, ln1_bias, ln2_gain, ln2_bias], axis=1)
+    vectors = jnp.stack([ln1_gain, ln1_bias, ln2_gain, ln2_bias])
+    vectors = dot(vectors, jnp.eye(4, dtype=BF16), 0, 0).astype(BF16)
     packed = jnp.concatenate([w_qkv, w_out, wide(jnp.concatenate([phi, vectors], axis=1))], axis=1)
     flow = Flow(gather_steps(grid, me, packed, 2 * features))
     cot, token = beside([flow], token, lambda token: mixer.padded_cotangent(cotangent))
@@ -604,10 +633,10 @@
     turned = columns.T
     vec = jnp.pad(turned[slots : slots + 4], ((0, 4), (0, 0)))
 
-    made, token = beside([other], token, lambda token: mixer.forward(n1, cot, one, two, vec))
+    made, token = beside([], token, lambda token: mixer.forward(n1, cot, one, two, vec))
     triple, mixed, hidden, logits, slot = made
     flow = Flow(out_steps(grid, slot.astype(BF16)))
-    _, token = beside([flow], token)
+    _, token = beside([flow, other], token)
     lefts, token = beside([flow], token, lambda token: (mixer.turned(n1), mixer.turned(mixed)))
     pieces = flow.value
     back, kept = expert_forward(pieces, [w_up, other.value[0], w_down, other.value[1]], images)
@@ -621,14 +650,13 @@
     )
     outs, branch, grad_triple, total, small = made
     packed = mixer.weight_grads(
-        *lefts, grad_triple, branch, one, two, total, wide(small.T), columns[:, slots : slots + 2]
+        me["c"], grid.n * grid.m, *lefts, grad_triple, branch, one, two, total, wide(small.T), columns[:, slots : slots + 2]
     )
-    grad_up, grad_down = grad_up + other.value[0].astype(F32), grad_down + other.value[1].astype(F32)
-    flow = Flow(reduce_steps(grid, me, packed, padded(packed.shape[1] // 2, 128)))
-    grad_in, low = None, 0
+    flow = Flow(reduce_steps(grid, me, packed, padded(packed[0].shape[1] // 2, 128)))
+    grad_in, low, flows = None, 0, [flow]
     for count in SHARES:
         grad_in, token = beside(
-            [flow],
+            flows,
             token,
             lambda token: mixer.input_back(
                 low * images // 12, (low + count) * images // 12, grad_triple, n1, root, branch, one, two, vec, grad_in, max(images // 6, 1)
@@ -638,6 +666,7 @@
     while not flow.done:
         _, token = beside([flow], token)
     sums = flow.value
+    grad_up, grad_down = grad_up + other.value[0].astype(F32), grad_down + other.value[1].astype(F32)
     small = sums[:, 4 * features :]
     return (
         outs.reshape(inputs.shape),

time: 324 us -> 315 us (0.972); the launches traced: 320 us -> 315 us
  waiting for transfers between devices: 53.3 us -> 38.9 us
  Pallas kernels: 154 us -> 162 us
  starting transfers between devices: 48.9 us -> 54.9 us
  local copies, waits for them, and re-layouts: 45.9 us -> 40.2 us
    ppermute x33, waiting for transfers between devices: 53.3 us -> 38.9 us  [send(): return lax.ppermute(a, BOTH, self.perm(axis, k))]
    ppermute x33, starting transfers between devices: 48.9 us -> 54.9 us  [send(): return lax.ppermute(a, BOTH, self.perm(axis, k))]
    pallas_call x1, Pallas kernels: 45.4 us -> 50.6 us  [backward(): by_image(partial(backward_kernel, self.tokens, self.slots, self.place), n...]
    pallas_call x1, Pallas kernels: 35.9 us -> 39.9 us  [forward(): by_image(partial(forward_kernel, self.tokens, self.slots, self.place), n,...]
    squeeze x5 -> x4, local copies, waits for them, and re-layouts: 4.32 us -> 1.01 us  [block(): lax.dynamic_index_in_dim(a, (me[axis] + k) % self.size[axis], at, keepdim...]
  transfers between devices with their start and end apart: 33 -> 33, of which waited for: 13 -> 11; matrix products, arithmetic and copies ran while one was open for 12% -> 12% of each run, Pallas kernels for 38% -> 42%
where the time goes in v1:
time: 315 us
  Pallas kernels  162 us (51%)
  starting transfers between devices  54.9 us (17%)
  local copies, waits for them, and re-layouts  40.2 us (13%)
  waiting for transfers between devices  38.9 us (12%)
  other arithmetic  17.2 us (5%)
    ppermute x33, starting transfers between devices, send(): return lax.ppermute(a, BOTH, self.perm(axis, k))  54.9 us
    pallas_call x1, Pallas kernels, backward(): by_image(partial(backward_kernel, self.tokens, self.slots, self.place), n...  50.6 us
    pallas_call x1, Pallas kernels, forward(): by_image(partial(forward_kernel, self.tokens, self.slots, self.place), n,...  39.9 us
    ppermute x33, waiting for transfers between devices, send(): return lax.ppermute(a, BOTH, self.perm(axis, k))  38.9 us
    pallas_call x3, Pallas kernels, input_back(): pl.pallas_call(partial(input_kernel, self.tokens), grid=((high - low) //...  24.5 us
    unnamed x51, local copies, waits for them, and re-layouts  22.3 us
    pallas_call x1, Pallas kernels, weight_grads(): pl.pallas_call(partial(weight_grad_kernel, self.slots, devices), grid_spe...  21.2 us
    reshape x2, local copies, waits for them, and re-layouts, turned(): return array.reshape(-1, array.shape[-1]).T  12.3 us
  transfers between devices with their start and end apart: 33, of which 11 were waited for; matrix products, arithmetic and copies ran while one was open for 12% of the time, Pallas kernels for 42%

profile of v1, /device:TPU:0, one launch (start us, length us, event | category | flops | bytes accessed | tf_op | source)
XLA Modules:
  0.0 315.3 jit_solution(14836496927787574626)
XLA Ops:
  3.4 3.1 collective-permute-start
  6.5 2.6 collective-permute-start.1
  11.2 4.3 %copy.86.cot_ref = bf16[4,3,197,768]{3,2,1,0:T(8,128)(2,1)} copy(bf16[4,3,197,768]{3,0,2,1:T(4,128)(2,1)} %param.23) | data formatting | bytes 7262208 | tf_op args[11]
  15.5 4.6 %shard_map.203.cot_ref = bf16[12,208,768]{2,1,0:T(8,128)(2,1)} custom-call(bf16[4,3,197,768]{3,2,1,0:T(8,128)(2,1)} %copy.86.cot_ref), custom_call_target="tpu_custom_call" | custom-call | tf_op jit(solution)/shard_map/pallas_call | solution.py:506
  23.6 6.1 %collective-permute-done.3 = bf16[4,24,1536]{2,1,0:T(8,128)(2,1)S(1)} collective-permute-done((bf16[4,24,1536]{2,1,0:T(8,128)(2,1)S(1)}, bf16[4,24,1536]{2,1,0:T(8,128)(2,1)S(1)}, u32[]{:S(2)}, u32[]{:S(2)}) %collective-permute-start.3) | collective-permute-done | bytes 294944 | tf_op jit(solution)/shard_map/ppermute | solution.py:45
  32.5 2.3 copy.93.x_ref
  34.8 5.6 %shard_map.204 = (bf16[12,208,768]{2,1,0:T(8,128)(2,1)}, f32[12,208,128]{2,1,0:T(8,128)S(1)}) custom-call(bf16[4,3,197,768]{3,2,1,0:T(8,128)(2,1)} %copy.93.x_ref), custom_call_target="tpu_custom_call" | custom-call | tf_op jit(solution)/shard_map/pallas_call | solution.py:518
  40.3 4.2 %collective-permute-done.5 = bf16[4,2,24,1536]{3,2,0,1:T(8,128)(2,1)S(1)} collective-permute-done((bf16[4,2,24,1536]{3,2,0,1:T(8,128)(2,1)S(1)}, bf16[4,2,24,1536]{3,2,0,1:T(8,128)(2,1)S(1)}, u32[]{:S(2)}, u32[]{:S(2)}) %collective-permute-start.5) | collective-permute-done | bytes 589856 | tf_op jit(solution)/shard_map/ppermute | solution.py:45
  58.0 39.9 %shard_map.205 = (bf16[12,208,2304]{2,1,0:T(8,128)(2,1)}, bf16[12,208,768]{2,1,0:T(8,128)(2,1)}, f32[12,208,768]{2,1,0:T(8,128)}, f32[12,208,128]{2,1,0:T(8,128)S(1)}, f32[96,1536]{1,0:T(8,128)S(1)}) custom-call(s32[13]{0:T(128)S(1)} %pad_add_fusion.live, bf16[4,3,197,768]{3,2,1,0:T(8,128)(2,1)} %copy.93.x_ref, ...), custom_call_target="tpu_custom_call" | custom-call | flops 35332816896 | bytes 35332816 | tf_op jit(solution)/shard_map/pallas_call | solution.py:530
  98.6 3.3 %collective-permute-done.13.refs_7_ = bf16[2,384,768]{2,1,0:T(8,128)(2,1)} collective-permute-done((bf16[2,384,768]{2,1,0:T(8,128)(2,1)}, bf16[2,384,768]{2,1,0:T(8,128)(2,1)}, u32[]{:S(2)}, u32[]{:S(2)}) %collective-permute-start.13) | collective-permute-done | bytes 1179680 | tf_op jit(solution)/shard_map/ppermute | solution.py:45
  103.1 3.8 %collective-permute-start.14 = (bf16[96,1536]{1,0:T(8,128)(2,1)S(1)}, bf16[96,1536]{1,0:T(8,128)(2,1)S(1)}, u32[]{:S(2)}, u32[]{:S(2)}) collective-permute-start(bf16[96,1536]{1,0:T(8,128)(2,1)S(1)} %pad_maximum_fusion.10.refs_0_), channel_id=1, source_target_pairs={{0,8},{1,9},{2,10},{3,11},{4,12},{5,13},{6,14},{7,15},{8,16},{9,17... | collective-permute-start | bytes 884744 | tf_op jit(solution)/shard_map/ppermute | solution.py:45
  106.9 2.1 collective-permute-start.15
  109.0 2.8 collective-permute-start.16
  111.8 6.1 %copy.94 = bf16[2496,768]{0,1:T(8,128)(2,1)} copy(bf16[2496,768]{1,0:T(8,128)(2,1)} %bitcast.99) | data formatting | bytes 7667712 | tf_op jit(solution)/shard_map/reshape | solution.py:564
  118.0 6.2 %copy.95 = bf16[2496,768]{0,1:T(8,128)(2,1)} copy(bf16[2496,768]{1,0:T(8,128)(2,1)} %bitcast.108) | data formatting | bytes 7667712 | tf_op jit(solution)/shard_map/reshape | solution.py:564
  124.2 3.0 collective-permute-done.15.refs_2_
  128.0 8.8 %shard_map.206 = (bf16[96,1536]{1,0:T(8,128)(2,1)S(1)}, bf16[96,1536]{1,0:T(8,128)(2,1)S(1)}, bf16[96,1536]{1,0:T(8,128)(2,1)S(1)}, bf16[96,1536]{1,0:T(8,128)(2...) custom-call(bf16[96,1536]{1,0:T(8,128)(2,1)S(1)} %pad_maximum_fusion.10.refs_0_, ...), custom_call_target="tpu_custom_call" | custom-call | tf_op jit(solution)/shard_map/pallas_call | solution.py:594
  136.8 9.3 %collective-permute-start.17 = (bf16[96,1536]{1,0:T(8,128)(2,1)S(1)}, bf16[96,1536]{1,0:T(8,128)(2,1)S(1)}, u32[]{:S(2)}, u32[]{:S(2)}) collective-permute-start(bf16[96,1536]{1,0:T(8,128)(2,1)S(1)} %get-tuple-element.118), channel_id=1, source_target_pairs={{0,24},{1,25},{2,26},{3,27},{4,28},{5,29},{6,30},{7,31},{8,0},{9,1... | collective-permute-start | bytes 884744 | tf_op jit(solution)/shard_map/ppermute | solution.py:45
  148.7 7.1 %shard_map.207 = (f32[2,768,384]{2,1,0:T(8,128)}, f32[2,384,768]{2,1,0:T(8,128)}, bf16[2,768,384]{2,1,0:T(8,128)(2,1)}, bf16[2,384,768]{2,1,0:T(8,128)(2,1)}) custom-call(bf16[96,1536]{1,0:T(8,128)(2,1)S(1)} %pad_maximum_fusion.10.refs_0_, bf16[96,1536]{1,0:T(8,128)(2,1)S(1)} %collective-permute-done.14.refs_1_, bf16[96,1536]{1,0:T(8,128)(2,1)S(1)} %copy-done.1, ...), custom_call_target="tpu_custom_call" | custom-call | tf_op jit(solution)/shard_map/pallas_call | solution.py:603
  155.8 15.1 %collective-permute-done.18 = bf16[96,1536]{1,0:T(8,128)(2,1)S(1)} collective-permute-done((bf16[96,1536]{1,0:T(8,128)(2,1)S(1)}, bf16[96,1536]{1,0:T(8,128)(2,1)S(1)}, u32[]{:S(2)}, u32[]{:S(2)}) %collective-permute-start.18) | collective-permute-done | bytes 294944 | tf_op jit(solution)/shard_map/ppermute | solution.py:45
  172.8 3.2 %collective-permute-start.20 = (bf16[2,768,384]{2,1,0:T(8,128)(2,1)}, bf16[2,768,384]{2,1,0:T(8,128)(2,1)S(1)}, u32[]{:S(2)}, u32[]{:S(2)}) collective-permute-start(bf16[2,768,384]{2,1,0:T(8,128)(2,1)} %get-tuple-element.127), channel_id=1, source_target_pairs={{0,4},{1,5},{2,6},{3,7},{4,0},{5,1},{6,2},{7,3},{8,12},{9,13},{10,... | collective-permute-start | bytes 3538952 | tf_op jit(solution)/shard_map/ppermute | solution.py:45
  177.1 50.6 %shard_map.208 = (bf16[12,197,768]{2,1,0:T(8,128)(2,1)}, bf16[12,208,768]{2,1,0:T(8,128)(2,1)}, bf16[12,208,2304]{2,1,0:T(8,128)(2,1)}, f32[8,2304]{1,0:T(8,128)S(1)}, f32[16,768]{1,0:T(8,128)S(1)}) custom-call(s32[13]{0:T(128)S(1)} %pad_add_fusion.live, bf16[12,208,768]{2,1,0:T(8,128)(2,1)} %shard_map.203.cot_ref, ...), custom_call_target="tpu_custom_call" | custom-call | flops 35332816896 | bytes 35332816 | tf_op jit(solution)/shard_map/pallas_call | solution.py:541
  229.3 21.2 %shard_map.209 = (bf16[384,3200]{1,0:T(8,128)(2,1)}, bf16[384,3200]{1,0:T(8,128)(2,1)}) custom-call(s32[1]{0:T(128)} %bitcast.33.core, bf16[768,2496]{1,0:T(8,128)(2,1)} %bitcast.106, bf16[768,2496]{1,0:T(8,128)(2,1)} %bitcast.107, bf16[12,208,2304]{2,1,0:T(8,128)(2,1)} %get-tuple-element.147.right_ref.triple_ref, ...), custom_call_target="tpu_custom_call" | custom-call | tf_op jit(solution)/shard_map/pallas_call | solution.py:575
  250.6 6.0 %shard_map.210.refs_0_ = bf16[12,197,768]{2,1,0:T(8,128)(2,1)} custom-call(bf16[12,208,2304]{2,1,0:T(8,128)(2,1)} %get-tuple-element.147.right_ref.triple_ref, bf16[12,208,768]{2,1,0:T(8,128)(2,1)} %get-tuple-element.99.n1_ref, f32[12,208,128]{2,1,0:T(8,128)S(1)} %get-tuple-element.153.root_ref, ...), custom_call_target="tpu_custom_call" | custom-call | tf_op jit(solution)/shard_map/pallas_call | solution.py:552
  256.6 2.3 fusion
  262.6 10.3 %shard_map.211.refs_0_ = bf16[12,197,768]{2,1,0:T(8,128)(2,1)} custom-call(bf16[12,208,2304]{2,1,0:T(8,128)(2,1)} %get-tuple-element.147.right_ref.triple_ref, bf16[12,208,768]{2,1,0:T(8,128)(2,1)} %get-tuple-element.99.n1_ref, f32[12,208,128]{2,1,0:T(8,128)S(1)} %get-tuple-element.153.root_ref, ...), custom_call_target="tpu_custom_call", output_to_operand_aliasing={{}: (7, {})} | custom-call | tf_op jit(solution)/shard_map/pallas_call | solution.py:552
  272.9 4.0 %collective-permute-done.27 = bf16[4,2,24,1536]{3,2,1,0:T(8,128)(2,1)} collective-permute-done((bf16[4,2,24,1536]{3,2,1,0:T(8,128)(2,1)}, bf16[4,2,24,1536]{3,2,1,0:T(8,128)(2,1)}, u32[]{:S(2)}, u32[]{:S(2)}) %collective-permute-start.27) | collective-permute-done | bytes 589856 | tf_op jit(solution)/shard_map/ppermute | solution.py:45
  284.0 8.2 %shard_map.212 = bf16[12,197,768]{2,1,0:T(8,128)(2,1)} custom-call(bf16[12,208,2304]{2,1,0:T(8,128)(2,1)} %get-tuple-element.147.right_ref.triple_ref, bf16[12,208,768]{2,1,0:T(8,128)(2,1)} %get-tuple-element.99.n1_ref, f32[12,208,128]{2,1,0:T(8,128)S(1)} %get-tuple-element.153.root_ref, ...), custom_call_target="tpu_custom_call", output_to_operand_aliasing={{}: (7, {})} | custom-call | tf_op jit(solution)/shard_map/pallas_call | solution.py:552
  294.2 6.1 %collective-permute-start.31 = (bf16[24,3200]{1,0:T(8,128)(2,1)S(1)}, bf16[24,3200]{1,0:T(8,128)(2,1)S(1)}, u32[]{:S(2)}, u32[]{:S(2)}) collective-permute-start(bf16[24,3200]{1,0:T(8,128)(2,1)S(1)} %get-tuple-element.229), channel_id=1, source_target_pairs={{0,16},{1,17},{2,18},{3,19},{4,20},{5,21},{6,22},{7,23},{8,24},{9,... | collective-permute-start | bytes 460808 | tf_op jit(solution)/shard_map/ppermute | solution.py:45
  300.3 2.8 collective-permute-start.32
  306.0 3.2 %copy.98 = bf16[4,3,197,768]{3,0,2,1:T(4,128)(2,1)} copy(bf16[4,3,197,768]{3,2,1,0:T(8,128)(2,1)S(1)} %bitcast.109) | data formatting | bytes 7262208
  309.3 3.2 %copy.99 = bf16[4,3,197,768]{3,0,2,1:T(4,128)(2,1)} copy(bf16[4,3,197,768]{3,2,1,0:T(8,128)(2,1)S(1)} %bitcast.105) | data formatting | bytes 7262208
  (154 shorter events, 52.9 us)
Async XLA Ops:
  3.4 16.7 %collective-permute-start = (bf16[24,3200]{1,0:T(8,128)(2,1)S(1)}, bf16[24,3200]{1,0:T(8,128)(2,1)S(1)}, u32[]{:S(2)}, u32[]{:S(2)}) collective-permute-start(bf16[24,3200]{1,0:T(8,128)(2,1)S(1)} %pad_maximum_fusion.11), channel_id=1, source_target_pairs={{0,8},{1,9},{2,10},{3,11},{4,12},{5,13},{6,14},{7,15},{8,16},{9,17... | collective-permute-start | bytes 460808 | tf_op jit(solution)/shard_map/ppermute | solution.py:45
  6.5 13.6 %collective-permute-start.1 = (bf16[24,3200]{1,0:T(8,128)(2,1)S(1)}, bf16[24,3200]{1,0:T(8,128)(2,1)S(1)}, u32[]{:S(2)}, u32[]{:S(2)}) collective-permute-start(bf16[24,3200]{1,0:T(8,128)(2,1)S(1)} %pad_maximum_fusion.11), channel_id=1, source_target_pairs={{0,16},{1,17},{2,18},{3,19},{4,20},{5,21},{6,22},{7,23},{8,24},{9,... | collective-permute-start | bytes 460808 | tf_op jit(solution)/shard_map/ppermute | solution.py:45
  9.1 11.0 %collective-permute-start.2 = (bf16[24,3200]{1,0:T(8,128)(2,1)S(1)}, bf16[24,3200]{1,0:T(8,128)(2,1)S(1)}, u32[]{:S(2)}, u32[]{:S(2)}) collective-permute-start(bf16[24,3200]{1,0:T(8,128)(2,1)S(1)} %pad_maximum_fusion.11), channel_id=1, source_target_pairs={{0,24},{1,25},{2,26},{3,27},{4,28},{5,29},{6,30},{7,31},{8,0},{9,1... | collective-permute-start | bytes 460808 | tf_op jit(solution)/shard_map/ppermute | solution.py:45
  20.4 9.3 %collective-permute-start.4 = (bf16[4,24,1664]{2,1,0:T(8,128)(2,1)S(1)}, bf16[4,24,1664]{2,1,0:T(8,128)(2,1)S(1)}, u32[]{:S(2)}, u32[]{:S(2)}) collective-permute-start(bf16[4,24,1664]{2,1,0:T(8,128)(2,1)S(1)} %pad_maximum_fusion.6), channel_id=1, source_target_pairs={{0,2},{1,3},{2,0},{3,1},{4,6},{5,7},{6,4},{7,5},{8,10},{9,11},{10,... | collective-permute-start | bytes 958472 | tf_op jit(solution)/shard_map/ppermute | solution.py:45
  22.0 7.7 %collective-permute-start.3 = (bf16[4,24,1536]{2,1,0:T(8,128)(2,1)S(1)}, bf16[4,24,1536]{2,1,0:T(8,128)(2,1)S(1)}, u32[]{:S(2)}, u32[]{:S(2)}) collective-permute-start(bf16[4,24,1536]{2,1,0:T(8,128)(2,1)S(1)} %pad_maximum_fusion.9), channel_id=1, source_target_pairs={{0,4},{1,5},{2,6},{3,7},{4,0},{5,1},{6,2},{7,3},{8,12},{9,13},{10,... | collective-permute-start | bytes 884744 | tf_op jit(solution)/shard_map/ppermute | solution.py:45
  29.9 14.6 %collective-permute-start.6 = (bf16[4,2,24,1664]{3,2,1,0:T(8,128)(2,1)S(1)}, bf16[4,2,24,1664]{3,2,1,0:T(8,128)(2,1)S(1)}, u32[]{:S(2)}, u32[]{:S(2)}) collective-permute-start(bf16[4,2,24,1664]{3,2,1,0:T(8,128)(2,1)S(1)} %pad_maximum_fusion.4), channel_id=1, source_target_pairs={{0,4},{1,5},{2,6},{3,7},{4,0},{5,1},{6,2},{7,3},{8,12},{9,13},{10,... | collective-permute-start | bytes 1916936 | tf_op jit(solution)/shard_map/ppermute | solution.py:45
  31.7 12.8 %collective-permute-start.5 = (bf16[4,2,24,1536]{3,2,0,1:T(8,128)(2,1)S(1)}, bf16[4,2,24,1536]{3,2,0,1:T(8,128)(2,1)S(1)}, u32[]{:S(2)}, u32[]{:S(2)}) collective-permute-start(bf16[4,2,24,1536]{3,2,0,1:T(8,128)(2,1)S(1)} %pad_maximum_fusion.5), channel_id=1, source_target_pairs={{0,2},{1,3},{2,0},{3,1},{4,6},{5,7},{6,4},{7,5},{8,10},{9,11},{10,... | collective-permute-start | bytes 1769480 | tf_op jit(solution)/shard_map/ppermute | solution.py:45
  45.8 5.3 %collective-permute-start.8 = (bf16[4,2,2,24,1664]{4,3,2,1,0:T(8,128)(2,1)}, bf16[4,2,2,24,1664]{4,3,2,1,0:T(8,128)(2,1)}, u32[]{:S(2)}, u32[]{:S(2)}) collective-permute-start(bf16[4,2,2,24,1664]{4,3,2,1,0:T(8,128)(2,1)} %pad_maximum_fusion.2), channel_id=1, source_target_pairs={{0,1},{1,0},{2,3},{3,2},{4,5},{5,4},{6,7},{7,6},{8,9},{9,8},{10,11... | collective-permute-start | bytes 3833864 | tf_op jit(solution)/shard_map/ppermute | solution.py:45
  48.4 50.2 %collective-permute-start.12 = (bf16[2,768,384]{2,1,0:T(8,128)(2,1)}, bf16[2,768,384]{2,1,0:T(8,128)(2,1)}, u32[]{:S(2)}, u32[]{:S(2)}) collective-permute-start(bf16[2,768,384]{2,1,0:T(8,128)(2,1)} %refs_4_.1), channel_id=1, source_target_pairs={{0,4},{1,5},{2,6},{3,7},{4,0},{5,1},{6,2},{7,3},{8,12},{9,13},{10,... | collective-permute-start | bytes 3538952 | tf_op jit(solution)/shard_map/ppermute | solution.py:45
  49.5 52.4 %collective-permute-start.13 = (bf16[2,384,768]{2,1,0:T(8,128)(2,1)}, bf16[2,384,768]{2,1,0:T(8,128)(2,1)}, u32[]{:S(2)}, u32[]{:S(2)}) collective-permute-start(bf16[2,384,768]{2,1,0:T(8,128)(2,1)} %refs_6_.1), channel_id=1, source_target_pairs={{0,4},{1,5},{2,6},{3,7},{4,0},{5,1},{6,2},{7,3},{8,12},{9,13},{10,... | collective-permute-start | bytes 3538952 | tf_op jit(solution)/shard_map/ppermute | solution.py:45
  98.0 5.0 %collective-permute-start.10 = (bf16[24,1536]{1,0:T(8,128)(2,1)S(1)}, bf16[24,1536]{1,0:T(8,128)(2,1)S(1)}, u32[]{:S(2)}, u32[]{:S(2)}) collective-permute-start(bf16[24,1536]{1,0:T(8,128)(2,1)S(1)} %get-tuple-element.242), channel_id=1, source_target_pairs={{0,2},{1,3},{2,0},{3,1},{4,6},{5,7},{6,4},{7,5},{8,10},{9,11},{10,... | collective-permute-start | bytes 221192 | tf_op jit(solution)/shard_map/ppermute | solution.py:45
  98.1 5.0 %collective-permute-start.11 = (bf16[24,1536]{1,0:T(8,128)(2,1)S(1)}, bf16[24,1536]{1,0:T(8,128)(2,1)S(1)}, u32[]{:S(2)}, u32[]{:S(2)}) collective-permute-start(bf16[24,1536]{1,0:T(8,128)(2,1)S(1)} %get-tuple-element.241), channel_id=1, source_target_pairs={{0,3},{1,0},{2,1},{3,2},{4,7},{5,4},{6,5},{7,6},{8,11},{9,8},{10,9... | collective-permute-start | bytes 221192 | tf_op jit(solution)/shard_map/ppermute | solution.py:45
  98.1 4.9 %collective-permute-start.9 = (bf16[24,1536]{1,0:T(8,128)(2,1)S(1)}, bf16[24,1536]{1,0:T(8,128)(2,1)S(1)}, u32[]{:S(2)}, u32[]{:S(2)}) collective-permute-start(bf16[24,1536]{1,0:T(8,128)(2,1)S(1)} %get-tuple-element.243), channel_id=1, source_target_pairs={{0,1},{1,2},{2,3},{3,0},{4,5},{5,6},{6,7},{7,4},{8,9},{9,10},{10,1... | collective-permute-start | bytes 221192 | tf_op jit(solution)/shard_map/ppermute | solution.py:45
  103.1 21.1 %collective-permute-start.14 = (bf16[96,1536]{1,0:T(8,128)(2,1)S(1)}, bf16[96,1536]{1,0:T(8,128)(2,1)S(1)}, u32[]{:S(2)}, u32[]{:S(2)}) collective-permute-start(bf16[96,1536]{1,0:T(8,128)(2,1)S(1)} %pad_maximum_fusion.10.refs_0_), channel_id=1, source_target_pairs={{0,8},{1,9},{2,10},{3,11},{4,12},{5,13},{6,14},{7,15},{8,16},{9,17... | collective-permute-start | bytes 884744 | tf_op jit(solution)/shard_map/ppermute | solution.py:45
  106.9 20.3 %collective-permute-start.15 = (bf16[96,1536]{1,0:T(8,128)(2,1)S(1)}, bf16[96,1536]{1,0:T(8,128)(2,1)S(1)}, u32[]{:S(2)}, u32[]{:S(2)}) collective-permute-start(bf16[96,1536]{1,0:T(8,128)(2,1)S(1)} %pad_maximum_fusion.10.refs_0_), channel_id=1, source_target_pairs={{0,16},{1,17},{2,18},{3,19},{4,20},{5,21},{6,22},{7,23},{8,24},{9,... | collective-permute-start | bytes 884744 | tf_op jit(solution)/shard_map/ppermute | solution.py:45
  109.0 18.2 %collective-permute-start.16 = (bf16[96,1536]{1,0:T(8,128)(2,1)S(1)}, bf16[96,1536]{1,0:T(8,128)(2,1)S(1)}, u32[]{:S(2)}, u32[]{:S(2)}) collective-permute-start(bf16[96,1536]{1,0:T(8,128)(2,1)S(1)} %pad_maximum_fusion.10.refs_0_), channel_id=1, source_target_pairs={{0,24},{1,25},{2,26},{3,27},{4,28},{5,29},{6,30},{7,31},{8,0},{9,1... | collective-permute-start | bytes 884744 | tf_op jit(solution)/shard_map/ppermute | solution.py:45
  136.8 19.0 %collective-permute-start.17 = (bf16[96,1536]{1,0:T(8,128)(2,1)S(1)}, bf16[96,1536]{1,0:T(8,128)(2,1)S(1)}, u32[]{:S(2)}, u32[]{:S(2)}) collective-permute-start(bf16[96,1536]{1,0:T(8,128)(2,1)S(1)} %get-tuple-element.118), channel_id=1, source_target_pairs={{0,24},{1,25},{2,26},{3,27},{4,28},{5,29},{6,30},{7,31},{8,0},{9,1... | collective-permute-start | bytes 884744 | tf_op jit(solution)/shard_map/ppermute | solution.py:45
  146.2 24.7 %collective-permute-start.18 = (bf16[96,1536]{1,0:T(8,128)(2,1)S(1)}, bf16[96,1536]{1,0:T(8,128)(2,1)S(1)}, u32[]{:S(2)}, u32[]{:S(2)}) collective-permute-start(bf16[96,1536]{1,0:T(8,128)(2,1)S(1)} %get-tuple-element.119), channel_id=1, source_target_pairs={{0,16},{1,17},{2,18},{3,19},{4,20},{5,21},{6,22},{7,23},{8,24},{9,... | collective-permute-start | bytes 884744 | tf_op jit(solution)/shard_map/ppermute | solution.py:45
  146.2 24.7 %collective-permute-start.19 = (bf16[96,1536]{1,0:T(8,128)(2,1)S(1)}, bf16[96,1536]{1,0:T(8,128)(2,1)S(1)}, u32[]{:S(2)}, u32[]{:S(2)}) collective-permute-start(bf16[96,1536]{1,0:T(8,128)(2,1)S(1)} %get-tuple-element.120), channel_id=1, source_target_pairs={{0,8},{1,9},{2,10},{3,11},{4,12},{5,13},{6,14},{7,15},{8,16},{9,17... | collective-permute-start | bytes 884744 | tf_op jit(solution)/shard_map/ppermute | solution.py:45
  171.1 5.0 %collective-permute-start.22 = (bf16[24,1536]{1,0:T(8,128)(2,1)S(1)}, bf16[24,1536]{1,0:T(8,128)(2,1)S(1)}, u32[]{:S(2)}, u32[]{:S(2)}) collective-permute-start(bf16[24,1536]{1,0:T(8,128)(2,1)S(1)} %get-tuple-element.239), channel_id=1, source_target_pairs={{0,3},{1,0},{2,1},{3,2},{4,7},{5,4},{6,5},{7,6},{8,11},{9,8},{10,9... | collective-permute-start | bytes 221192 | tf_op jit(solution)/shard_map/ppermute | solution.py:45
  171.1 5.6 %collective-permute-start.23 = (bf16[24,1536]{1,0:T(8,128)(2,1)S(1)}, bf16[24,1536]{1,0:T(8,128)(2,1)S(1)}, u32[]{:S(2)}, u32[]{:S(2)}) collective-permute-start(bf16[24,1536]{1,0:T(8,128)(2,1)S(1)} %get-tuple-element.238), channel_id=1, source_target_pairs={{0,2},{1,3},{2,0},{3,1},{4,6},{5,7},{6,4},{7,5},{8,10},{9,11},{10,... | collective-permute-start | bytes 221192 | tf_op jit(solution)/shard_map/ppermute | solution.py:45
  172.4 4.6 %collective-permute-start.24 = (bf16[24,1536]{1,0:T(8,128)(2,1)S(1)}, bf16[24,1536]{1,0:T(8,128)(2,1)S(1)}, u32[]{:S(2)}, u32[]{:S(2)}) collective-permute-start(bf16[24,1536]{1,0:T(8,128)(2,1)S(1)} %get-tuple-element.237), channel_id=1, source_target_pairs={{0,1},{1,2},{2,3},{3,0},{4,5},{5,6},{6,7},{7,4},{8,9},{9,10},{10,1... | collective-permute-start | bytes 221192 | tf_op jit(solution)/shard_map/ppermute | solution.py:45
  172.8 54.9 %collective-permute-start.20 = (bf16[2,768,384]{2,1,0:T(8,128)(2,1)}, bf16[2,768,384]{2,1,0:T(8,128)(2,1)S(1)}, u32[]{:S(2)}, u32[]{:S(2)}) collective-permute-start(bf16[2,768,384]{2,1,0:T(8,128)(2,1)} %get-tuple-element.127), channel_id=1, source_target_pairs={{0,4},{1,5},{2,6},{3,7},{4,0},{5,1},{6,2},{7,3},{8,12},{9,13},{10,... | collective-permute-start | bytes 3538952 | tf_op jit(solution)/shard_map/ppermute | solution.py:45
  176.0 52.1 %collective-permute-start.21 = (bf16[2,384,768]{2,1,0:T(8,128)(2,1)}, bf16[2,384,768]{2,1,0:T(8,128)(2,1)S(1)}, u32[]{:S(2)}, u32[]{:S(2)}) collective-permute-start(bf16[2,384,768]{2,1,0:T(8,128)(2,1)} %get-tuple-element.128), channel_id=1, source_target_pairs={{0,4},{1,5},{2,6},{3,7},{4,0},{5,1},{6,2},{7,3},{8,12},{9,13},{10,... | collective-permute-start | bytes 3538952 | tf_op jit(solution)/shard_map/ppermute | solution.py:45
  250.5 6.1 %collective-permute-start.25 = (bf16[4,2,2,24,3200]{4,3,2,1,0:T(8,128)(2,1)}, bf16[4,2,2,24,3200]{4,3,2,1,0:T(8,128)(2,1)}, u32[]{:S(2)}, u32[]{:S(2)}) collective-permute-start(bf16[4,2,2,24,3200]{4,3,2,1,0:T(8,128)(2,1)} %bitcast.113), channel_id=1, source_target_pairs={{0,1},{1,0},{2,3},{3,2},{4,5},{5,4},{6,7},{7,6},{8,9},{9,8},{10,11... | collective-permute-start | bytes 7372808 | tf_op jit(solution)/shard_map/ppermute | solution.py:45
  259.2 17.7 %collective-permute-start.26 = (bf16[4,2,24,1664]{3,2,1,0:T(8,128)(2,1)S(1)}, bf16[4,2,24,1664]{3,2,1,0:T(8,128)(2,1)}, u32[]{:S(2)}, u32[]{:S(2)}) collective-permute-start(bf16[4,2,24,1664]{3,2,1,0:T(8,128)(2,1)S(1)} %dynamic-slice_bitcast_fusion), channel_id=1, source_target_pairs={{0,2},{1,3},{2,0},{3,1},{4,6},{5,7},{6,4},{7,5},{8,10},{9,11},{10,... | collective-permute-start | bytes 1916936 | tf_op jit(solution)/shard_map/ppermute | solution.py:45
  260.9 16.0 %collective-permute-start.27 = (bf16[4,2,24,1536]{3,2,1,0:T(8,128)(2,1)}, bf16[4,2,24,1536]{3,2,1,0:T(8,128)(2,1)}, u32[]{:S(2)}, u32[]{:S(2)}) collective-permute-start(bf16[4,2,24,1536]{3,2,1,0:T(8,128)(2,1)} %dynamic-slice_bitcast_fusion.1), channel_id=1, source_target_pairs={{0,4},{1,5},{2,6},{3,7},{4,0},{5,1},{6,2},{7,3},{8,12},{9,13},{10,... | collective-permute-start | bytes 1769480 | tf_op jit(solution)/shard_map/ppermute | solution.py:45
  278.3 14.0 %collective-permute-start.29 = (bf16[4,24,1536]{2,1,0:T(8,128)(2,1)S(1)}, bf16[4,24,1536]{2,1,0:T(8,128)(2,1)S(1)}, u32[]{:S(2)}, u32[]{:S(2)}) collective-permute-start(bf16[4,24,1536]{2,1,0:T(8,128)(2,1)S(1)} %dynamic-slice_bitcast_fusion.3), channel_id=1, source_target_pairs={{0,2},{1,3},{2,0},{3,1},{4,6},{5,7},{6,4},{7,5},{8,10},{9,11},{10,... | collective-permute-start | bytes 884744 | tf_op jit(solution)/shard_map/ppermute | solution.py:45
  280.6 11.6 %collective-permute-start.28 = (bf16[4,24,1664]{2,1,0:T(8,128)(2,1)S(1)}, bf16[4,24,1664]{2,1,0:T(8,128)(2,1)S(1)}, u32[]{:S(2)}, u32[]{:S(2)}) collective-permute-start(bf16[4,24,1664]{2,1,0:T(8,128)(2,1)S(1)} %dynamic-slice_bitcast_fusion.2), channel_id=1, source_target_pairs={{0,4},{1,5},{2,6},{3,7},{4,0},{5,1},{6,2},{7,3},{8,12},{9,13},{10,... | collective-permute-start | bytes 958472 | tf_op jit(solution)/shard_map/ppermute | solution.py:45
  292.5 20.0 %collective-permute-start.30 = (bf16[24,3200]{1,0:T(8,128)(2,1)S(1)}, bf16[24,3200]{1,0:T(8,128)(2,1)S(1)}, u32[]{:S(2)}, u32[]{:S(2)}) collective-permute-start(bf16[24,3200]{1,0:T(8,128)(2,1)S(1)} %get-tuple-element.228), channel_id=1, source_target_pairs={{0,8},{1,9},{2,10},{3,11},{4,12},{5,13},{6,14},{7,15},{8,16},{9,17... | collective-permute-start | bytes 460808 | tf_op jit(solution)/shard_map/ppermute | solution.py:45
  294.2 18.4 %collective-permute-start.31 = (bf16[24,3200]{1,0:T(8,128)(2,1)S(1)}, bf16[24,3200]{1,0:T(8,128)(2,1)S(1)}, u32[]{:S(2)}, u32[]{:S(2)}) collective-permute-start(bf16[24,3200]{1,0:T(8,128)(2,1)S(1)} %get-tuple-element.229), channel_id=1, source_target_pairs={{0,16},{1,17},{2,18},{3,19},{4,20},{5,21},{6,22},{7,23},{8,24},{9,... | collective-permute-start | bytes 460808 | tf_op jit(solution)/shard_map/ppermute | solution.py:45
  300.3 12.2 %collective-permute-start.32 = (bf16[24,3200]{1,0:T(8,128)(2,1)S(1)}, bf16[24,3200]{1,0:T(8,128)(2,1)S(1)}, u32[]{:S(2)}, u32[]{:S(2)}) collective-permute-start(bf16[24,3200]{1,0:T(8,128)(2,1)S(1)} %get-tuple-element.227), channel_id=1, source_target_pairs={{0,24},{1,25},{2,26},{3,27},{4,28},{5,29},{6,30},{7,31},{8,0},{9,1... | collective-permute-start | bytes 460808 | tf_op jit(solution)/shard_map/ppermute | solution.py:45
  (23 other events, 100.9 us)

commit v2 on v1

--- a/solution.py
+++ b/solution.py
@@ -13,7 +13,7 @@
 F32, BF16 = jnp.float32, jnp.bfloat16
 LOW = -1e30
 LIMIT = 52
-SHARES = (2, 6, 4)
+SHARES = (2, 8, 2)
 SMALL = 52
 GATHER_CUT = 1664
 
@@ -154,9 +154,10 @@
 
 def standardized(v):
     width = v.shape[-1]
-    center = v - jnp.sum(v, axis=-1, keepdims=True) * (1.0 / width)
+    mean = jnp.sum(v, axis=-1, keepdims=True) * (1.0 / width)
+    center = v - mean
     root = lax.rsqrt(jnp.sum(center * center, axis=-1, keepdims=True) * (1.0 / width) + EPSILON)
-    return center * root, root
+    return center * root, mean, root
 
 
 def lanes_of(head, width):
@@ -205,14 +206,14 @@
 
     for k in range(x_ref.shape[1]):
         pad_ref[k, :tokens] = x_ref[0, k].astype(F32)
-        n1, root = standardized(pad_ref[k])
+        n1, _, root = standardized(pad_ref[k])
         n1_ref[k] = n1.astype(BF16)
         root_ref[k] = jnp.broadcast_to(root, root_ref.shape[1:])
 
 
 def forward_kernel(
     tokens, slots, place, live, x_ref, n1_ref, cot_ref, one_ref, two_ref, vec_ref,
-    triple_ref, mixed_ref, hidden_ref, logits_ref, slot_ref, pad_ref,
+    triple_ref, mixed_ref, hidden_ref, kept_ref, slot_ref, pad_ref,
 ):
     i = pl.program_id(0)
     rows, features = pad_ref.shape
@@ -247,11 +248,12 @@
             mixed_ref[0, :, low : low + 128] = own_columns(total).astype(BF16)
         hidden = pad_ref[...] + dot(mixed_ref[0], two_ref[:, features : 2 * features])
         hidden_ref[0] = hidden
-        n2, _ = standardized(hidden)
+        n2, mean, root = standardized(hidden)
         normed_two = (n2 * vec_ref[2:3] + vec_ref[3:4]).astype(BF16)
         logits = dot(normed_two, two_ref[:, 2 * features :])
-        logits_ref[0] = logits
         dispatch, combine = routed(logits, tokens, slots)
+        for part, value in enumerate((dispatch, combine, mean, root)):
+            kept_ref[0, :, part * 128 : (part + 1) * 128] = jnp.broadcast_to(value, (rows, 128))
         slot_in = dot(dispatch.astype(BF16), normed_two, 0, 0)
         grad_slot = dot(combine.astype(BF16), cot_ref[0], 0, 0)
         for s in range(slots):
@@ -300,7 +302,7 @@
 
 
 def backward_kernel(
-    tokens, slots, place, live, cot_ref, triple_ref, hidden_ref, logits_ref, home_ref, two_ref, phit_ref, vec_ref,
+    tokens, slots, place, live, cot_ref, triple_ref, hidden_ref, kept_ref, home_ref, two_ref, phit_ref, vec_ref,
     out_ref, branch_ref, grad_ref, total_ref, small_ref, gm_ref,
 ):
     i = pl.program_id(0)
@@ -322,11 +324,11 @@
     @pl.when(live[i] != 0)
     def _():
         hidden = hidden_ref[0]
-        n2, root = standardized(hidden)
+        over_tokens, over_slots = kept_ref[0, :, :slots], kept_ref[0, :, 128 : 128 + slots]
+        mean, root = (jnp.concatenate([kept_ref[0, :, low : low + 128]] * (features // 128), axis=1) for low in (256, 384))
+        n2 = (hidden - mean) * root
         gain = vec_ref[2:3]
         normed_two = (n2 * gain + vec_ref[3:4]).astype(BF16)
-        over_tokens, over_slots = routed(logits_ref[0], tokens, slots)
-        over_tokens, over_slots = over_tokens[:, :slots], over_slots[:, :slots]
         dispatch, combine = over_tokens.astype(BF16), over_slots.astype(BF16)
         home = jnp.concatenate([home_ref[pl.ds(place(live, s, i), 1)] for s in range(slots)], axis=0).astype(BF16)
         slot_out, grad_in = home[:, :features], home[:, features:]
@@ -530,8 +532,8 @@
         return by_image(
             partial(forward_kernel, self.tokens, self.slots, self.place), n,
             [self.image(0), own(r, f), own(r, f), fixed(*one.shape), fixed(*two.shape), fixed(*vec.shape)],
-            [own(r, 3 * f), own(r, f), own(r, f), own(r, 128), fixed(self.slots * n, 2 * f)],
-            [shaped(n, r, 3 * f), shaped(n, r, f), shaped(n, r, f, dtype=F32), shaped(n, r, 128, dtype=F32), shaped(self.slots * n, 2 * f, dtype=F32)],
+            [own(r, 3 * f), own(r, f), own(r, f), own(r, 512), fixed(self.slots * n, 2 * f)],
+            [shaped(n, r, 3 * f), shaped(n, r, f), shaped(n, r, f, dtype=F32), shaped(n, r, 512, dtype=F32), shaped(self.slots * n, 2 * f, dtype=F32)],
             [self.pad], 3 * n * self.flops, LIMIT,
         )(self.live, self.inputs, n1, cot, one, two, vec)
 
@@ -540,7 +542,7 @@
         small = padded(self.slots + 2, 8)
         return by_image(
             partial(backward_kernel, self.tokens, self.slots, self.place), n,
-            [own(r, f), own(r, 3 * f), own(r, f), own(r, 128), fixed(self.slots * n, 2 * f), fixed(*two.shape), fixed(*phit.shape), fixed(*vec.shape)],
+            [own(r, f), own(r, 3 * f), own(r, f), own(r, 512), fixed(self.slots * n, 2 * f), fixed(*two.shape), fixed(*phit.shape), fixed(*vec.shape)],
             [self.made(), own(r, f), own(r, 3 * f), fixed(8, 3 * f), fixed(small, f)],
             [shaped(n, self.tokens, f), shaped(n, r, f), shaped(n, r, 3 * f), shaped(8, 3 * f, dtype=F32), shaped(small, f, dtype=F32)],
             [pltpu.VMEM((self.keys, f), BF16)], 3 * n * self.flops, LIMIT,
@@ -644,29 +646,32 @@
     made, token = beside([flow], token, lambda token: expert_grads(pieces, kept, w_up, w_down))
     grad_up, grad_down, *others = made
     _, token = beside([flow], token)
-    other = Flow(neighbour_steps(grid, others))
+    split = (per + 1) // 2
+    other = Flow(neighbour_steps(grid, [others[0], others[1][:split]]))
     made, token = beside(
         [other], token, lambda token: mixer.backward(cot, triple, hidden, logits, flow.value.astype(F32), two, turned.astype(BF16), vec)
     )
     outs, branch, grad_triple, total, small = made
-    packed = mixer.weight_grads(
+    rest = Flow(neighbour_steps(grid, lax.optimization_barrier((others[1][split:], token))[:1]))
+    packed, token = beside([rest], token, lambda token: mixer.weight_grads(
         me["c"], grid.n * grid.m, *lefts, grad_triple, branch, one, two, total, wide(small.T), columns[:, slots : slots + 2]
-    )
+    ))
     flow = Flow(reduce_steps(grid, me, packed, padded(packed[0].shape[1] // 2, 128)))
     grad_in, low, flows = None, 0, [flow]
     for count in SHARES:
-        grad_in, token = beside(
+        (grad_in, outs), token = beside(
             flows,
             token,
-            lambda token: mixer.input_back(
+            lambda token: (mixer.input_back(
                 low * images // 12, (low + count) * images // 12, grad_triple, n1, root, branch, one, two, vec, grad_in, max(images // 6, 1)
-            ),
+            ), outs),
         )
         low += count
     while not flow.done:
         _, token = beside([flow], token)
     sums = flow.value
-    grad_up, grad_down = grad_up + other.value[0].astype(F32), grad_down + other.value[1].astype(F32)
+    grad_up = grad_up + other.value[0].astype(F32)
+    grad_down = grad_down + jnp.concatenate([other.value[1], rest.value[0]], axis=0).astype(F32)
     small = sums[:, 4 * features :]
     return (
         outs.reshape(inputs.shape),

time: 315 us -> 306 us (0.971)
  Pallas kernels: 162 us -> 150 us
    pallas_call x1, Pallas kernels: 50.6 us -> 42.3 us  [backward(): by_image(partial(backward_kernel, self.tokens, self.slots, self.place), n...]
    pallas_call x1, Pallas kernels: 39.9 us -> 36 us  [forward(): by_image(partial(forward_kernel, self.tokens, self.slots, self.place), n,...]
    ppermute x33 -> x34, starting transfers between devices: 54.9 us -> 52.5 us  [send(): return lax.ppermute(a, BOTH, self.perm(axis, k))]
    ppermute x33 -> x34, waiting for transfers between devices: 38.9 us -> 41.1 us  [send(): return lax.ppermute(a, BOTH, self.perm(axis, k))]
    unnamed x51 -> x57, local copies, waits for them, and re-layouts: 22.3 us -> 22.6 us
  transfers between devices with their start and end apart: 33 -> 34, of which waited for: 11 -> 12; matrix products, arithmetic and copies ran while one was open for 12% -> 13% of each run, Pallas kernels for 42% -> 46%
where the time goes in v2:
time: 306 us; the launch traced here: 303 us
  Pallas kernels  150 us (49%)
  starting transfers between devices  52.5 us (17%)
  waiting for transfers between devices  41.1 us (13%)
  local copies, waits for them, and re-layouts  40.6 us (13%)
  other arithmetic  17.2 us (6%)
    ppermute x34, starting transfers between devices, send(): return lax.ppermute(a, BOTH, self.perm(axis, k))  52.5 us
    pallas_call x1, Pallas kernels, backward(): by_image(partial(backward_kernel, self.tokens, self.slots, self.place), n...  42.3 us
    ppermute x34, waiting for transfers between devices, send(): return lax.ppermute(a, BOTH, self.perm(axis, k))  41.1 us
    pallas_call x1, Pallas kernels, forward(): by_image(partial(forward_kernel, self.tokens, self.slots, self.place), n,...  36 us
    pallas_call x3, Pallas kernels, input_back(): pl.pallas_call(partial(input_kernel, self.tokens), grid=((high - low) //...  24.3 us
    unnamed x57, local copies, waits for them, and re-layouts  22.6 us
    pallas_call x1, Pallas kernels, weight_grads(): pl.pallas_call(partial(weight_grad_kernel, self.slots, devices), grid_spe...  21.2 us
    reshape x2, local copies, waits for them, and re-layouts, turned(): return array.reshape(-1, array.shape[-1]).T  12.3 us
  transfers between devices with their start and end apart: 34, of which 12 were waited for; matrix products, arithmetic and copies ran while one was open for 13% of the time, Pallas kernels for 46%

profile of v2, /device:TPU:0, one launch (start us, length us, event | category | flops | bytes accessed | tf_op | source)
XLA Modules:
  0.0 303.3 jit_solution(5116420095907602694)
XLA Ops:
  3.4 3.1 %collective-permute-start = (bf16[24,3200]{1,0:T(8,128)(2,1)S(1)}, bf16[24,3200]{1,0:T(8,128)(2,1)S(1)}, u32[]{:S(2)}, u32[]{:S(2)}) collective-permute-start(bf16[24,3200]{1,0:T(8,128)(2,1)S(1)} %pad_maximum_fusion.11), channel_id=1, source_target_pairs={{0,8},{1,9},{2,10},{3,11},{4,12},{5,13},{6,14},{7,15},{8,16},{9,17... | collective-permute-start | bytes 460808 | tf_op jit(solution)/shard_map/ppermute | solution.py:45
  6.5 2.6 collective-permute-start.1
  11.2 4.3 %copy.86.cot_ref = bf16[4,3,197,768]{3,2,1,0:T(8,128)(2,1)} copy(bf16[4,3,197,768]{3,0,2,1:T(4,128)(2,1)} %param.23) | data formatting | bytes 7262208 | tf_op args[11]
  15.5 4.5 %shard_map.203.cot_ref = bf16[12,208,768]{2,1,0:T(8,128)(2,1)} custom-call(bf16[4,3,197,768]{3,2,1,0:T(8,128)(2,1)} %copy.86.cot_ref), custom_call_target="tpu_custom_call" | custom-call | tf_op jit(solution)/shard_map/pallas_call | solution.py:508
  23.6 6.1 %collective-permute-done.3 = bf16[4,24,1536]{2,1,0:T(8,128)(2,1)S(1)} collective-permute-done((bf16[4,24,1536]{2,1,0:T(8,128)(2,1)S(1)}, bf16[4,24,1536]{2,1,0:T(8,128)(2,1)S(1)}, u32[]{:S(2)}, u32[]{:S(2)}) %collective-permute-start.3) | collective-permute-done | bytes 294944 | tf_op jit(solution)/shard_map/ppermute | solution.py:45
  32.4 2.3 copy.93.x_ref
  34.7 5.5 %shard_map.204 = (bf16[12,208,768]{2,1,0:T(8,128)(2,1)}, f32[12,208,128]{2,1,0:T(8,128)S(1)}) custom-call(bf16[4,3,197,768]{3,2,1,0:T(8,128)(2,1)} %copy.93.x_ref), custom_call_target="tpu_custom_call" | custom-call | tf_op jit(solution)/shard_map/pallas_call | solution.py:520
  40.3 4.2 %collective-permute-done.5 = bf16[4,2,24,1536]{3,2,0,1:T(8,128)(2,1)S(1)} collective-permute-done((bf16[4,2,24,1536]{3,2,0,1:T(8,128)(2,1)S(1)}, bf16[4,2,24,1536]{3,2,0,1:T(8,128)(2,1)S(1)}, u32[]{:S(2)}, u32[]{:S(2)}) %collective-permute-start.5) | collective-permute-done | bytes 589856 | tf_op jit(solution)/shard_map/ppermute | solution.py:45
  58.0 36.0 %shard_map.205 = (bf16[12,208,2304]{2,1,0:T(8,128)(2,1)}, bf16[12,208,768]{2,1,0:T(8,128)(2,1)}, f32[12,208,768]{2,1,0:T(8,128)}, f32[12,208,512]{2,1,0:T(8,128)}, f32[96,1536]{1,0:T(8,128)S(1)}) custom-call(s32[13]{0:T(128)S(1)} %pad_add_fusion.live, bf16[4,3,197,768]{3,2,1,0:T(8,128)(2,1)} %copy.93.x_ref, bf16[12,208,768]{2,1,0:T(8,128)(2,1)} %get-tuple-element.118.n1_ref, ...), custom_call_target="tpu_custom_call" | custom-call | flops 35332816896 | bytes 35332816 | tf_op jit(solution)/shard_map/pallas_call | solution.py:532
  95.8 4.2 %collective-permute-start.11 = (bf16[24,1536]{1,0:T(8,128)(2,1)S(1)}, bf16[24,1536]{1,0:T(8,128)(2,1)S(1)}, u32[]{:S(2)}, u32[]{:S(2)}) collective-permute-start(bf16[24,1536]{1,0:T(8,128)(2,1)S(1)} %get-tuple-element.281), channel_id=1, source_target_pairs={{0,3},{1,0},{2,1},{3,2},{4,7},{5,4},{6,5},{7,6},{8,11},{9,8},{10,9... | collective-permute-start | bytes 221192 | tf_op jit(solution)/shard_map/ppermute | solution.py:45
  103.8 3.8 %collective-permute-start.14 = (bf16[96,1536]{1,0:T(8,128)(2,1)S(1)}, bf16[96,1536]{1,0:T(8,128)(2,1)S(1)}, u32[]{:S(2)}, u32[]{:S(2)}) collective-permute-start(bf16[96,1536]{1,0:T(8,128)(2,1)S(1)} %pad_maximum_fusion.10.refs_0_), channel_id=1, source_target_pairs={{0,8},{1,9},{2,10},{3,11},{4,12},{5,13},{6,14},{7,15},{8,16},{9,17... | collective-permute-start | bytes 884744 | tf_op jit(solution)/shard_map/ppermute | solution.py:45
  107.7 2.3 collective-permute-start.16
  110.0 6.2 %copy.94 = bf16[2496,768]{0,1:T(8,128)(2,1)} copy(bf16[2496,768]{1,0:T(8,128)(2,1)} %bitcast.99) | data formatting | bytes 7667712 | tf_op jit(solution)/shard_map/reshape | solution.py:566
  116.2 6.1 %copy.95 = bf16[2496,768]{0,1:T(8,128)(2,1)} copy(bf16[2496,768]{1,0:T(8,128)(2,1)} %bitcast.108) | data formatting | bytes 7667712 | tf_op jit(solution)/shard_map/reshape | solution.py:566
  122.3 5.3 %collective-permute-done.15.refs_2_ = bf16[96,1536]{1,0:T(8,128)(2,1)S(1)} collective-permute-done((bf16[96,1536]{1,0:T(8,128)(2,1)S(1)}, bf16[96,1536]{1,0:T(8,128)(2,1)S(1)}, u32[]{:S(2)}, u32[]{:S(2)}) %collective-permute-start.15) | collective-permute-done | bytes 294944 | tf_op jit(solution)/shard_map/ppermute | solution.py:45
  128.5 8.8 %shard_map.206 = (bf16[96,1536]{1,0:T(8,128)(2,1)S(1)}, bf16[96,1536]{1,0:T(8,128)(2,1)S(1)}, bf16[96,1536]{1,0:T(8,128)(2,1)S(1)}, bf16[96,1536]{1,0:T(8,128)(2...) custom-call(bf16[96,1536]{1,0:T(8,128)(2,1)S(1)} %pad_maximum_fusion.10.refs_0_, ...), custom_call_target="tpu_custom_call" | custom-call | tf_op jit(solution)/shard_map/pallas_call | solution.py:596
  137.3 8.5 %collective-permute-start.17 = (bf16[96,1536]{1,0:T(8,128)(2,1)S(1)}, bf16[96,1536]{1,0:T(8,128)(2,1)S(1)}, u32[]{:S(2)}, u32[]{:S(2)}) collective-permute-start(bf16[96,1536]{1,0:T(8,128)(2,1)S(1)} %get-tuple-element.145), channel_id=1, source_target_pairs={{0,24},{1,25},{2,26},{3,27},{4,28},{5,29},{6,30},{7,31},{8,0},{9,1... | collective-permute-start | bytes 884744 | tf_op jit(solution)/shard_map/ppermute | solution.py:45
  148.3 7.2 %shard_map.207 = (f32[2,768,384]{2,1,0:T(8,128)}, f32[2,384,768]{2,1,0:T(8,128)}, bf16[2,768,384]{2,1,0:T(8,128)(2,1)}, bf16[2,384,768]{2,1,0:T(8,128)(2,1)}) custom-call(bf16[96,1536]{1,0:T(8,128)(2,1)S(1)} %pad_maximum_fusion.10.refs_0_, bf16[96,1536]{1,0:T(8,128)(2,1)S(1)} %collective-permute-done.14.refs_1_, bf16[96,1536]{1,0:T(8,128)(2,1)S(1)} %copy-done.1, ...), custom_call_target="tpu_custom_call" | custom-call | tf_op jit(solution)/shard_map/pallas_call | solution.py:605
  155.5 15.8 %collective-permute-done.18 = bf16[96,1536]{1,0:T(8,128)(2,1)S(1)} collective-permute-done((bf16[96,1536]{1,0:T(8,128)(2,1)S(1)}, bf16[96,1536]{1,0:T(8,128)(2,1)S(1)}, u32[]{:S(2)}, u32[]{:S(2)}) %collective-permute-start.18) | collective-permute-done | bytes 294944 | tf_op jit(solution)/shard_map/ppermute | solution.py:45
  172.5 2.1 collective-permute-start.21
  177.1 42.3 %shard_map.208 = (bf16[12,197,768]{2,1,0:T(8,128)(2,1)}, bf16[12,208,768]{2,1,0:T(8,128)(2,1)}, bf16[12,208,2304]{2,1,0:T(8,128)(2,1)}, f32[8,2304]{1,0:T(8,128)S(1)}, f32[16,768]{1,0:T(8,128)S(1)}) custom-call(s32[13]{0:T(128)S(1)} %pad_add_fusion.live, bf16[12,208,768]{2,1,0:T(8,128)(2,1)} %shard_map.203.cot_ref, ...), custom_call_target="tpu_custom_call" | custom-call | flops 35332816896 | bytes 35332816 | tf_op jit(solution)/shard_map/pallas_call | solution.py:543
  221.1 21.2 %shard_map.209 = (bf16[384,3200]{1,0:T(8,128)(2,1)}, bf16[384,3200]{1,0:T(8,128)(2,1)}) custom-call(s32[1]{0:T(128)} %bitcast.32.core, bf16[768,2496]{1,0:T(8,128)(2,1)} %bitcast.106, bf16[768,2496]{1,0:T(8,128)(2,1)} %bitcast.107, bf16[12,208,2304]{2,1,0:T(8,128)(2,1)} %get-tuple-element.178.right_ref.triple_ref, ...), custom_call_target="tpu_custom_call" | custom-call | tf_op jit(solution)/shard_map/pallas_call | solution.py:577
  242.3 5.5 %collective-permute-start.26 = (bf16[4,2,2,24,3200]{4,3,2,1,0:T(8,128)(2,1)}, bf16[4,2,2,24,3200]{4,3,2,1,0:T(8,128)(2,1)}, u32[]{:S(2)}, u32[]{:S(2)}) collective-permute-start(bf16[4,2,2,24,3200]{4,3,2,1,0:T(8,128)(2,1)} %bitcast.113), channel_id=1, source_target_pairs={{0,1},{1,0},{2,3},{3,2},{4,5},{5,4},{6,7},{7,6},{8,9},{9,8},{10,11... | collective-permute-start | bytes 7372808 | tf_op jit(solution)/shard_map/ppermute | solution.py:45
  247.8 6.0 %shard_map.210.refs_0_ = bf16[12,197,768]{2,1,0:T(8,128)(2,1)} custom-call(bf16[12,208,2304]{2,1,0:T(8,128)(2,1)} %get-tuple-element.178.right_ref.triple_ref, bf16[12,208,768]{2,1,0:T(8,128)(2,1)} %get-tuple-element.118.n1_ref, f32[12,208,128]{2,1,0:T(8,128)S(1)} %get-tuple-element.186.root_ref, ...), custom_call_target="tpu_custom_call" | custom-call | tf_op jit(solution)/shard_map/pallas_call | solution.py:554
  253.8 2.3 fusion
  258.7 12.4 %shard_map.211.refs_0_ = bf16[12,197,768]{2,1,0:T(8,128)(2,1)} custom-call(bf16[12,208,2304]{2,1,0:T(8,128)(2,1)} %get-tuple-element.178.right_ref.triple_ref, bf16[12,208,768]{2,1,0:T(8,128)(2,1)} %get-tuple-element.118.n1_ref, f32[12,208,128]{2,1,0:T(8,128)S(1)} %get-tuple-element.186.root_ref, ...), custom_call_target="tpu_custom_call", output_to_operand_aliasing={{}: (7, {})} | custom-call | tf_op jit(solution)/shard_map/pallas_call | solution.py:554
  271.1 2.6 collective-permute-done.28
  279.7 5.9 %shard_map.212 = bf16[12,197,768]{2,1,0:T(8,128)(2,1)} custom-call(bf16[12,208,2304]{2,1,0:T(8,128)(2,1)} %get-tuple-element.178.right_ref.triple_ref, bf16[12,208,768]{2,1,0:T(8,128)(2,1)} %get-tuple-element.118.n1_ref, f32[12,208,128]{2,1,0:T(8,128)S(1)} %get-tuple-element.186.root_ref, ...), custom_call_target="tpu_custom_call", output_to_operand_aliasing={{}: (7, {})} | custom-call | tf_op jit(solution)/shard_map/pallas_call | solution.py:554
  286.1 2.2 collective-permute-start.32
  288.2 2.8 collective-permute-start.33
  294.0 3.2 %copy.98 = bf16[4,3,197,768]{3,0,2,1:T(4,128)(2,1)} copy(bf16[4,3,197,768]{3,2,1,0:T(8,128)(2,1)S(1)} %bitcast.109) | data formatting | bytes 7262208
  297.2 3.2 %copy.99 = bf16[4,3,197,768]{3,0,2,1:T(4,128)(2,1)} copy(bf16[4,3,197,768]{3,2,1,0:T(8,128)(2,1)S(1)} %bitcast.105) | data formatting | bytes 7262208
  (163 shorter events, 53.5 us)
Async XLA Ops:
  3.4 16.7 %collective-permute-start = (bf16[24,3200]{1,0:T(8,128)(2,1)S(1)}, bf16[24,3200]{1,0:T(8,128)(2,1)S(1)}, u32[]{:S(2)}, u32[]{:S(2)}) collective-permute-start(bf16[24,3200]{1,0:T(8,128)(2,1)S(1)} %pad_maximum_fusion.11), channel_id=1, source_target_pairs={{0,8},{1,9},{2,10},{3,11},{4,12},{5,13},{6,14},{7,15},{8,16},{9,17... | collective-permute-start | bytes 460808 | tf_op jit(solution)/shard_map/ppermute | solution.py:45
  6.5 13.6 %collective-permute-start.1 = (bf16[24,3200]{1,0:T(8,128)(2,1)S(1)}, bf16[24,3200]{1,0:T(8,128)(2,1)S(1)}, u32[]{:S(2)}, u32[]{:S(2)}) collective-permute-start(bf16[24,3200]{1,0:T(8,128)(2,1)S(1)} %pad_maximum_fusion.11), channel_id=1, source_target_pairs={{0,16},{1,17},{2,18},{3,19},{4,20},{5,21},{6,22},{7,23},{8,24},{9,... | collective-permute-start | bytes 460808 | tf_op jit(solution)/shard_map/ppermute | solution.py:45
  9.1 11.0 %collective-permute-start.2 = (bf16[24,3200]{1,0:T(8,128)(2,1)S(1)}, bf16[24,3200]{1,0:T(8,128)(2,1)S(1)}, u32[]{:S(2)}, u32[]{:S(2)}) collective-permute-start(bf16[24,3200]{1,0:T(8,128)(2,1)S(1)} %pad_maximum_fusion.11), channel_id=1, source_target_pairs={{0,24},{1,25},{2,26},{3,27},{4,28},{5,29},{6,30},{7,31},{8,0},{9,1... | collective-permute-start | bytes 460808 | tf_op jit(solution)/shard_map/ppermute | solution.py:45
  20.4 9.3 %collective-permute-start.4 = (bf16[4,24,1664]{2,1,0:T(8,128)(2,1)S(1)}, bf16[4,24,1664]{2,1,0:T(8,128)(2,1)S(1)}, u32[]{:S(2)}, u32[]{:S(2)}) collective-permute-start(bf16[4,24,1664]{2,1,0:T(8,128)(2,1)S(1)} %pad_maximum_fusion.6), channel_id=1, source_target_pairs={{0,2},{1,3},{2,0},{3,1},{4,6},{5,7},{6,4},{7,5},{8,10},{9,11},{10,... | collective-permute-start | bytes 958472 | tf_op jit(solution)/shard_map/ppermute | solution.py:45
  22.0 7.7 %collective-permute-start.3 = (bf16[4,24,1536]{2,1,0:T(8,128)(2,1)S(1)}, bf16[4,24,1536]{2,1,0:T(8,128)(2,1)S(1)}, u32[]{:S(2)}, u32[]{:S(2)}) collective-permute-start(bf16[4,24,1536]{2,1,0:T(8,128)(2,1)S(1)} %pad_maximum_fusion.9), channel_id=1, source_target_pairs={{0,4},{1,5},{2,6},{3,7},{4,0},{5,1},{6,2},{7,3},{8,12},{9,13},{10,... | collective-permute-start | bytes 884744 | tf_op jit(solution)/shard_map/ppermute | solution.py:45
  29.9 14.6 %collective-permute-start.6 = (bf16[4,2,24,1664]{3,2,1,0:T(8,128)(2,1)S(1)}, bf16[4,2,24,1664]{3,2,1,0:T(8,128)(2,1)S(1)}, u32[]{:S(2)}, u32[]{:S(2)}) collective-permute-start(bf16[4,2,24,1664]{3,2,1,0:T(8,128)(2,1)S(1)} %pad_maximum_fusion.4), channel_id=1, source_target_pairs={{0,4},{1,5},{2,6},{3,7},{4,0},{5,1},{6,2},{7,3},{8,12},{9,13},{10,... | collective-permute-start | bytes 1916936 | tf_op jit(solution)/shard_map/ppermute | solution.py:45
  31.7 12.8 %collective-permute-start.5 = (bf16[4,2,24,1536]{3,2,0,1:T(8,128)(2,1)S(1)}, bf16[4,2,24,1536]{3,2,0,1:T(8,128)(2,1)S(1)}, u32[]{:S(2)}, u32[]{:S(2)}) collective-permute-start(bf16[4,2,24,1536]{3,2,0,1:T(8,128)(2,1)S(1)} %pad_maximum_fusion.5), channel_id=1, source_target_pairs={{0,2},{1,3},{2,0},{3,1},{4,6},{5,7},{6,4},{7,5},{8,10},{9,11},{10,... | collective-permute-start | bytes 1769480 | tf_op jit(solution)/shard_map/ppermute | solution.py:45
  45.8 5.3 %collective-permute-start.8 = (bf16[4,2,2,24,1664]{4,3,2,1,0:T(8,128)(2,1)}, bf16[4,2,2,24,1664]{4,3,2,1,0:T(8,128)(2,1)}, u32[]{:S(2)}, u32[]{:S(2)}) collective-permute-start(bf16[4,2,2,24,1664]{4,3,2,1,0:T(8,128)(2,1)} %pad_maximum_fusion.2), channel_id=1, source_target_pairs={{0,1},{1,0},{2,3},{3,2},{4,5},{5,4},{6,7},{7,6},{8,9},{9,8},{10,11... | collective-permute-start | bytes 3833864 | tf_op jit(solution)/shard_map/ppermute | solution.py:45
  48.4 51.6 %collective-permute-start.12 = (bf16[2,768,384]{2,1,0:T(8,128)(2,1)}, bf16[2,768,384]{2,1,0:T(8,128)(2,1)}, u32[]{:S(2)}, u32[]{:S(2)}) collective-permute-start(bf16[2,768,384]{2,1,0:T(8,128)(2,1)} %refs_4_.1), channel_id=1, source_target_pairs={{0,4},{1,5},{2,6},{3,7},{4,0},{5,1},{6,2},{7,3},{8,12},{9,13},{10,... | collective-permute-start | bytes 3538952 | tf_op jit(solution)/shard_map/ppermute | solution.py:45
  49.5 52.4 %collective-permute-start.13 = (bf16[2,384,768]{2,1,0:T(8,128)(2,1)}, bf16[2,384,768]{2,1,0:T(8,128)(2,1)}, u32[]{:S(2)}, u32[]{:S(2)}) collective-permute-start(bf16[2,384,768]{2,1,0:T(8,128)(2,1)} %refs_6_.1), channel_id=1, source_target_pairs={{0,4},{1,5},{2,6},{3,7},{4,0},{5,1},{6,2},{7,3},{8,12},{9,13},{10,... | collective-permute-start | bytes 3538952 | tf_op jit(solution)/shard_map/ppermute | solution.py:45
  94.0 7.9 %collective-permute-start.10 = (bf16[24,1536]{1,0:T(8,128)(2,1)S(1)}, bf16[24,1536]{1,0:T(8,128)(2,1)S(1)}, u32[]{:S(2)}, u32[]{:S(2)}) collective-permute-start(bf16[24,1536]{1,0:T(8,128)(2,1)S(1)} %get-tuple-element.282), channel_id=1, source_target_pairs={{0,2},{1,3},{2,0},{3,1},{4,6},{5,7},{6,4},{7,5},{8,10},{9,11},{10,... | collective-permute-start | bytes 221192 | tf_op jit(solution)/shard_map/ppermute | solution.py:45
  95.8 6.6 %collective-permute-start.11 = (bf16[24,1536]{1,0:T(8,128)(2,1)S(1)}, bf16[24,1536]{1,0:T(8,128)(2,1)S(1)}, u32[]{:S(2)}, u32[]{:S(2)}) collective-permute-start(bf16[24,1536]{1,0:T(8,128)(2,1)S(1)} %get-tuple-element.281), channel_id=1, source_target_pairs={{0,3},{1,0},{2,1},{3,2},{4,7},{5,4},{6,5},{7,6},{8,11},{9,8},{10,9... | collective-permute-start | bytes 221192 | tf_op jit(solution)/shard_map/ppermute | solution.py:45
  100.0 3.8 %collective-permute-start.9 = (bf16[24,1536]{1,0:T(8,128)(2,1)S(1)}, bf16[24,1536]{1,0:T(8,128)(2,1)S(1)}, u32[]{:S(2)}, u32[]{:S(2)}) collective-permute-start(bf16[24,1536]{1,0:T(8,128)(2,1)S(1)} %get-tuple-element.283), channel_id=1, source_target_pairs={{0,1},{1,2},{2,3},{3,0},{4,5},{5,6},{6,7},{7,4},{8,9},{9,10},{10,1... | collective-permute-start | bytes 221192 | tf_op jit(solution)/shard_map/ppermute | solution.py:45
  103.8 18.6 %collective-permute-start.14 = (bf16[96,1536]{1,0:T(8,128)(2,1)S(1)}, bf16[96,1536]{1,0:T(8,128)(2,1)S(1)}, u32[]{:S(2)}, u32[]{:S(2)}) collective-permute-start(bf16[96,1536]{1,0:T(8,128)(2,1)S(1)} %pad_maximum_fusion.10.refs_0_), channel_id=1, source_target_pairs={{0,8},{1,9},{2,10},{3,11},{4,12},{5,13},{6,14},{7,15},{8,16},{9,17... | collective-permute-start | bytes 884744 | tf_op jit(solution)/shard_map/ppermute | solution.py:45
  107.6 20.1 %collective-permute-start.15 = (bf16[96,1536]{1,0:T(8,128)(2,1)S(1)}, bf16[96,1536]{1,0:T(8,128)(2,1)S(1)}, u32[]{:S(2)}, u32[]{:S(2)}) collective-permute-start(bf16[96,1536]{1,0:T(8,128)(2,1)S(1)} %pad_maximum_fusion.10.refs_0_), channel_id=1, source_target_pairs={{0,16},{1,17},{2,18},{3,19},{4,20},{5,21},{6,22},{7,23},{8,24},{9,... | collective-permute-start | bytes 884744 | tf_op jit(solution)/shard_map/ppermute | solution.py:45
  107.7 20.0 %collective-permute-start.16 = (bf16[96,1536]{1,0:T(8,128)(2,1)S(1)}, bf16[96,1536]{1,0:T(8,128)(2,1)S(1)}, u32[]{:S(2)}, u32[]{:S(2)}) collective-permute-start(bf16[96,1536]{1,0:T(8,128)(2,1)S(1)} %pad_maximum_fusion.10.refs_0_), channel_id=1, source_target_pairs={{0,24},{1,25},{2,26},{3,27},{4,28},{5,29},{6,30},{7,31},{8,0},{9,1... | collective-permute-start | bytes 884744 | tf_op jit(solution)/shard_map/ppermute | solution.py:45
  137.3 18.2 %collective-permute-start.17 = (bf16[96,1536]{1,0:T(8,128)(2,1)S(1)}, bf16[96,1536]{1,0:T(8,128)(2,1)S(1)}, u32[]{:S(2)}, u32[]{:S(2)}) collective-permute-start(bf16[96,1536]{1,0:T(8,128)(2,1)S(1)} %get-tuple-element.145), channel_id=1, source_target_pairs={{0,24},{1,25},{2,26},{3,27},{4,28},{5,29},{6,30},{7,31},{8,0},{9,1... | collective-permute-start | bytes 884744 | tf_op jit(solution)/shard_map/ppermute | solution.py:45
  145.8 25.5 %collective-permute-start.18 = (bf16[96,1536]{1,0:T(8,128)(2,1)S(1)}, bf16[96,1536]{1,0:T(8,128)(2,1)S(1)}, u32[]{:S(2)}, u32[]{:S(2)}) collective-permute-start(bf16[96,1536]{1,0:T(8,128)(2,1)S(1)} %get-tuple-element.146), channel_id=1, source_target_pairs={{0,16},{1,17},{2,18},{3,19},{4,20},{5,21},{6,22},{7,23},{8,24},{9,... | collective-permute-start | bytes 884744 | tf_op jit(solution)/shard_map/ppermute | solution.py:45
  145.8 25.5 %collective-permute-start.19 = (bf16[96,1536]{1,0:T(8,128)(2,1)S(1)}, bf16[96,1536]{1,0:T(8,128)(2,1)S(1)}, u32[]{:S(2)}, u32[]{:S(2)}) collective-permute-start(bf16[96,1536]{1,0:T(8,128)(2,1)S(1)} %get-tuple-element.147), channel_id=1, source_target_pairs={{0,8},{1,9},{2,10},{3,11},{4,12},{5,13},{6,14},{7,15},{8,16},{9,17... | collective-permute-start | bytes 884744 | tf_op jit(solution)/shard_map/ppermute | solution.py:45
  171.6 5.1 %collective-permute-start.23 = (bf16[24,1536]{1,0:T(8,128)(2,1)S(1)}, bf16[24,1536]{1,0:T(8,128)(2,1)S(1)}, u32[]{:S(2)}, u32[]{:S(2)}) collective-permute-start(bf16[24,1536]{1,0:T(8,128)(2,1)S(1)} %get-tuple-element.278), channel_id=1, source_target_pairs={{0,2},{1,3},{2,0},{3,1},{4,6},{5,7},{6,4},{7,5},{8,10},{9,11},{10,... | collective-permute-start | bytes 221192 | tf_op jit(solution)/shard_map/ppermute | solution.py:45
  172.4 4.7 %collective-permute-start.24 = (bf16[24,1536]{1,0:T(8,128)(2,1)S(1)}, bf16[24,1536]{1,0:T(8,128)(2,1)S(1)}, u32[]{:S(2)}, u32[]{:S(2)}) collective-permute-start(bf16[24,1536]{1,0:T(8,128)(2,1)S(1)} %get-tuple-element.277), channel_id=1, source_target_pairs={{0,1},{1,2},{2,3},{3,0},{4,5},{5,6},{6,7},{7,4},{8,9},{9,10},{10,1... | collective-permute-start | bytes 221192 | tf_op jit(solution)/shard_map/ppermute | solution.py:45
  172.5 46.9 %collective-permute-start.21 = (bf16[1,384,768]{2,1,0:T(8,128)(2,1)S(1)}, bf16[1,384,768]{2,1,0:T(8,128)(2,1)S(1)}, u32[]{:S(2)}, u32[]{:S(2)}) collective-permute-start(bf16[1,384,768]{2,1,0:T(8,128)(2,1)S(1)} %get-tuple-element.261), channel_id=1, source_target_pairs={{0,4},{1,5},{2,6},{3,7},{4,0},{5,1},{6,2},{7,3},{8,12},{9,13},{10,... | collective-permute-start | bytes 1769480 | tf_op jit(solution)/shard_map/ppermute | solution.py:45
  174.7 44.8 %collective-permute-start.20 = (bf16[2,768,384]{2,1,0:T(8,128)(2,1)S(1)}, bf16[2,768,384]{2,1,0:T(8,128)(2,1)S(1)}, u32[]{:S(2)}, u32[]{:S(2)}) collective-permute-start(bf16[2,768,384]{2,1,0:T(8,128)(2,1)S(1)} %copy-done.24), channel_id=1, source_target_pairs={{0,4},{1,5},{2,6},{3,7},{4,0},{5,1},{6,2},{7,3},{8,12},{9,13},{10,... | collective-permute-start | bytes 3538952 | tf_op jit(solution)/shard_map/ppermute | solution.py:45
  219.5 22.8 %collective-permute-start.25 = (bf16[1,384,768]{2,1,0:T(8,128)(2,1)S(1)}, bf16[1,384,768]{2,1,0:T(8,128)(2,1)S(1)}, u32[]{:S(2)}, u32[]{:S(2)}) collective-permute-start(bf16[1,384,768]{2,1,0:T(8,128)(2,1)S(1)} %get-tuple-element.175), channel_id=1, source_target_pairs={{0,4},{1,5},{2,6},{3,7},{4,0},{5,1},{6,2},{7,3},{8,12},{9,13},{10,... | collective-permute-start | bytes 1769480 | tf_op jit(solution)/shard_map/ppermute | solution.py:45
  242.3 11.5 %collective-permute-start.26 = (bf16[4,2,2,24,3200]{4,3,2,1,0:T(8,128)(2,1)}, bf16[4,2,2,24,3200]{4,3,2,1,0:T(8,128)(2,1)}, u32[]{:S(2)}, u32[]{:S(2)}) collective-permute-start(bf16[4,2,2,24,3200]{4,3,2,1,0:T(8,128)(2,1)} %bitcast.113), channel_id=1, source_target_pairs={{0,1},{1,0},{2,3},{3,2},{4,5},{5,4},{6,7},{7,6},{8,9},{9,8},{10,11... | collective-permute-start | bytes 7372808 | tf_op jit(solution)/shard_map/ppermute | solution.py:45
  256.4 17.4 %collective-permute-start.27 = (bf16[4,2,24,1664]{3,2,1,0:T(8,128)(2,1)S(1)}, bf16[4,2,24,1664]{3,2,1,0:T(8,128)(2,1)}, u32[]{:S(2)}, u32[]{:S(2)}) collective-permute-start(bf16[4,2,24,1664]{3,2,1,0:T(8,128)(2,1)S(1)} %dynamic-slice_bitcast_fusion), channel_id=1, source_target_pairs={{0,2},{1,3},{2,0},{3,1},{4,6},{5,7},{6,4},{7,5},{8,10},{9,11},{10,... | collective-permute-start | bytes 1916936 | tf_op jit(solution)/shard_map/ppermute | solution.py:45
  258.1 15.6 %collective-permute-start.28 = (bf16[4,2,24,1536]{3,2,1,0:T(8,128)(2,1)}, bf16[4,2,24,1536]{3,2,1,0:T(8,128)(2,1)}, u32[]{:S(2)}, u32[]{:S(2)}) collective-permute-start(bf16[4,2,24,1536]{3,2,1,0:T(8,128)(2,1)} %dynamic-slice_bitcast_fusion.1), channel_id=1, source_target_pairs={{0,4},{1,5},{2,6},{3,7},{4,0},{5,1},{6,2},{7,3},{8,12},{9,13},{10,... | collective-permute-start | bytes 1769480 | tf_op jit(solution)/shard_map/ppermute | solution.py:45
  275.1 10.6 %collective-permute-start.30 = (bf16[4,24,1536]{2,1,0:T(8,128)(2,1)S(1)}, bf16[4,24,1536]{2,1,0:T(8,128)(2,1)S(1)}, u32[]{:S(2)}, u32[]{:S(2)}) collective-permute-start(bf16[4,24,1536]{2,1,0:T(8,128)(2,1)S(1)} %dynamic-slice_bitcast_fusion.3), channel_id=1, source_target_pairs={{0,2},{1,3},{2,0},{3,1},{4,6},{5,7},{6,4},{7,5},{8,10},{9,11},{10,... | collective-permute-start | bytes 884744 | tf_op jit(solution)/shard_map/ppermute | solution.py:45
  277.4 8.4 %collective-permute-start.29 = (bf16[4,24,1664]{2,1,0:T(8,128)(2,1)S(1)}, bf16[4,24,1664]{2,1,0:T(8,128)(2,1)S(1)}, u32[]{:S(2)}, u32[]{:S(2)}) collective-permute-start(bf16[4,24,1664]{2,1,0:T(8,128)(2,1)S(1)} %dynamic-slice_bitcast_fusion.2), channel_id=1, source_target_pairs={{0,4},{1,5},{2,6},{3,7},{4,0},{5,1},{6,2},{7,3},{8,12},{9,13},{10,... | collective-permute-start | bytes 958472 | tf_op jit(solution)/shard_map/ppermute | solution.py:45
  286.0 14.4 %collective-permute-start.31 = (bf16[24,3200]{1,0:T(8,128)(2,1)S(1)}, bf16[24,3200]{1,0:T(8,128)(2,1)S(1)}, u32[]{:S(2)}, u32[]{:S(2)}) collective-permute-start(bf16[24,3200]{1,0:T(8,128)(2,1)S(1)} %get-tuple-element.268), channel_id=1, source_target_pairs={{0,8},{1,9},{2,10},{3,11},{4,12},{5,13},{6,14},{7,15},{8,16},{9,17... | collective-permute-start | bytes 460808 | tf_op jit(solution)/shard_map/ppermute | solution.py:45
  286.1 14.4 %collective-permute-start.32 = (bf16[24,3200]{1,0:T(8,128)(2,1)S(1)}, bf16[24,3200]{1,0:T(8,128)(2,1)S(1)}, u32[]{:S(2)}, u32[]{:S(2)}) collective-permute-start(bf16[24,3200]{1,0:T(8,128)(2,1)S(1)} %get-tuple-element.269), channel_id=1, source_target_pairs={{0,16},{1,17},{2,18},{3,19},{4,20},{5,21},{6,22},{7,23},{8,24},{9,... | collective-permute-start | bytes 460808 | tf_op jit(solution)/shard_map/ppermute | solution.py:45
  288.2 12.2 %collective-permute-start.33 = (bf16[24,3200]{1,0:T(8,128)(2,1)S(1)}, bf16[24,3200]{1,0:T(8,128)(2,1)S(1)}, u32[]{:S(2)}, u32[]{:S(2)}) collective-permute-start(bf16[24,3200]{1,0:T(8,128)(2,1)S(1)} %get-tuple-element.267), channel_id=1, source_target_pairs={{0,24},{1,25},{2,26},{3,27},{4,28},{5,29},{6,30},{7,31},{8,0},{9,1... | collective-permute-start | bytes 460808 | tf_op jit(solution)/shard_map/ppermute | solution.py:45
  (27 other events, 123.4 us)

commit v3 on v2

--- a/solution.py
+++ b/solution.py
@@ -12,9 +12,9 @@
 BOTH = ("dp", "expert")
 F32, BF16 = jnp.float32, jnp.bfloat16
 LOW = -1e30
-LIMIT = 52
+LIMIT = 51
 SHARES = (2, 8, 2)
-SMALL = 52
+SMALL = 51
 GATHER_CUT = 1664
 
 

time: 306 us -> 307 us (level)
  starting transfers between devices: 52.5 us -> 68.3 us
  Pallas kernels: 150 us -> 143 us
  local copies, waits for them, and re-layouts: 40.6 us -> 35.2 us
    ppermute x34, starting transfers between devices: 52.5 us -> 68.3 us  [send(): return lax.ppermute(a, BOTH, self.perm(axis, k))]
    unnamed x57 -> x49, local copies, waits for them, and re-layouts: 22.6 us -> 18.6 us
    pallas_call x1, Pallas kernels: 36 us -> 32.1 us  [forward(): by_image(partial(forward_kernel, self.tokens, self.slots, self.place), n,...]
  transfers between devices with their start and end apart: 34 -> 34, of which waited for: 12 -> 12; matrix products, arithmetic and copies ran while one was open for 13% -> 12% of each run, Pallas kernels for 46% -> 44%
where the time goes in v3:
time: 307 us
  Pallas kernels  143 us (47%)
  starting transfers between devices  68.3 us (22%)
  waiting for transfers between devices  41.1 us (13%)
  local copies, waits for them, and re-layouts  35.2 us (11%)
  other arithmetic  17.2 us (6%)
    ppermute x34, starting transfers between devices, send(): return lax.ppermute(a, BOTH, self.perm(axis, k))  68.3 us
    ppermute x34, waiting for transfers between devices, send(): return lax.ppermute(a, BOTH, self.perm(axis, k))  41.1 us
    pallas_call x1, Pallas kernels, backward(): by_image(partial(backward_kernel, self.tokens, self.slots, self.place), n...  39.6 us
    pallas_call x1, Pallas kernels, forward(): by_image(partial(forward_kernel, self.tokens, self.slots, self.place), n,...  32.1 us
    pallas_call x3, Pallas kernels, input_back(): pl.pallas_call(partial(input_kernel, self.tokens), grid=((high - low) //...  24.3 us
    pallas_call x1, Pallas kernels, weight_grads(): pl.pallas_call(partial(weight_grad_kernel, self.slots, devices), grid_spe...  21.2 us
    unnamed x49, local copies, waits for them, and re-layouts  18.6 us
    reshape x2, local copies, waits for them, and re-layouts, turned(): return array.reshape(-1, array.shape[-1]).T  12.3 us
  transfers between devices with their start and end apart: 34, of which 12 were waited for; matrix products, arithmetic and copies ran while one was open for 12% of the time, Pallas kernels for 44%

profile of v3, /device:TPU:0, one launch (start us, length us, event | category | flops | bytes accessed | tf_op | source)
XLA Modules:
  0.0 306.6 jit_solution(1540500343808456840)
XLA Ops:
  3.4 3.1 %collective-permute-start = (bf16[24,3200]{1,0:T(8,128)(2,1)S(1)}, bf16[24,3200]{1,0:T(8,128)(2,1)S(1)}, u32[]{:S(2)}, u32[]{:S(2)}) collective-permute-start(bf16[24,3200]{1,0:T(8,128)(2,1)S(1)} %pad_maximum_fusion.11), channel_id=1, source_target_pairs={{0,8},{1,9},{2,10},{3,11},{4,12},{5,13},{6,14},{7,15},{8,16},{9,17... | collective-permute-start | bytes 460808 | tf_op jit(solution)/shard_map/ppermute | solution.py:45
  6.5 2.6 collective-permute-start.1
  11.2 4.3 %copy.86.cot_ref = bf16[4,3,197,768]{3,2,1,0:T(8,128)(2,1)} copy(bf16[4,3,197,768]{3,0,2,1:T(4,128)(2,1)} %param.23) | data formatting | bytes 7262208 | tf_op args[11]
  15.5 4.5 %shard_map.203.cot_ref = bf16[12,208,768]{2,1,0:T(8,128)(2,1)} custom-call(bf16[4,3,197,768]{3,2,1,0:T(8,128)(2,1)} %copy.86.cot_ref), custom_call_target="tpu_custom_call" | custom-call | tf_op jit(solution)/shard_map/pallas_call | solution.py:508
  23.6 6.1 %collective-permute-done.3 = bf16[4,24,1536]{2,1,0:T(8,128)(2,1)S(1)} collective-permute-done((bf16[4,24,1536]{2,1,0:T(8,128)(2,1)S(1)}, bf16[4,24,1536]{2,1,0:T(8,128)(2,1)S(1)}, u32[]{:S(2)}, u32[]{:S(2)}) %collective-permute-start.3) | collective-permute-done | bytes 294944 | tf_op jit(solution)/shard_map/ppermute | solution.py:45
  32.4 2.3 copy.93.x_ref
  34.7 5.6 %shard_map.204 = (bf16[12,208,768]{2,1,0:T(8,128)(2,1)}, f32[12,208,128]{2,1,0:T(8,128)S(1)}) custom-call(bf16[4,3,197,768]{3,2,1,0:T(8,128)(2,1)} %copy.93.x_ref), custom_call_target="tpu_custom_call" | custom-call | tf_op jit(solution)/shard_map/pallas_call | solution.py:520
  40.3 4.2 %collective-permute-done.5 = bf16[4,2,24,1536]{3,2,0,1:T(8,128)(2,1)S(1)} collective-permute-done((bf16[4,2,24,1536]{3,2,0,1:T(8,128)(2,1)S(1)}, bf16[4,2,24,1536]{3,2,0,1:T(8,128)(2,1)S(1)}, u32[]{:S(2)}, u32[]{:S(2)}) %collective-permute-start.5) | collective-permute-done | bytes 589856 | tf_op jit(solution)/shard_map/ppermute | solution.py:45
  56.3 32.1 %shard_map.205 = (bf16[12,208,2304]{2,1,0:T(8,128)(2,1)}, bf16[12,208,768]{2,1,0:T(8,128)(2,1)}, f32[12,208,768]{2,1,0:T(8,128)}, f32[12,208,512]{2,1,0:T(8,128)}, f32[96,1536]{1,0:T(8,128)S(1)}) custom-call(s32[13]{0:T(128)S(1)} %pad_add_fusion.live, bf16[4,3,197,768]{3,2,1,0:T(8,128)(2,1)} %copy.93.x_ref, bf16[12,208,768]{2,1,0:T(8,128)(2,1)} %get-tuple-element.118.n1_ref, ...), custom_call_target="tpu_custom_call" | custom-call | flops 35332816896 | bytes 35332816 | tf_op jit(solution)/shard_map/pallas_call | solution.py:532
  88.5 6.1 %collective-permute-start.10 = (bf16[24,1536]{1,0:T(8,128)(2,1)S(1)}, bf16[24,1536]{1,0:T(8,128)(2,1)S(1)}, u32[]{:S(2)}, u32[]{:S(2)}) collective-permute-start(bf16[24,1536]{1,0:T(8,128)(2,1)S(1)} %get-tuple-element.282), channel_id=1, source_target_pairs={{0,2},{1,3},{2,0},{3,1},{4,6},{5,7},{6,4},{7,5},{8,10},{9,11},{10,... | collective-permute-start | bytes 221192 | tf_op jit(solution)/shard_map/ppermute | solution.py:45
  94.5 4.3 %collective-permute-start.11 = (bf16[24,1536]{1,0:T(8,128)(2,1)S(1)}, bf16[24,1536]{1,0:T(8,128)(2,1)S(1)}, u32[]{:S(2)}, u32[]{:S(2)}) collective-permute-start(bf16[24,1536]{1,0:T(8,128)(2,1)S(1)} %get-tuple-element.281), channel_id=1, source_target_pairs={{0,3},{1,0},{2,1},{3,2},{4,7},{5,4},{6,5},{7,6},{8,11},{9,8},{10,9... | collective-permute-start | bytes 221192 | tf_op jit(solution)/shard_map/ppermute | solution.py:45
  102.7 3.4 %collective-permute-start.14 = (bf16[96,1536]{1,0:T(8,128)(2,1)S(1)}, bf16[96,1536]{1,0:T(8,128)(2,1)S(1)}, u32[]{:S(2)}, u32[]{:S(2)}) collective-permute-start(bf16[96,1536]{1,0:T(8,128)(2,1)S(1)} %pad_maximum_fusion.10.refs_0_), channel_id=1, source_target_pairs={{0,8},{1,9},{2,10},{3,11},{4,12},{5,13},{6,14},{7,15},{8,16},{9,17... | collective-permute-start | bytes 884744 | tf_op jit(solution)/shard_map/ppermute | solution.py:45
  106.1 2.4 collective-permute-start.16
  108.5 6.2 %copy.94 = bf16[2496,768]{0,1:T(8,128)(2,1)} copy(bf16[2496,768]{1,0:T(8,128)(2,1)} %bitcast.104) | data formatting | bytes 7667712 | tf_op jit(solution)/shard_map/reshape | solution.py:566
  114.7 6.1 %copy.95 = bf16[2496,768]{0,1:T(8,128)(2,1)} copy(bf16[2496,768]{1,0:T(8,128)(2,1)} %bitcast.108) | data formatting | bytes 7667712 | tf_op jit(solution)/shard_map/reshape | solution.py:566
  120.8 4.3 %collective-permute-done.15.refs_2_ = bf16[96,1536]{1,0:T(8,128)(2,1)S(1)} collective-permute-done((bf16[96,1536]{1,0:T(8,128)(2,1)S(1)}, bf16[96,1536]{1,0:T(8,128)(2,1)S(1)}, u32[]{:S(2)}, u32[]{:S(2)}) %collective-permute-start.15) | collective-permute-done | bytes 294944 | tf_op jit(solution)/shard_map/ppermute | solution.py:45
  125.1 8.7 %shard_map.206 = (bf16[96,1536]{1,0:T(8,128)(2,1)S(1)}, bf16[96,1536]{1,0:T(8,128)(2,1)S(1)}, bf16[96,1536]{1,0:T(8,128)(2,1)S(1)}, bf16[96,1536]{1,0:T(8,128)(2...) custom-call(bf16[96,1536]{1,0:T(8,128)(2,1)S(1)} %pad_maximum_fusion.10.refs_0_, ...), custom_call_target="tpu_custom_call" | custom-call | tf_op jit(solution)/shard_map/pallas_call | solution.py:596
  133.8 8.6 %collective-permute-start.17 = (bf16[96,1536]{1,0:T(8,128)(2,1)S(1)}, bf16[96,1536]{1,0:T(8,128)(2,1)S(1)}, u32[]{:S(2)}, u32[]{:S(2)}) collective-permute-start(bf16[96,1536]{1,0:T(8,128)(2,1)S(1)} %get-tuple-element.145), channel_id=1, source_target_pairs={{0,24},{1,25},{2,26},{3,27},{4,28},{5,29},{6,30},{7,31},{8,0},{9,1... | collective-permute-start | bytes 884744 | tf_op jit(solution)/shard_map/ppermute | solution.py:45
  142.9 6.8 %shard_map.207 = (f32[2,768,384]{2,1,0:T(8,128)}, f32[2,384,768]{2,1,0:T(8,128)}, bf16[2,768,384]{2,1,0:T(8,128)(2,1)S(1)}, bf16[2,384,768]{2,1,0:T(8,128)(2,1)}) custom-call(bf16[96,1536]{1,0:T(8,128)(2,1)S(1)} %pad_maximum_fusion.10.refs_0_, bf16[96,1536]{1,0:T(8,128)(2,1)S(1)} %collective-permute-done.14.refs_1_, ...), custom_call_target="tpu_custom_call" | custom-call | tf_op jit(solution)/shard_map/pallas_call | solution.py:605
  149.9 18.0 %collective-permute-done.18 = bf16[96,1536]{1,0:T(8,128)(2,1)S(1)} collective-permute-done((bf16[96,1536]{1,0:T(8,128)(2,1)S(1)}, bf16[96,1536]{1,0:T(8,128)(2,1)S(1)}, u32[]{:S(2)}, u32[]{:S(2)}) %collective-permute-start.18) | collective-permute-done | bytes 294944 | tf_op jit(solution)/shard_map/ppermute | solution.py:45
  170.6 3.2 %collective-permute-start.21 = (bf16[1,384,768]{2,1,0:T(8,128)(2,1)S(1)}, bf16[1,384,768]{2,1,0:T(8,128)(2,1)S(1)}, u32[]{:S(2)}, u32[]{:S(2)}) collective-permute-start(bf16[1,384,768]{2,1,0:T(8,128)(2,1)S(1)} %get-tuple-element.261), channel_id=1, source_target_pairs={{0,4},{1,5},{2,6},{3,7},{4,0},{5,1},{6,2},{7,3},{8,12},{9,13},{10,... | collective-permute-start | bytes 1769480 | tf_op jit(solution)/shard_map/ppermute | solution.py:45
  174.8 39.6 %shard_map.208 = (bf16[12,197,768]{2,1,0:T(8,128)(2,1)}, bf16[12,208,768]{2,1,0:T(8,128)(2,1)}, bf16[12,208,2304]{2,1,0:T(8,128)(2,1)}, f32[8,2304]{1,0:T(8,128)S(1)}, f32[16,768]{1,0:T(8,128)S(1)}) custom-call(s32[13]{0:T(128)S(1)} %pad_add_fusion.live, bf16[12,208,768]{2,1,0:T(8,128)(2,1)} %shard_map.203.cot_ref, ...), custom_call_target="tpu_custom_call" | custom-call | flops 35332816896 | bytes 35332816 | tf_op jit(solution)/shard_map/pallas_call | solution.py:543
  216.0 21.2 %shard_map.209 = (bf16[384,3200]{1,0:T(8,128)(2,1)}, bf16[384,3200]{1,0:T(8,128)(2,1)}) custom-call(s32[1]{0:T(128)} %bitcast.32.core, bf16[768,2496]{1,0:T(8,128)(2,1)} %bitcast.106, bf16[768,2496]{1,0:T(8,128)(2,1)} %bitcast.107, bf16[12,208,2304]{2,1,0:T(8,128)(2,1)} %get-tuple-element.178.right_ref.triple_ref, ...), custom_call_target="tpu_custom_call" | custom-call | tf_op jit(solution)/shard_map/pallas_call | solution.py:577
  237.2 10.2 %collective-permute-start.26 = (bf16[4,2,2,24,3200]{4,3,2,1,0:T(8,128)(2,1)}, bf16[4,2,2,24,3200]{4,3,2,1,0:T(8,128)(2,1)}, u32[]{:S(2)}, u32[]{:S(2)}) collective-permute-start(bf16[4,2,2,24,3200]{4,3,2,1,0:T(8,128)(2,1)} %bitcast.113), channel_id=1, source_target_pairs={{0,1},{1,0},{2,3},{3,2},{4,5},{5,4},{6,7},{7,6},{8,9},{9,8},{10,11... | collective-permute-start | bytes 7372808 | tf_op jit(solution)/shard_map/ppermute | solution.py:45
  247.5 6.0 %shard_map.210.refs_0_ = bf16[12,197,768]{2,1,0:T(8,128)(2,1)} custom-call(bf16[12,208,2304]{2,1,0:T(8,128)(2,1)} %get-tuple-element.178.right_ref.triple_ref, bf16[12,208,768]{2,1,0:T(8,128)(2,1)} %get-tuple-element.118.n1_ref, f32[12,208,128]{2,1,0:T(8,128)S(1)} %copy-done.2, bf16[12,208,768]{2,1,0:T(8,128)(2,1)} %get-tuple-element.179.right_out_ref.branch_ref, ...), custom_call_target="tpu_custom_call" | custom-call | tf_op jit(solution)/shard_map/pallas_call | solution.py:554
  258.5 12.4 %shard_map.211.refs_0_ = bf16[12,197,768]{2,1,0:T(8,128)(2,1)} custom-call(bf16[12,208,2304]{2,1,0:T(8,128)(2,1)} %get-tuple-element.178.right_ref.triple_ref, bf16[12,208,768]{2,1,0:T(8,128)(2,1)} %get-tuple-element.118.n1_ref, f32[12,208,128]{2,1,0:T(8,128)S(1)} %copy-done.2, ...), custom_call_target="tpu_custom_call", output_to_operand_aliasing={{}: (7, {})} | custom-call | tf_op jit(solution)/shard_map/pallas_call | solution.py:554
  270.9 2.4 collective-permute-done.28
  279.5 5.9 %shard_map.212 = bf16[12,197,768]{2,1,0:T(8,128)(2,1)} custom-call(bf16[12,208,2304]{2,1,0:T(8,128)(2,1)} %get-tuple-element.178.right_ref.triple_ref, bf16[12,208,768]{2,1,0:T(8,128)(2,1)} %get-tuple-element.118.n1_ref, f32[12,208,128]{2,1,0:T(8,128)S(1)} %copy-done.2, ...), custom_call_target="tpu_custom_call", output_to_operand_aliasing={{}: (7, {})} | custom-call | tf_op jit(solution)/shard_map/pallas_call | solution.py:554
  285.7 6.3 %collective-permute-start.31 = (bf16[24,3200]{1,0:T(8,128)(2,1)S(1)}, bf16[24,3200]{1,0:T(8,128)(2,1)S(1)}, u32[]{:S(2)}, u32[]{:S(2)}) collective-permute-start(bf16[24,3200]{1,0:T(8,128)(2,1)S(1)} %get-tuple-element.268), channel_id=1, source_target_pairs={{0,8},{1,9},{2,10},{3,11},{4,12},{5,13},{6,14},{7,15},{8,16},{9,17... | collective-permute-start | bytes 460808 | tf_op jit(solution)/shard_map/ppermute | solution.py:45
  292.0 2.4 collective-permute-start.33
  297.4 3.2 %copy.98 = bf16[4,3,197,768]{3,0,2,1:T(4,128)(2,1)} copy(bf16[4,3,197,768]{3,2,1,0:T(8,128)(2,1)S(1)} %bitcast.109) | data formatting | bytes 7262208
  300.6 3.2 %copy.99 = bf16[4,3,197,768]{3,0,2,1:T(4,128)(2,1)} copy(bf16[4,3,197,768]{3,2,1,0:T(8,128)(2,1)S(1)} %bitcast.105) | data formatting | bytes 7262208
  (155 shorter events, 49.7 us)
Async XLA Ops:
  3.4 16.7 %collective-permute-start = (bf16[24,3200]{1,0:T(8,128)(2,1)S(1)}, bf16[24,3200]{1,0:T(8,128)(2,1)S(1)}, u32[]{:S(2)}, u32[]{:S(2)}) collective-permute-start(bf16[24,3200]{1,0:T(8,128)(2,1)S(1)} %pad_maximum_fusion.11), channel_id=1, source_target_pairs={{0,8},{1,9},{2,10},{3,11},{4,12},{5,13},{6,14},{7,15},{8,16},{9,17... | collective-permute-start | bytes 460808 | tf_op jit(solution)/shard_map/ppermute | solution.py:45
  6.5 13.6 %collective-permute-start.1 = (bf16[24,3200]{1,0:T(8,128)(2,1)S(1)}, bf16[24,3200]{1,0:T(8,128)(2,1)S(1)}, u32[]{:S(2)}, u32[]{:S(2)}) collective-permute-start(bf16[24,3200]{1,0:T(8,128)(2,1)S(1)} %pad_maximum_fusion.11), channel_id=1, source_target_pairs={{0,16},{1,17},{2,18},{3,19},{4,20},{5,21},{6,22},{7,23},{8,24},{9,... | collective-permute-start | bytes 460808 | tf_op jit(solution)/shard_map/ppermute | solution.py:45
  9.1 11.0 %collective-permute-start.2 = (bf16[24,3200]{1,0:T(8,128)(2,1)S(1)}, bf16[24,3200]{1,0:T(8,128)(2,1)S(1)}, u32[]{:S(2)}, u32[]{:S(2)}) collective-permute-start(bf16[24,3200]{1,0:T(8,128)(2,1)S(1)} %pad_maximum_fusion.11), channel_id=1, source_target_pairs={{0,24},{1,25},{2,26},{3,27},{4,28},{5,29},{6,30},{7,31},{8,0},{9,1... | collective-permute-start | bytes 460808 | tf_op jit(solution)/shard_map/ppermute | solution.py:45
  20.4 9.3 %collective-permute-start.4 = (bf16[4,24,1664]{2,1,0:T(8,128)(2,1)S(1)}, bf16[4,24,1664]{2,1,0:T(8,128)(2,1)S(1)}, u32[]{:S(2)}, u32[]{:S(2)}) collective-permute-start(bf16[4,24,1664]{2,1,0:T(8,128)(2,1)S(1)} %pad_maximum_fusion.6), channel_id=1, source_target_pairs={{0,2},{1,3},{2,0},{3,1},{4,6},{5,7},{6,4},{7,5},{8,10},{9,11},{10,... | collective-permute-start | bytes 958472 | tf_op jit(solution)/shard_map/ppermute | solution.py:45
  22.0 7.7 %collective-permute-start.3 = (bf16[4,24,1536]{2,1,0:T(8,128)(2,1)S(1)}, bf16[4,24,1536]{2,1,0:T(8,128)(2,1)S(1)}, u32[]{:S(2)}, u32[]{:S(2)}) collective-permute-start(bf16[4,24,1536]{2,1,0:T(8,128)(2,1)S(1)} %pad_maximum_fusion.9), channel_id=1, source_target_pairs={{0,4},{1,5},{2,6},{3,7},{4,0},{5,1},{6,2},{7,3},{8,12},{9,13},{10,... | collective-permute-start | bytes 884744 | tf_op jit(solution)/shard_map/ppermute | solution.py:45
  29.9 14.6 %collective-permute-start.6 = (bf16[4,2,24,1664]{3,2,1,0:T(8,128)(2,1)S(1)}, bf16[4,2,24,1664]{3,2,1,0:T(8,128)(2,1)S(1)}, u32[]{:S(2)}, u32[]{:S(2)}) collective-permute-start(bf16[4,2,24,1664]{3,2,1,0:T(8,128)(2,1)S(1)} %pad_maximum_fusion.4), channel_id=1, source_target_pairs={{0,4},{1,5},{2,6},{3,7},{4,0},{5,1},{6,2},{7,3},{8,12},{9,13},{10,... | collective-permute-start | bytes 1916936 | tf_op jit(solution)/shard_map/ppermute | solution.py:45
  31.7 12.8 %collective-permute-start.5 = (bf16[4,2,24,1536]{3,2,0,1:T(8,128)(2,1)S(1)}, bf16[4,2,24,1536]{3,2,0,1:T(8,128)(2,1)S(1)}, u32[]{:S(2)}, u32[]{:S(2)}) collective-permute-start(bf16[4,2,24,1536]{3,2,0,1:T(8,128)(2,1)S(1)} %pad_maximum_fusion.5), channel_id=1, source_target_pairs={{0,2},{1,3},{2,0},{3,1},{4,6},{5,7},{6,4},{7,5},{8,10},{9,11},{10,... | collective-permute-start | bytes 1769480 | tf_op jit(solution)/shard_map/ppermute | solution.py:45
  45.8 5.0 %collective-permute-start.8 = (bf16[4,2,2,24,1664]{4,3,2,1,0:T(8,128)(2,1)}, bf16[4,2,2,24,1664]{4,3,2,1,0:T(8,128)(2,1)}, u32[]{:S(2)}, u32[]{:S(2)}) collective-permute-start(bf16[4,2,2,24,1664]{4,3,2,1,0:T(8,128)(2,1)} %pad_maximum_fusion.2), channel_id=1, source_target_pairs={{0,1},{1,0},{2,3},{3,2},{4,5},{5,4},{6,7},{7,6},{8,9},{9,8},{10,11... | collective-permute-start | bytes 3833864 | tf_op jit(solution)/shard_map/ppermute | solution.py:45
  47.6 51.3 %collective-permute-start.12 = (bf16[2,768,384]{2,1,0:T(8,128)(2,1)}, bf16[2,768,384]{2,1,0:T(8,128)(2,1)}, u32[]{:S(2)}, u32[]{:S(2)}) collective-permute-start(bf16[2,768,384]{2,1,0:T(8,128)(2,1)} %refs_4_.1), channel_id=1, source_target_pairs={{0,4},{1,5},{2,6},{3,7},{4,0},{5,1},{6,2},{7,3},{8,12},{9,13},{10,... | collective-permute-start | bytes 3538952 | tf_op jit(solution)/shard_map/ppermute | solution.py:45
  48.7 52.4 %collective-permute-start.13 = (bf16[2,384,768]{2,1,0:T(8,128)(2,1)}, bf16[2,384,768]{2,1,0:T(8,128)(2,1)}, u32[]{:S(2)}, u32[]{:S(2)}) collective-permute-start(bf16[2,384,768]{2,1,0:T(8,128)(2,1)} %refs_6_.1), channel_id=1, source_target_pairs={{0,4},{1,5},{2,6},{3,7},{4,0},{5,1},{6,2},{7,3},{8,12},{9,13},{10,... | collective-permute-start | bytes 3538952 | tf_op jit(solution)/shard_map/ppermute | solution.py:45
  88.5 12.6 %collective-permute-start.10 = (bf16[24,1536]{1,0:T(8,128)(2,1)S(1)}, bf16[24,1536]{1,0:T(8,128)(2,1)S(1)}, u32[]{:S(2)}, u32[]{:S(2)}) collective-permute-start(bf16[24,1536]{1,0:T(8,128)(2,1)S(1)} %get-tuple-element.282), channel_id=1, source_target_pairs={{0,2},{1,3},{2,0},{3,1},{4,6},{5,7},{6,4},{7,5},{8,10},{9,11},{10,... | collective-permute-start | bytes 221192 | tf_op jit(solution)/shard_map/ppermute | solution.py:45
  94.5 6.8 %collective-permute-start.11 = (bf16[24,1536]{1,0:T(8,128)(2,1)S(1)}, bf16[24,1536]{1,0:T(8,128)(2,1)S(1)}, u32[]{:S(2)}, u32[]{:S(2)}) collective-permute-start(bf16[24,1536]{1,0:T(8,128)(2,1)S(1)} %get-tuple-element.281), channel_id=1, source_target_pairs={{0,3},{1,0},{2,1},{3,2},{4,7},{5,4},{6,5},{7,6},{8,11},{9,8},{10,9... | collective-permute-start | bytes 221192 | tf_op jit(solution)/shard_map/ppermute | solution.py:45
  102.7 18.1 %collective-permute-start.14 = (bf16[96,1536]{1,0:T(8,128)(2,1)S(1)}, bf16[96,1536]{1,0:T(8,128)(2,1)S(1)}, u32[]{:S(2)}, u32[]{:S(2)}) collective-permute-start(bf16[96,1536]{1,0:T(8,128)(2,1)S(1)} %pad_maximum_fusion.10.refs_0_), channel_id=1, source_target_pairs={{0,8},{1,9},{2,10},{3,11},{4,12},{5,13},{6,14},{7,15},{8,16},{9,17... | collective-permute-start | bytes 884744 | tf_op jit(solution)/shard_map/ppermute | solution.py:45
  106.1 19.0 %collective-permute-start.15 = (bf16[96,1536]{1,0:T(8,128)(2,1)S(1)}, bf16[96,1536]{1,0:T(8,128)(2,1)S(1)}, u32[]{:S(2)}, u32[]{:S(2)}) collective-permute-start(bf16[96,1536]{1,0:T(8,128)(2,1)S(1)} %pad_maximum_fusion.10.refs_0_), channel_id=1, source_target_pairs={{0,16},{1,17},{2,18},{3,19},{4,20},{5,21},{6,22},{7,23},{8,24},{9,... | collective-permute-start | bytes 884744 | tf_op jit(solution)/shard_map/ppermute | solution.py:45
  106.1 19.0 %collective-permute-start.16 = (bf16[96,1536]{1,0:T(8,128)(2,1)S(1)}, bf16[96,1536]{1,0:T(8,128)(2,1)S(1)}, u32[]{:S(2)}, u32[]{:S(2)}) collective-permute-start(bf16[96,1536]{1,0:T(8,128)(2,1)S(1)} %pad_maximum_fusion.10.refs_0_), channel_id=1, source_target_pairs={{0,24},{1,25},{2,26},{3,27},{4,28},{5,29},{6,30},{7,31},{8,0},{9,1... | collective-permute-start | bytes 884744 | tf_op jit(solution)/shard_map/ppermute | solution.py:45
  133.8 16.1 %collective-permute-start.17 = (bf16[96,1536]{1,0:T(8,128)(2,1)S(1)}, bf16[96,1536]{1,0:T(8,128)(2,1)S(1)}, u32[]{:S(2)}, u32[]{:S(2)}) collective-permute-start(bf16[96,1536]{1,0:T(8,128)(2,1)S(1)} %get-tuple-element.145), channel_id=1, source_target_pairs={{0,24},{1,25},{2,26},{3,27},{4,28},{5,29},{6,30},{7,31},{8,0},{9,1... | collective-permute-start | bytes 884744 | tf_op jit(solution)/shard_map/ppermute | solution.py:45
  142.4 25.5 %collective-permute-start.18 = (bf16[96,1536]{1,0:T(8,128)(2,1)S(1)}, bf16[96,1536]{1,0:T(8,128)(2,1)S(1)}, u32[]{:S(2)}, u32[]{:S(2)}) collective-permute-start(bf16[96,1536]{1,0:T(8,128)(2,1)S(1)} %get-tuple-element.146), channel_id=1, source_target_pairs={{0,16},{1,17},{2,18},{3,19},{4,20},{5,21},{6,22},{7,23},{8,24},{9,... | collective-permute-start | bytes 884744 | tf_op jit(solution)/shard_map/ppermute | solution.py:45
  142.4 25.5 %collective-permute-start.19 = (bf16[96,1536]{1,0:T(8,128)(2,1)S(1)}, bf16[96,1536]{1,0:T(8,128)(2,1)S(1)}, u32[]{:S(2)}, u32[]{:S(2)}) collective-permute-start(bf16[96,1536]{1,0:T(8,128)(2,1)S(1)} %get-tuple-element.147), channel_id=1, source_target_pairs={{0,8},{1,9},{2,10},{3,11},{4,12},{5,13},{6,14},{7,15},{8,16},{9,17... | collective-permute-start | bytes 884744 | tf_op jit(solution)/shard_map/ppermute | solution.py:45
  168.1 5.8 %collective-permute-start.22 = (bf16[24,1536]{1,0:T(8,128)(2,1)S(1)}, bf16[24,1536]{1,0:T(8,128)(2,1)S(1)}, u32[]{:S(2)}, u32[]{:S(2)}) collective-permute-start(bf16[24,1536]{1,0:T(8,128)(2,1)S(1)} %get-tuple-element.279), channel_id=1, source_target_pairs={{0,3},{1,0},{2,1},{3,2},{4,7},{5,4},{6,5},{7,6},{8,11},{9,8},{10,9... | collective-permute-start | bytes 221192 | tf_op jit(solution)/shard_map/ppermute | solution.py:45
  169.0 5.5 %collective-permute-start.23 = (bf16[24,1536]{1,0:T(8,128)(2,1)S(1)}, bf16[24,1536]{1,0:T(8,128)(2,1)S(1)}, u32[]{:S(2)}, u32[]{:S(2)}) collective-permute-start(bf16[24,1536]{1,0:T(8,128)(2,1)S(1)} %get-tuple-element.278), channel_id=1, source_target_pairs={{0,2},{1,3},{2,0},{3,1},{4,6},{5,7},{6,4},{7,5},{8,10},{9,11},{10,... | collective-permute-start | bytes 221192 | tf_op jit(solution)/shard_map/ppermute | solution.py:45
  170.3 4.4 %collective-permute-start.24 = (bf16[24,1536]{1,0:T(8,128)(2,1)S(1)}, bf16[24,1536]{1,0:T(8,128)(2,1)S(1)}, u32[]{:S(2)}, u32[]{:S(2)}) collective-permute-start(bf16[24,1536]{1,0:T(8,128)(2,1)S(1)} %get-tuple-element.277), channel_id=1, source_target_pairs={{0,1},{1,2},{2,3},{3,0},{4,5},{5,6},{6,7},{7,4},{8,9},{9,10},{10,1... | collective-permute-start | bytes 221192 | tf_op jit(solution)/shard_map/ppermute | solution.py:45
  170.6 43.9 %collective-permute-start.21 = (bf16[1,384,768]{2,1,0:T(8,128)(2,1)S(1)}, bf16[1,384,768]{2,1,0:T(8,128)(2,1)S(1)}, u32[]{:S(2)}, u32[]{:S(2)}) collective-permute-start(bf16[1,384,768]{2,1,0:T(8,128)(2,1)S(1)} %get-tuple-element.261), channel_id=1, source_target_pairs={{0,4},{1,5},{2,6},{3,7},{4,0},{5,1},{6,2},{7,3},{8,12},{9,13},{10,... | collective-permute-start | bytes 1769480 | tf_op jit(solution)/shard_map/ppermute | solution.py:45
  173.8 40.7 %collective-permute-start.20 = (bf16[2,768,384]{2,1,0:T(8,128)(2,1)S(1)}, bf16[2,768,384]{2,1,0:T(8,128)(2,1)S(1)}, u32[]{:S(2)}, u32[]{:S(2)}) collective-permute-start(bf16[2,768,384]{2,1,0:T(8,128)(2,1)S(1)} %get-tuple-element.156), channel_id=1, source_target_pairs={{0,4},{1,5},{2,6},{3,7},{4,0},{5,1},{6,2},{7,3},{8,12},{9,13},{10,... | collective-permute-start | bytes 3538952 | tf_op jit(solution)/shard_map/ppermute | solution.py:45
  214.5 22.7 %collective-permute-start.25 = (bf16[1,384,768]{2,1,0:T(8,128)(2,1)S(1)}, bf16[1,384,768]{2,1,0:T(8,128)(2,1)S(1)}, u32[]{:S(2)}, u32[]{:S(2)}) collective-permute-start(bf16[1,384,768]{2,1,0:T(8,128)(2,1)S(1)} %get-tuple-element.175), channel_id=1, source_target_pairs={{0,4},{1,5},{2,6},{3,7},{4,0},{5,1},{6,2},{7,3},{8,12},{9,13},{10,... | collective-permute-start | bytes 1769480 | tf_op jit(solution)/shard_map/ppermute | solution.py:45
  237.2 16.2 %collective-permute-start.26 = (bf16[4,2,2,24,3200]{4,3,2,1,0:T(8,128)(2,1)}, bf16[4,2,2,24,3200]{4,3,2,1,0:T(8,128)(2,1)}, u32[]{:S(2)}, u32[]{:S(2)}) collective-permute-start(bf16[4,2,2,24,3200]{4,3,2,1,0:T(8,128)(2,1)} %bitcast.113), channel_id=1, source_target_pairs={{0,1},{1,0},{2,3},{3,2},{4,5},{5,4},{6,7},{7,6},{8,9},{9,8},{10,11... | collective-permute-start | bytes 7372808 | tf_op jit(solution)/shard_map/ppermute | solution.py:45
  256.0 17.4 %collective-permute-start.27 = (bf16[4,2,24,1664]{3,2,1,0:T(8,128)(2,1)S(1)}, bf16[4,2,24,1664]{3,2,1,0:T(8,128)(2,1)}, u32[]{:S(2)}, u32[]{:S(2)}) collective-permute-start(bf16[4,2,24,1664]{3,2,1,0:T(8,128)(2,1)S(1)} %dynamic-slice_bitcast_fusion), channel_id=1, source_target_pairs={{0,2},{1,3},{2,0},{3,1},{4,6},{5,7},{6,4},{7,5},{8,10},{9,11},{10,... | collective-permute-start | bytes 1916936 | tf_op jit(solution)/shard_map/ppermute | solution.py:45
  257.7 15.6 %collective-permute-start.28 = (bf16[4,2,24,1536]{3,2,1,0:T(8,128)(2,1)}, bf16[4,2,24,1536]{3,2,1,0:T(8,128)(2,1)}, u32[]{:S(2)}, u32[]{:S(2)}) collective-permute-start(bf16[4,2,24,1536]{3,2,1,0:T(8,128)(2,1)} %dynamic-slice_bitcast_fusion.1), channel_id=1, source_target_pairs={{0,4},{1,5},{2,6},{3,7},{4,0},{5,1},{6,2},{7,3},{8,12},{9,13},{10,... | collective-permute-start | bytes 1769480 | tf_op jit(solution)/shard_map/ppermute | solution.py:45
  274.7 10.7 %collective-permute-start.30 = (bf16[4,24,1536]{2,1,0:T(8,128)(2,1)S(1)}, bf16[4,24,1536]{2,1,0:T(8,128)(2,1)S(1)}, u32[]{:S(2)}, u32[]{:S(2)}) collective-permute-start(bf16[4,24,1536]{2,1,0:T(8,128)(2,1)S(1)} %dynamic-slice_bitcast_fusion.3), channel_id=1, source_target_pairs={{0,2},{1,3},{2,0},{3,1},{4,6},{5,7},{6,4},{7,5},{8,10},{9,11},{10,... | collective-permute-start | bytes 884744 | tf_op jit(solution)/shard_map/ppermute | solution.py:45
  277.1 8.4 %collective-permute-start.29 = (bf16[4,24,1664]{2,1,0:T(8,128)(2,1)S(1)}, bf16[4,24,1664]{2,1,0:T(8,128)(2,1)S(1)}, u32[]{:S(2)}, u32[]{:S(2)}) collective-permute-start(bf16[4,24,1664]{2,1,0:T(8,128)(2,1)S(1)} %dynamic-slice_bitcast_fusion.2), channel_id=1, source_target_pairs={{0,4},{1,5},{2,6},{3,7},{4,0},{5,1},{6,2},{7,3},{8,12},{9,13},{10,... | collective-permute-start | bytes 958472 | tf_op jit(solution)/shard_map/ppermute | solution.py:45
  285.7 18.1 %collective-permute-start.31 = (bf16[24,3200]{1,0:T(8,128)(2,1)S(1)}, bf16[24,3200]{1,0:T(8,128)(2,1)S(1)}, u32[]{:S(2)}, u32[]{:S(2)}) collective-permute-start(bf16[24,3200]{1,0:T(8,128)(2,1)S(1)} %get-tuple-element.268), channel_id=1, source_target_pairs={{0,8},{1,9},{2,10},{3,11},{4,12},{5,13},{6,14},{7,15},{8,16},{9,17... | collective-permute-start | bytes 460808 | tf_op jit(solution)/shard_map/ppermute | solution.py:45
  292.0 11.8 %collective-permute-start.32 = (bf16[24,3200]{1,0:T(8,128)(2,1)S(1)}, bf16[24,3200]{1,0:T(8,128)(2,1)S(1)}, u32[]{:S(2)}, u32[]{:S(2)}) collective-permute-start(bf16[24,3200]{1,0:T(8,128)(2,1)S(1)} %get-tuple-element.269), channel_id=1, source_target_pairs={{0,16},{1,17},{2,18},{3,19},{4,20},{5,21},{6,22},{7,23},{8,24},{9,... | collective-permute-start | bytes 460808 | tf_op jit(solution)/shard_map/ppermute | solution.py:45
  292.0 11.8 %collective-permute-start.33 = (bf16[24,3200]{1,0:T(8,128)(2,1)S(1)}, bf16[24,3200]{1,0:T(8,128)(2,1)S(1)}, u32[]{:S(2)}, u32[]{:S(2)}) collective-permute-start(bf16[24,3200]{1,0:T(8,128)(2,1)S(1)} %get-tuple-element.267), channel_id=1, source_target_pairs={{0,24},{1,25},{2,26},{3,27},{4,28},{5,29},{6,30},{7,31},{8,0},{9,1... | collective-permute-start | bytes 460808 | tf_op jit(solution)/shard_map/ppermute | solution.py:45
  (23 other events, 203.0 us)

commit v4 on v3

--- a/solution.py
+++ b/solution.py
@@ -195,7 +195,8 @@
 def pad_kernel(tokens, cot_ref, out_ref):
     rows = out_ref.shape[1]
     for k in range(cot_ref.shape[1]):
-        out_ref[k] = jnp.zeros((rows, out_ref.shape[2]), BF16)
+        full = tokens // 16 * 16
+        out_ref[k, full:] = jnp.zeros((rows - full, out_ref.shape[2]), BF16)
         out_ref[k, :tokens] = cot_ref[0, k]
 
 

time: 307 us -> 304 us (level)
  starting transfers between devices: 68.3 us -> 52.1 us
  waiting for transfers between devices: 41.1 us -> 46.7 us
  Pallas kernels: 143 us -> 148 us
    ppermute x34, starting transfers between devices: 68.3 us -> 52.1 us  [send(): return lax.ppermute(a, BOTH, self.perm(axis, k))]
    ppermute x34, waiting for transfers between devices: 41.1 us -> 46.7 us  [send(): return lax.ppermute(a, BOTH, self.perm(axis, k))]
  transfers between devices with their start and end apart: 34 -> 34, of which waited for: 12 -> 13; matrix products, arithmetic and copies ran while one was open for 12% -> 13% of each run, Pallas kernels for 44% -> 46%
where the time goes in v4:
time: 304 us; the launch traced here: 301 us
  Pallas kernels  148 us (49%)
  starting transfers between devices  52.1 us (17%)
  waiting for transfers between devices  46.7 us (15%)
  local copies, waits for them, and re-layouts  34.6 us (11%)
  other arithmetic  17.2 us (6%)
    ppermute x34, starting transfers between devices, send(): return lax.ppermute(a, BOTH, self.perm(axis, k))  52.1 us
    ppermute x34, waiting for transfers between devices, send(): return lax.ppermute(a, BOTH, self.perm(axis, k))  46.7 us
    pallas_call x1, Pallas kernels, backward(): by_image(partial(backward_kernel, self.tokens, self.slots, self.place), n...  42.2 us
    pallas_call x1, Pallas kernels, forward(): by_image(partial(forward_kernel, self.tokens, self.slots, self.place), n,...  34.8 us
    pallas_call x3, Pallas kernels, input_back(): pl.pallas_call(partial(input_kernel, self.tokens), grid=((high - low) //...  24.3 us
    pallas_call x1, Pallas kernels, weight_grads(): pl.pallas_call(partial(weight_grad_kernel, self.slots, devices), grid_spe...  21.2 us
    unnamed x49, local copies, waits for them, and re-layouts  18 us
    reshape x2, local copies, waits for them, and re-layouts, turned(): return array.reshape(-1, array.shape[-1]).T  12.3 us
  transfers between devices with their start and end apart: 34, of which 13 were waited for; matrix products, arithmetic and copies ran while one was open for 13% of the time, Pallas kernels for 46%

profile of v4, /device:TPU:0, one launch (start us, length us, event | category | flops | bytes accessed | tf_op | source)
XLA Modules:
  0.0 300.8 jit_solution(1540500343808456840)
XLA Ops:
  3.4 3.1 %collective-permute-start = (bf16[24,3200]{1,0:T(8,128)(2,1)S(1)}, bf16[24,3200]{1,0:T(8,128)(2,1)S(1)}, u32[]{:S(2)}, u32[]{:S(2)}) collective-permute-start(bf16[24,3200]{1,0:T(8,128)(2,1)S(1)} %pad_maximum_fusion.11), channel_id=1, source_target_pairs={{0,8},{1,9},{2,10},{3,11},{4,12},{5,13},{6,14},{7,15},{8,16},{9,17... | collective-permute-start | bytes 460808 | tf_op jit(solution)/shard_map/ppermute | solution.py:45
  6.5 2.6 collective-permute-start.1
  11.2 4.3 %copy.86.cot_ref = bf16[4,3,197,768]{3,2,1,0:T(8,128)(2,1)} copy(bf16[4,3,197,768]{3,0,2,1:T(4,128)(2,1)} %param.23) | data formatting | bytes 7262208 | tf_op args[11]
  15.5 4.5 %shard_map.203.cot_ref = bf16[12,208,768]{2,1,0:T(8,128)(2,1)} custom-call(bf16[4,3,197,768]{3,2,1,0:T(8,128)(2,1)} %copy.86.cot_ref), custom_call_target="tpu_custom_call" | custom-call | tf_op jit(solution)/shard_map/pallas_call | solution.py:509
  23.6 6.1 %collective-permute-done.3 = bf16[4,24,1536]{2,1,0:T(8,128)(2,1)S(1)} collective-permute-done((bf16[4,24,1536]{2,1,0:T(8,128)(2,1)S(1)}, bf16[4,24,1536]{2,1,0:T(8,128)(2,1)S(1)}, u32[]{:S(2)}, u32[]{:S(2)}) %collective-permute-start.3) | collective-permute-done | bytes 294944 | tf_op jit(solution)/shard_map/ppermute | solution.py:45
  32.4 2.3 copy.93.x_ref
  34.7 5.6 %shard_map.204 = (bf16[12,208,768]{2,1,0:T(8,128)(2,1)}, f32[12,208,128]{2,1,0:T(8,128)S(1)}) custom-call(bf16[4,3,197,768]{3,2,1,0:T(8,128)(2,1)} %copy.93.x_ref), custom_call_target="tpu_custom_call" | custom-call | tf_op jit(solution)/shard_map/pallas_call | solution.py:521
  40.3 4.2 %collective-permute-done.5 = bf16[4,2,24,1536]{3,2,0,1:T(8,128)(2,1)S(1)} collective-permute-done((bf16[4,2,24,1536]{3,2,0,1:T(8,128)(2,1)S(1)}, bf16[4,2,24,1536]{3,2,0,1:T(8,128)(2,1)S(1)}, u32[]{:S(2)}, u32[]{:S(2)}) %collective-permute-start.5) | collective-permute-done | bytes 589856 | tf_op jit(solution)/shard_map/ppermute | solution.py:45
  56.3 34.8 %shard_map.205 = (bf16[12,208,2304]{2,1,0:T(8,128)(2,1)}, bf16[12,208,768]{2,1,0:T(8,128)(2,1)}, f32[12,208,768]{2,1,0:T(8,128)}, f32[12,208,512]{2,1,0:T(8,128)}, f32[96,1536]{1,0:T(8,128)S(1)}) custom-call(s32[13]{0:T(128)S(1)} %pad_add_fusion.live, bf16[4,3,197,768]{3,2,1,0:T(8,128)(2,1)} %copy.93.x_ref, bf16[12,208,768]{2,1,0:T(8,128)(2,1)} %get-tuple-element.118.n1_ref, ...), custom_call_target="tpu_custom_call" | custom-call | flops 35332816896 | bytes 35332816 | tf_op jit(solution)/shard_map/pallas_call | solution.py:533
  92.7 8.3 %collective-permute-done.13.refs_7_ = bf16[2,384,768]{2,1,0:T(8,128)(2,1)} collective-permute-done((bf16[2,384,768]{2,1,0:T(8,128)(2,1)}, bf16[2,384,768]{2,1,0:T(8,128)(2,1)}, u32[]{:S(2)}, u32[]{:S(2)}) %collective-permute-start.13) | collective-permute-done | bytes 1179680 | tf_op jit(solution)/shard_map/ppermute | solution.py:45
  101.1 5.3 %collective-permute-start.14 = (bf16[96,1536]{1,0:T(8,128)(2,1)S(1)}, bf16[96,1536]{1,0:T(8,128)(2,1)S(1)}, u32[]{:S(2)}, u32[]{:S(2)}) collective-permute-start(bf16[96,1536]{1,0:T(8,128)(2,1)S(1)} %pad_maximum_fusion.10.refs_0_), channel_id=1, source_target_pairs={{0,8},{1,9},{2,10},{3,11},{4,12},{5,13},{6,14},{7,15},{8,16},{9,17... | collective-permute-start | bytes 884744 | tf_op jit(solution)/shard_map/ppermute | solution.py:45
  106.4 2.4 collective-permute-start.16
  108.9 6.2 %copy.94 = bf16[2496,768]{0,1:T(8,128)(2,1)} copy(bf16[2496,768]{1,0:T(8,128)(2,1)} %bitcast.104) | data formatting | bytes 7667712 | tf_op jit(solution)/shard_map/reshape | solution.py:567
  115.1 6.1 %copy.95 = bf16[2496,768]{0,1:T(8,128)(2,1)} copy(bf16[2496,768]{1,0:T(8,128)(2,1)} %bitcast.108) | data formatting | bytes 7667712 | tf_op jit(solution)/shard_map/reshape | solution.py:567
  121.2 2.9 collective-permute-done.15.refs_2_
  125.7 8.7 %shard_map.206 = (bf16[96,1536]{1,0:T(8,128)(2,1)S(1)}, bf16[96,1536]{1,0:T(8,128)(2,1)S(1)}, bf16[96,1536]{1,0:T(8,128)(2,1)S(1)}, bf16[96,1536]{1,0:T(8,128)(2...) custom-call(bf16[96,1536]{1,0:T(8,128)(2,1)S(1)} %pad_maximum_fusion.10.refs_0_, ...), custom_call_target="tpu_custom_call" | custom-call | tf_op jit(solution)/shard_map/pallas_call | solution.py:597
  134.3 9.4 %collective-permute-start.17 = (bf16[96,1536]{1,0:T(8,128)(2,1)S(1)}, bf16[96,1536]{1,0:T(8,128)(2,1)S(1)}, u32[]{:S(2)}, u32[]{:S(2)}) collective-permute-start(bf16[96,1536]{1,0:T(8,128)(2,1)S(1)} %get-tuple-element.145), channel_id=1, source_target_pairs={{0,24},{1,25},{2,26},{3,27},{4,28},{5,29},{6,30},{7,31},{8,0},{9,1... | collective-permute-start | bytes 884744 | tf_op jit(solution)/shard_map/ppermute | solution.py:45
  144.3 6.8 %shard_map.207 = (f32[2,768,384]{2,1,0:T(8,128)}, f32[2,384,768]{2,1,0:T(8,128)}, bf16[2,768,384]{2,1,0:T(8,128)(2,1)S(1)}, bf16[2,384,768]{2,1,0:T(8,128)(2,1)}) custom-call(bf16[96,1536]{1,0:T(8,128)(2,1)S(1)} %pad_maximum_fusion.10.refs_0_, bf16[96,1536]{1,0:T(8,128)(2,1)S(1)} %collective-permute-done.14.refs_1_, ...), custom_call_target="tpu_custom_call" | custom-call | tf_op jit(solution)/shard_map/pallas_call | solution.py:606
  151.2 16.6 %collective-permute-done.18 = bf16[96,1536]{1,0:T(8,128)(2,1)S(1)} collective-permute-done((bf16[96,1536]{1,0:T(8,128)(2,1)S(1)}, bf16[96,1536]{1,0:T(8,128)(2,1)S(1)}, u32[]{:S(2)}, u32[]{:S(2)}) %collective-permute-start.18) | collective-permute-done | bytes 294944 | tf_op jit(solution)/shard_map/ppermute | solution.py:45
  170.7 2.5 collective-permute-done.23
  173.6 42.2 %shard_map.208 = (bf16[12,197,768]{2,1,0:T(8,128)(2,1)}, bf16[12,208,768]{2,1,0:T(8,128)(2,1)}, bf16[12,208,2304]{2,1,0:T(8,128)(2,1)}, f32[8,2304]{1,0:T(8,128)S(1)}, f32[16,768]{1,0:T(8,128)S(1)}) custom-call(s32[13]{0:T(128)S(1)} %pad_add_fusion.live, bf16[12,208,768]{2,1,0:T(8,128)(2,1)} %shard_map.203.cot_ref, ...), custom_call_target="tpu_custom_call" | custom-call | flops 35332816896 | bytes 35332816 | tf_op jit(solution)/shard_map/pallas_call | solution.py:544
  215.8 8.1 %collective-permute-start.25 = (bf16[1,384,768]{2,1,0:T(8,128)(2,1)S(1)}, bf16[1,384,768]{2,1,0:T(8,128)(2,1)S(1)}, u32[]{:S(2)}, u32[]{:S(2)}) collective-permute-start(bf16[1,384,768]{2,1,0:T(8,128)(2,1)S(1)} %get-tuple-element.175), channel_id=1, source_target_pairs={{0,4},{1,5},{2,6},{3,7},{4,0},{5,1},{6,2},{7,3},{8,12},{9,13},{10,... | collective-permute-start | bytes 1769480 | tf_op jit(solution)/shard_map/ppermute | solution.py:45
  224.3 21.2 %shard_map.209 = (bf16[384,3200]{1,0:T(8,128)(2,1)}, bf16[384,3200]{1,0:T(8,128)(2,1)}) custom-call(s32[1]{0:T(128)} %bitcast.32.core, bf16[768,2496]{1,0:T(8,128)(2,1)} %bitcast.106, bf16[768,2496]{1,0:T(8,128)(2,1)} %bitcast.107, bf16[12,208,2304]{2,1,0:T(8,128)(2,1)} %get-tuple-element.178.right_ref.triple_ref, ...), custom_call_target="tpu_custom_call" | custom-call | tf_op jit(solution)/shard_map/pallas_call | solution.py:578
  245.7 6.0 %shard_map.210.refs_0_ = bf16[12,197,768]{2,1,0:T(8,128)(2,1)} custom-call(bf16[12,208,2304]{2,1,0:T(8,128)(2,1)} %get-tuple-element.178.right_ref.triple_ref, bf16[12,208,768]{2,1,0:T(8,128)(2,1)} %get-tuple-element.118.n1_ref, f32[12,208,128]{2,1,0:T(8,128)S(1)} %copy-done.2, bf16[12,208,768]{2,1,0:T(8,128)(2,1)} %get-tuple-element.179.right_out_ref.branch_ref, ...), custom_call_target="tpu_custom_call" | custom-call | tf_op jit(solution)/shard_map/pallas_call | solution.py:555
  251.7 2.3 fusion
  256.9 12.4 %shard_map.211.refs_0_ = bf16[12,197,768]{2,1,0:T(8,128)(2,1)} custom-call(bf16[12,208,2304]{2,1,0:T(8,128)(2,1)} %get-tuple-element.178.right_ref.triple_ref, bf16[12,208,768]{2,1,0:T(8,128)(2,1)} %get-tuple-element.118.n1_ref, f32[12,208,128]{2,1,0:T(8,128)S(1)} %copy-done.2, ...), custom_call_target="tpu_custom_call", output_to_operand_aliasing={{}: (7, {})} | custom-call | tf_op jit(solution)/shard_map/pallas_call | solution.py:555
  269.4 2.6 collective-permute-done.28
  278.3 5.9 %shard_map.212 = bf16[12,197,768]{2,1,0:T(8,128)(2,1)} custom-call(bf16[12,208,2304]{2,1,0:T(8,128)(2,1)} %get-tuple-element.178.right_ref.triple_ref, bf16[12,208,768]{2,1,0:T(8,128)(2,1)} %get-tuple-element.118.n1_ref, f32[12,208,128]{2,1,0:T(8,128)S(1)} %copy-done.2, ...), custom_call_target="tpu_custom_call", output_to_operand_aliasing={{}: (7, {})} | custom-call | tf_op jit(solution)/shard_map/pallas_call | solution.py:555
  284.9 3.7 %collective-permute-start.33 = (bf16[24,3200]{1,0:T(8,128)(2,1)S(1)}, bf16[24,3200]{1,0:T(8,128)(2,1)S(1)}, u32[]{:S(2)}, u32[]{:S(2)}) collective-permute-start(bf16[24,3200]{1,0:T(8,128)(2,1)S(1)} %get-tuple-element.267), channel_id=1, source_target_pairs={{0,24},{1,25},{2,26},{3,27},{4,28},{5,29},{6,30},{7,31},{8,0},{9,1... | collective-permute-start | bytes 460808 | tf_op jit(solution)/shard_map/ppermute | solution.py:45
  288.5 1.7 convert_add_fusion.1
  291.4 3.2 %copy.98 = bf16[4,3,197,768]{3,0,2,1:T(4,128)(2,1)} copy(bf16[4,3,197,768]{3,2,1,0:T(8,128)(2,1)S(1)} %bitcast.109) | data formatting | bytes 7262208
  294.7 3.2 %copy.99 = bf16[4,3,197,768]{3,0,2,1:T(4,128)(2,1)} copy(bf16[4,3,197,768]{3,2,1,0:T(8,128)(2,1)S(1)} %bitcast.105) | data formatting | bytes 7262208
  (155 shorter events, 44.5 us)
Async XLA Ops:
  3.4 16.7 %collective-permute-start = (bf16[24,3200]{1,0:T(8,128)(2,1)S(1)}, bf16[24,3200]{1,0:T(8,128)(2,1)S(1)}, u32[]{:S(2)}, u32[]{:S(2)}) collective-permute-start(bf16[24,3200]{1,0:T(8,128)(2,1)S(1)} %pad_maximum_fusion.11), channel_id=1, source_target_pairs={{0,8},{1,9},{2,10},{3,11},{4,12},{5,13},{6,14},{7,15},{8,16},{9,17... | collective-permute-start | bytes 460808 | tf_op jit(solution)/shard_map/ppermute | solution.py:45
  6.5 13.6 %collective-permute-start.1 = (bf16[24,3200]{1,0:T(8,128)(2,1)S(1)}, bf16[24,3200]{1,0:T(8,128)(2,1)S(1)}, u32[]{:S(2)}, u32[]{:S(2)}) collective-permute-start(bf16[24,3200]{1,0:T(8,128)(2,1)S(1)} %pad_maximum_fusion.11), channel_id=1, source_target_pairs={{0,16},{1,17},{2,18},{3,19},{4,20},{5,21},{6,22},{7,23},{8,24},{9,... | collective-permute-start | bytes 460808 | tf_op jit(solution)/shard_map/ppermute | solution.py:45
  9.1 11.0 %collective-permute-start.2 = (bf16[24,3200]{1,0:T(8,128)(2,1)S(1)}, bf16[24,3200]{1,0:T(8,128)(2,1)S(1)}, u32[]{:S(2)}, u32[]{:S(2)}) collective-permute-start(bf16[24,3200]{1,0:T(8,128)(2,1)S(1)} %pad_maximum_fusion.11), channel_id=1, source_target_pairs={{0,24},{1,25},{2,26},{3,27},{4,28},{5,29},{6,30},{7,31},{8,0},{9,1... | collective-permute-start | bytes 460808 | tf_op jit(solution)/shard_map/ppermute | solution.py:45
  20.4 9.3 %collective-permute-start.4 = (bf16[4,24,1664]{2,1,0:T(8,128)(2,1)S(1)}, bf16[4,24,1664]{2,1,0:T(8,128)(2,1)S(1)}, u32[]{:S(2)}, u32[]{:S(2)}) collective-permute-start(bf16[4,24,1664]{2,1,0:T(8,128)(2,1)S(1)} %pad_maximum_fusion.6), channel_id=1, source_target_pairs={{0,2},{1,3},{2,0},{3,1},{4,6},{5,7},{6,4},{7,5},{8,10},{9,11},{10,... | collective-permute-start | bytes 958472 | tf_op jit(solution)/shard_map/ppermute | solution.py:45
  22.0 7.7 %collective-permute-start.3 = (bf16[4,24,1536]{2,1,0:T(8,128)(2,1)S(1)}, bf16[4,24,1536]{2,1,0:T(8,128)(2,1)S(1)}, u32[]{:S(2)}, u32[]{:S(2)}) collective-permute-start(bf16[4,24,1536]{2,1,0:T(8,128)(2,1)S(1)} %pad_maximum_fusion.9), channel_id=1, source_target_pairs={{0,4},{1,5},{2,6},{3,7},{4,0},{5,1},{6,2},{7,3},{8,12},{9,13},{10,... | collective-permute-start | bytes 884744 | tf_op jit(solution)/shard_map/ppermute | solution.py:45
  29.9 14.6 %collective-permute-start.6 = (bf16[4,2,24,1664]{3,2,1,0:T(8,128)(2,1)S(1)}, bf16[4,2,24,1664]{3,2,1,0:T(8,128)(2,1)S(1)}, u32[]{:S(2)}, u32[]{:S(2)}) collective-permute-start(bf16[4,2,24,1664]{3,2,1,0:T(8,128)(2,1)S(1)} %pad_maximum_fusion.4), channel_id=1, source_target_pairs={{0,4},{1,5},{2,6},{3,7},{4,0},{5,1},{6,2},{7,3},{8,12},{9,13},{10,... | collective-permute-start | bytes 1916936 | tf_op jit(solution)/shard_map/ppermute | solution.py:45
  31.7 12.8 %collective-permute-start.5 = (bf16[4,2,24,1536]{3,2,0,1:T(8,128)(2,1)S(1)}, bf16[4,2,24,1536]{3,2,0,1:T(8,128)(2,1)S(1)}, u32[]{:S(2)}, u32[]{:S(2)}) collective-permute-start(bf16[4,2,24,1536]{3,2,0,1:T(8,128)(2,1)S(1)} %pad_maximum_fusion.5), channel_id=1, source_target_pairs={{0,2},{1,3},{2,0},{3,1},{4,6},{5,7},{6,4},{7,5},{8,10},{9,11},{10,... | collective-permute-start | bytes 1769480 | tf_op jit(solution)/shard_map/ppermute | solution.py:45
  45.8 5.0 %collective-permute-start.8 = (bf16[4,2,2,24,1664]{4,3,2,1,0:T(8,128)(2,1)}, bf16[4,2,2,24,1664]{4,3,2,1,0:T(8,128)(2,1)}, u32[]{:S(2)}, u32[]{:S(2)}) collective-permute-start(bf16[4,2,2,24,1664]{4,3,2,1,0:T(8,128)(2,1)} %pad_maximum_fusion.2), channel_id=1, source_target_pairs={{0,1},{1,0},{2,3},{3,2},{4,5},{5,4},{6,7},{7,6},{8,9},{9,8},{10,11... | collective-permute-start | bytes 3833864 | tf_op jit(solution)/shard_map/ppermute | solution.py:45
  47.6 45.2 %collective-permute-start.12 = (bf16[2,768,384]{2,1,0:T(8,128)(2,1)}, bf16[2,768,384]{2,1,0:T(8,128)(2,1)}, u32[]{:S(2)}, u32[]{:S(2)}) collective-permute-start(bf16[2,768,384]{2,1,0:T(8,128)(2,1)} %refs_4_.1), channel_id=1, source_target_pairs={{0,4},{1,5},{2,6},{3,7},{4,0},{5,1},{6,2},{7,3},{8,12},{9,13},{10,... | collective-permute-start | bytes 3538952 | tf_op jit(solution)/shard_map/ppermute | solution.py:45
  48.7 52.4 %collective-permute-start.13 = (bf16[2,384,768]{2,1,0:T(8,128)(2,1)}, bf16[2,384,768]{2,1,0:T(8,128)(2,1)}, u32[]{:S(2)}, u32[]{:S(2)}) collective-permute-start(bf16[2,384,768]{2,1,0:T(8,128)(2,1)} %refs_6_.1), channel_id=1, source_target_pairs={{0,4},{1,5},{2,6},{3,7},{4,0},{5,1},{6,2},{7,3},{8,12},{9,13},{10,... | collective-permute-start | bytes 3538952 | tf_op jit(solution)/shard_map/ppermute | solution.py:45
  91.2 9.9 %collective-permute-start.10 = (bf16[24,1536]{1,0:T(8,128)(2,1)S(1)}, bf16[24,1536]{1,0:T(8,128)(2,1)S(1)}, u32[]{:S(2)}, u32[]{:S(2)}) collective-permute-start(bf16[24,1536]{1,0:T(8,128)(2,1)S(1)} %get-tuple-element.282), channel_id=1, source_target_pairs={{0,2},{1,3},{2,0},{3,1},{4,6},{5,7},{6,4},{7,5},{8,10},{9,11},{10,... | collective-permute-start | bytes 221192 | tf_op jit(solution)/shard_map/ppermute | solution.py:45
  92.2 8.8 %collective-permute-start.11 = (bf16[24,1536]{1,0:T(8,128)(2,1)S(1)}, bf16[24,1536]{1,0:T(8,128)(2,1)S(1)}, u32[]{:S(2)}, u32[]{:S(2)}) collective-permute-start(bf16[24,1536]{1,0:T(8,128)(2,1)S(1)} %get-tuple-element.281), channel_id=1, source_target_pairs={{0,3},{1,0},{2,1},{3,2},{4,7},{5,4},{6,5},{7,6},{8,11},{9,8},{10,9... | collective-permute-start | bytes 221192 | tf_op jit(solution)/shard_map/ppermute | solution.py:45
  92.2 8.8 %collective-permute-start.9 = (bf16[24,1536]{1,0:T(8,128)(2,1)S(1)}, bf16[24,1536]{1,0:T(8,128)(2,1)S(1)}, u32[]{:S(2)}, u32[]{:S(2)}) collective-permute-start(bf16[24,1536]{1,0:T(8,128)(2,1)S(1)} %get-tuple-element.283), channel_id=1, source_target_pairs={{0,1},{1,2},{2,3},{3,0},{4,5},{5,6},{6,7},{7,4},{8,9},{9,10},{10,1... | collective-permute-start | bytes 221192 | tf_op jit(solution)/shard_map/ppermute | solution.py:45
  101.1 20.1 %collective-permute-start.14 = (bf16[96,1536]{1,0:T(8,128)(2,1)S(1)}, bf16[96,1536]{1,0:T(8,128)(2,1)S(1)}, u32[]{:S(2)}, u32[]{:S(2)}) collective-permute-start(bf16[96,1536]{1,0:T(8,128)(2,1)S(1)} %pad_maximum_fusion.10.refs_0_), channel_id=1, source_target_pairs={{0,8},{1,9},{2,10},{3,11},{4,12},{5,13},{6,14},{7,15},{8,16},{9,17... | collective-permute-start | bytes 884744 | tf_op jit(solution)/shard_map/ppermute | solution.py:45
  106.4 17.6 %collective-permute-start.15 = (bf16[96,1536]{1,0:T(8,128)(2,1)S(1)}, bf16[96,1536]{1,0:T(8,128)(2,1)S(1)}, u32[]{:S(2)}, u32[]{:S(2)}) collective-permute-start(bf16[96,1536]{1,0:T(8,128)(2,1)S(1)} %pad_maximum_fusion.10.refs_0_), channel_id=1, source_target_pairs={{0,16},{1,17},{2,18},{3,19},{4,20},{5,21},{6,22},{7,23},{8,24},{9,... | collective-permute-start | bytes 884744 | tf_op jit(solution)/shard_map/ppermute | solution.py:45
  106.4 19.2 %collective-permute-start.16 = (bf16[96,1536]{1,0:T(8,128)(2,1)S(1)}, bf16[96,1536]{1,0:T(8,128)(2,1)S(1)}, u32[]{:S(2)}, u32[]{:S(2)}) collective-permute-start(bf16[96,1536]{1,0:T(8,128)(2,1)S(1)} %pad_maximum_fusion.10.refs_0_), channel_id=1, source_target_pairs={{0,24},{1,25},{2,26},{3,27},{4,28},{5,29},{6,30},{7,31},{8,0},{9,1... | collective-permute-start | bytes 884744 | tf_op jit(solution)/shard_map/ppermute | solution.py:45
  134.3 16.9 %collective-permute-start.17 = (bf16[96,1536]{1,0:T(8,128)(2,1)S(1)}, bf16[96,1536]{1,0:T(8,128)(2,1)S(1)}, u32[]{:S(2)}, u32[]{:S(2)}) collective-permute-start(bf16[96,1536]{1,0:T(8,128)(2,1)S(1)} %get-tuple-element.145), channel_id=1, source_target_pairs={{0,24},{1,25},{2,26},{3,27},{4,28},{5,29},{6,30},{7,31},{8,0},{9,1... | collective-permute-start | bytes 884744 | tf_op jit(solution)/shard_map/ppermute | solution.py:45
  143.7 24.1 %collective-permute-start.18 = (bf16[96,1536]{1,0:T(8,128)(2,1)S(1)}, bf16[96,1536]{1,0:T(8,128)(2,1)S(1)}, u32[]{:S(2)}, u32[]{:S(2)}) collective-permute-start(bf16[96,1536]{1,0:T(8,128)(2,1)S(1)} %get-tuple-element.146), channel_id=1, source_target_pairs={{0,16},{1,17},{2,18},{3,19},{4,20},{5,21},{6,22},{7,23},{8,24},{9,... | collective-permute-start | bytes 884744 | tf_op jit(solution)/shard_map/ppermute | solution.py:45
  143.7 24.1 %collective-permute-start.19 = (bf16[96,1536]{1,0:T(8,128)(2,1)S(1)}, bf16[96,1536]{1,0:T(8,128)(2,1)S(1)}, u32[]{:S(2)}, u32[]{:S(2)}) collective-permute-start(bf16[96,1536]{1,0:T(8,128)(2,1)S(1)} %get-tuple-element.147), channel_id=1, source_target_pairs={{0,8},{1,9},{2,10},{3,11},{4,12},{5,13},{6,14},{7,15},{8,16},{9,17... | collective-permute-start | bytes 884744 | tf_op jit(solution)/shard_map/ppermute | solution.py:45
  168.1 5.1 %collective-permute-start.23 = (bf16[24,1536]{1,0:T(8,128)(2,1)S(1)}, bf16[24,1536]{1,0:T(8,128)(2,1)S(1)}, u32[]{:S(2)}, u32[]{:S(2)}) collective-permute-start(bf16[24,1536]{1,0:T(8,128)(2,1)S(1)} %get-tuple-element.278), channel_id=1, source_target_pairs={{0,2},{1,3},{2,0},{3,1},{4,6},{5,7},{6,4},{7,5},{8,10},{9,11},{10,... | collective-permute-start | bytes 221192 | tf_op jit(solution)/shard_map/ppermute | solution.py:45
  168.4 5.2 %collective-permute-start.24 = (bf16[24,1536]{1,0:T(8,128)(2,1)S(1)}, bf16[24,1536]{1,0:T(8,128)(2,1)S(1)}, u32[]{:S(2)}, u32[]{:S(2)}) collective-permute-start(bf16[24,1536]{1,0:T(8,128)(2,1)S(1)} %get-tuple-element.277), channel_id=1, source_target_pairs={{0,1},{1,2},{2,3},{3,0},{4,5},{5,6},{6,7},{7,4},{8,9},{9,10},{10,1... | collective-permute-start | bytes 221192 | tf_op jit(solution)/shard_map/ppermute | solution.py:45
  168.7 47.1 %collective-permute-start.21 = (bf16[1,384,768]{2,1,0:T(8,128)(2,1)S(1)}, bf16[1,384,768]{2,1,0:T(8,128)(2,1)S(1)}, u32[]{:S(2)}, u32[]{:S(2)}) collective-permute-start(bf16[1,384,768]{2,1,0:T(8,128)(2,1)S(1)} %get-tuple-element.261), channel_id=1, source_target_pairs={{0,4},{1,5},{2,6},{3,7},{4,0},{5,1},{6,2},{7,3},{8,12},{9,13},{10,... | collective-permute-start | bytes 1769480 | tf_op jit(solution)/shard_map/ppermute | solution.py:45
  170.2 45.6 %collective-permute-start.20 = (bf16[2,768,384]{2,1,0:T(8,128)(2,1)S(1)}, bf16[2,768,384]{2,1,0:T(8,128)(2,1)S(1)}, u32[]{:S(2)}, u32[]{:S(2)}) collective-permute-start(bf16[2,768,384]{2,1,0:T(8,128)(2,1)S(1)} %get-tuple-element.156), channel_id=1, source_target_pairs={{0,4},{1,5},{2,6},{3,7},{4,0},{5,1},{6,2},{7,3},{8,12},{9,13},{10,... | collective-permute-start | bytes 3538952 | tf_op jit(solution)/shard_map/ppermute | solution.py:45
  215.8 29.7 %collective-permute-start.25 = (bf16[1,384,768]{2,1,0:T(8,128)(2,1)S(1)}, bf16[1,384,768]{2,1,0:T(8,128)(2,1)S(1)}, u32[]{:S(2)}, u32[]{:S(2)}) collective-permute-start(bf16[1,384,768]{2,1,0:T(8,128)(2,1)S(1)} %get-tuple-element.175), channel_id=1, source_target_pairs={{0,4},{1,5},{2,6},{3,7},{4,0},{5,1},{6,2},{7,3},{8,12},{9,13},{10,... | collective-permute-start | bytes 1769480 | tf_op jit(solution)/shard_map/ppermute | solution.py:45
  245.5 6.1 %collective-permute-start.26 = (bf16[4,2,2,24,3200]{4,3,2,1,0:T(8,128)(2,1)}, bf16[4,2,2,24,3200]{4,3,2,1,0:T(8,128)(2,1)}, u32[]{:S(2)}, u32[]{:S(2)}) collective-permute-start(bf16[4,2,2,24,3200]{4,3,2,1,0:T(8,128)(2,1)} %bitcast.113), channel_id=1, source_target_pairs={{0,1},{1,0},{2,3},{3,2},{4,5},{5,4},{6,7},{7,6},{8,9},{9,8},{10,11... | collective-permute-start | bytes 7372808 | tf_op jit(solution)/shard_map/ppermute | solution.py:45
  254.2 17.7 %collective-permute-start.27 = (bf16[4,2,24,1664]{3,2,1,0:T(8,128)(2,1)S(1)}, bf16[4,2,24,1664]{3,2,1,0:T(8,128)(2,1)}, u32[]{:S(2)}, u32[]{:S(2)}) collective-permute-start(bf16[4,2,24,1664]{3,2,1,0:T(8,128)(2,1)S(1)} %dynamic-slice_bitcast_fusion), channel_id=1, source_target_pairs={{0,2},{1,3},{2,0},{3,1},{4,6},{5,7},{6,4},{7,5},{8,10},{9,11},{10,... | collective-permute-start | bytes 1916936 | tf_op jit(solution)/shard_map/ppermute | solution.py:45
  256.0 16.0 %collective-permute-start.28 = (bf16[4,2,24,1536]{3,2,1,0:T(8,128)(2,1)}, bf16[4,2,24,1536]{3,2,1,0:T(8,128)(2,1)}, u32[]{:S(2)}, u32[]{:S(2)}) collective-permute-start(bf16[4,2,24,1536]{3,2,1,0:T(8,128)(2,1)} %dynamic-slice_bitcast_fusion.1), channel_id=1, source_target_pairs={{0,4},{1,5},{2,6},{3,7},{4,0},{5,1},{6,2},{7,3},{8,12},{9,13},{10,... | collective-permute-start | bytes 1769480 | tf_op jit(solution)/shard_map/ppermute | solution.py:45
  273.3 10.9 %collective-permute-start.30 = (bf16[4,24,1536]{2,1,0:T(8,128)(2,1)S(1)}, bf16[4,24,1536]{2,1,0:T(8,128)(2,1)S(1)}, u32[]{:S(2)}, u32[]{:S(2)}) collective-permute-start(bf16[4,24,1536]{2,1,0:T(8,128)(2,1)S(1)} %dynamic-slice_bitcast_fusion.3), channel_id=1, source_target_pairs={{0,2},{1,3},{2,0},{3,1},{4,6},{5,7},{6,4},{7,5},{8,10},{9,11},{10,... | collective-permute-start | bytes 884744 | tf_op jit(solution)/shard_map/ppermute | solution.py:45
  275.7 8.8 %collective-permute-start.29 = (bf16[4,24,1664]{2,1,0:T(8,128)(2,1)S(1)}, bf16[4,24,1664]{2,1,0:T(8,128)(2,1)S(1)}, u32[]{:S(2)}, u32[]{:S(2)}) collective-permute-start(bf16[4,24,1664]{2,1,0:T(8,128)(2,1)S(1)} %dynamic-slice_bitcast_fusion.2), channel_id=1, source_target_pairs={{0,4},{1,5},{2,6},{3,7},{4,0},{5,1},{6,2},{7,3},{8,12},{9,13},{10,... | collective-permute-start | bytes 958472 | tf_op jit(solution)/shard_map/ppermute | solution.py:45
  284.7 13.2 %collective-permute-start.31 = (bf16[24,3200]{1,0:T(8,128)(2,1)S(1)}, bf16[24,3200]{1,0:T(8,128)(2,1)S(1)}, u32[]{:S(2)}, u32[]{:S(2)}) collective-permute-start(bf16[24,3200]{1,0:T(8,128)(2,1)S(1)} %get-tuple-element.268), channel_id=1, source_target_pairs={{0,8},{1,9},{2,10},{3,11},{4,12},{5,13},{6,14},{7,15},{8,16},{9,17... | collective-permute-start | bytes 460808 | tf_op jit(solution)/shard_map/ppermute | solution.py:45
  284.7 13.2 %collective-permute-start.32 = (bf16[24,3200]{1,0:T(8,128)(2,1)S(1)}, bf16[24,3200]{1,0:T(8,128)(2,1)S(1)}, u32[]{:S(2)}, u32[]{:S(2)}) collective-permute-start(bf16[24,3200]{1,0:T(8,128)(2,1)S(1)} %get-tuple-element.269), channel_id=1, source_target_pairs={{0,16},{1,17},{2,18},{3,19},{4,20},{5,21},{6,22},{7,23},{8,24},{9,... | collective-permute-start | bytes 460808 | tf_op jit(solution)/shard_map/ppermute | solution.py:45
  284.9 13.1 %collective-permute-start.33 = (bf16[24,3200]{1,0:T(8,128)(2,1)S(1)}, bf16[24,3200]{1,0:T(8,128)(2,1)S(1)}, u32[]{:S(2)}, u32[]{:S(2)}) collective-permute-start(bf16[24,3200]{1,0:T(8,128)(2,1)S(1)} %get-tuple-element.267), channel_id=1, source_target_pairs={{0,24},{1,25},{2,26},{3,27},{4,28},{5,29},{6,30},{7,31},{8,0},{9,1... | collective-permute-start | bytes 460808 | tf_op jit(solution)/shard_map/ppermute | solution.py:45
  (23 other events, 181.6 us)
